TPU v7x, 32 devices: a whole 2x2x4 slice. The times are simulated.
32 devices in a mesh: dp: 8 (over z, x), head: 4 (over y, core).
Axes of the slice: x: 2, y: 2, z: 4, core: 2. Of those that a mesh axis runs over, the one named last changes fastest.
Arguments:
- residual_in: float32 [16384, 512], P(('dp', 'head')), may hold values from -6 to 6
- cotangent: float32 [16384, 512], P(('dp', 'head')), may hold values from -6 to 6
- triple_weight: bfloat16 [512, 1536], P(None, 'head'), may hold values from -0.25 to 0.25
- proj_weight: bfloat16 [512, 512], P('head'), may hold values from -1.5 to 1.5
- up_weight: bfloat16 [512, 2048], P(None, 'head'), may hold values from -0.25 to 0.25
- up_bias: bfloat16 [2048], P('head'), may hold values from -1.5 to 1.5
- down_weight: bfloat16 [2048, 512], P('head'), may hold values from -0.125 to 0.125
- proj_bias: float32 [512], replicated, may hold values from -1.5 to 1.5
- down_bias: float32 [512], replicated, may hold values from -1.5 to 1.5
- first_gain: float32 [512], replicated, may hold values from 0.5 to 1.5
- first_shift: float32 [512], replicated, may hold values from -1.5 to 1.5
- second_gain: float32 [512], replicated, may hold values from 0.5 to 1.5
- second_shift: float32 [512], replicated, may hold values from -1.5 to 1.5
- start_steps: int32 [128], P('dp'), may hold values from 0 to 20
- cond_counts: int32 [128], P('dp'), may hold values from 0 to 12
- valid_lengths: int32 [128], P('dp'), may hold values from 64 to 126
Outputs:
- block_out: float32 [16384, 512], P(('dp', 'head'))
- grad_input: float32 [16384, 512], P(('dp', 'head'))
- grad_triple: float32 [512, 1536], P(None, 'head')
- grad_proj: float32 [512, 512], P('head')
- grad_up: float32 [512, 2048], P(None, 'head')
- grad_up_bias: float32 [2048], P('head')
- grad_down: float32 [2048, 512], P('head')
- grad_proj_bias: float32 [512], replicated
- grad_down_bias: float32 [512], replicated
- grad_first_gain: float32 [512], replicated
- grad_first_shift: float32 [512], replicated
- grad_second_gain: float32 [512], replicated
- grad_second_shift: float32 [512], replicated
All inputs are finite; a program needn't handle non-finite values.
Results may differ from a plain program's by a relative error of at most 0.0095.
The roundings to bfloat16 on the way count: a program that leaves them out, or rounds other values in their place, can miss the bound.
Values may be sent and summed in bfloat16 or wider, within the bound.
No kernel may reach another device: no remote copies, remote signals or barrier semaphores. Data moves between devices by JAX's collectives and lax.ppermute only.
A program may use at most 128 MiB of HBM per device.

v0:
```python
import jax
import jax.numpy as jnp
from jax import lax
from jax.sharding import PartitionSpec as P

HEAD_DIM = 64
SEQ = 128
STEP_TOKENS = 6


EPSILON = 1e-05
NEG_FILL = -1e30


def normalize(rows, gain, shift):
    centre = rows - jnp.mean(rows, axis=-1, keepdims=True)
    spread = jnp.mean(centre * centre, axis=-1, keepdims=True)
    return centre * lax.rsqrt(spread + EPSILON) * gain + shift


def visible(starts, counts, lengths):
    places = jnp.arange(SEQ, dtype=jnp.int32)
    groups = jnp.maximum((places // STEP_TOKENS)[None, :], starts[:, None])
    causal = groups[:, None, :] <= groups[:, :, None]
    prefix = places[None, None, :] < counts[:, None, None]
    present = places[None, None, :] < lengths[:, None, None]
    return present & (causal | prefix)


def split_triple(triple_low, heads):
    shaped = triple_low.reshape(triple_low.shape[0] // SEQ, SEQ, heads, 3, HEAD_DIM)
    return (shaped[:, :, :, 0], shaped[:, :, :, 1], shaped[:, :, :, 2])


def masked_scores(queries, keys_all, allowed):
    scores = jnp.einsum(
        "snhe,smhe->shnm", queries, keys_all, preferred_element_type=jnp.float32
    ) * HEAD_DIM ** (-0.5)
    return jnp.where(allowed[:, None], scores, NEG_FILL)


def attend_forward(triple_low, allowed, heads):
    queries, keys_all, values = split_triple(triple_low, heads)
    scores = masked_scores(queries, keys_all, allowed)
    top = jnp.max(scores, axis=-1, keepdims=True)
    weights = jnp.exp(scores - top)
    total = jnp.sum(weights, axis=-1, keepdims=True)
    probs = weights / total
    mixed = jnp.einsum(
        "shnm,smhe->snhe", probs.astype(jnp.bfloat16), values, preferred_element_type=jnp.float32
    )
    return (
        mixed.reshape(triple_low.shape[0], heads * HEAD_DIM).astype(jnp.bfloat16),
        top + jnp.log(total),
    )


def attend_backward(triple_low, grad_mixed, logsum, allowed, heads):
    queries, keys_all, values = split_triple(triple_low, heads)
    probs = jnp.exp(masked_scores(queries, keys_all, allowed) - logsum)
    grad_heads = grad_mixed.reshape(queries.shape)
    grad_probs = jnp.einsum(
        "snhe,smhe->shnm", grad_heads, values, preferred_element_type=jnp.float32
    )
    inner = jnp.sum(grad_probs * probs, axis=-1, keepdims=True)
    grad_scores = (probs * (grad_probs - inner)).astype(jnp.bfloat16)
    factor = HEAD_DIM ** (-0.5)
    grad_queries = (
        jnp.einsum("shnm,smhe->snhe", grad_scores, keys_all, preferred_element_type=jnp.float32)
        * factor
    )
    grad_keys = (
        jnp.einsum("shnm,snhe->smhe", grad_scores, queries, preferred_element_type=jnp.float32)
        * factor
    )
    grad_values = jnp.einsum(
        "shnm,snhe->smhe",
        probs.astype(jnp.bfloat16),
        grad_heads,
        preferred_element_type=jnp.float32,
    )
    stacked = jnp.stack([grad_queries, grad_keys, grad_values], axis=3)
    return stacked.reshape(triple_low.shape[0], heads * 3 * HEAD_DIM).astype(jnp.bfloat16)


def shards(
    residual_in,
    cotangent,
    triple_weight,
    proj_weight,
    up_weight,
    up_bias,
    down_weight,
    proj_bias,
    down_bias,
    first_gain,
    first_shift,
    second_gain,
    second_shift,
    start_steps,
    cond_counts,
    valid_lengths,
):
    triple_use, proj_use, up_use, upbias_use, down_use = (
        triple_weight,
        proj_weight,
        up_weight,
        up_bias,
        down_weight,
    )
    starts, counts, lengths = (start_steps, cond_counts, valid_lengths)
    heads = triple_use.shape[1] // (3 * HEAD_DIM)
    allowed = visible(starts, counts, lengths)
    first_low = normalize(residual_in, first_gain, first_shift).astype(jnp.bfloat16)
    first_rows = lax.all_gather(first_low, "head", axis=0, tiled=True)
    triple_low = jnp.dot(first_rows, triple_use, preferred_element_type=jnp.float32).astype(
        jnp.bfloat16
    )
    mixed_low, logsum = attend_forward(triple_low, allowed, heads)
    part = mixed_low
    attn_out = lax.psum_scatter(
        jnp.dot(part, proj_use, preferred_element_type=jnp.float32),
        "head",
        scatter_dimension=0,
        tiled=True,
    )
    middle = residual_in + attn_out + proj_bias
    second_low = normalize(middle, second_gain, second_shift).astype(jnp.bfloat16)
    second_rows = lax.all_gather(second_low, "head", axis=0, tiled=True)
    up_pre = jnp.dot(second_rows, up_use, preferred_element_type=jnp.float32) + upbias_use.astype(
        jnp.float32
    )
    act_low = jax.nn.gelu(up_pre).astype(jnp.bfloat16)
    part = act_low
    mlp_out = lax.psum_scatter(
        jnp.dot(part, down_use, preferred_element_type=jnp.float32),
        "head",
        scatter_dimension=0,
        tiled=True,
    )
    block_out = middle + mlp_out + down_bias
    out_low = cotangent.astype(jnp.bfloat16)
    out_rows = lax.all_gather(out_low, "head", axis=0, tiled=True)
    grad_down = jnp.einsum("nf,nd->fd", act_low, out_rows, preferred_element_type=jnp.float32)
    grad_act = jnp.einsum("nd,fd->nf", out_rows, down_use, preferred_element_type=jnp.float32)
    gelu_back = jax.vjp(jax.nn.gelu, up_pre)[1]
    grad_pre = gelu_back(grad_act)[0].astype(jnp.bfloat16)
    grad_upbias = jnp.sum(grad_pre.astype(jnp.float32), axis=0)
    grad_up = jnp.einsum("nd,nf->df", second_rows, grad_pre, preferred_element_type=jnp.float32)
    part = grad_pre
    grad_second = lax.psum_scatter(
        jnp.einsum("nf,df->nd", part, up_use, preferred_element_type=jnp.float32),
        "head",
        scatter_dimension=0,
        tiled=True,
    )
    second_back = jax.vjp(normalize, middle, second_gain, second_shift)[1]
    middle_rows, second_gain_part, second_shift_part = second_back(grad_second)
    grad_middle = cotangent + middle_rows
    middle_low = grad_middle.astype(jnp.bfloat16)
    middle_all = lax.all_gather(middle_low, "head", axis=0, tiled=True)
    grad_proj = jnp.einsum("nh,nd->hd", mixed_low, middle_all, preferred_element_type=jnp.float32)
    grad_mixed = jnp.einsum(
        "nd,hd->nh", middle_all, proj_use, preferred_element_type=jnp.float32
    ).astype(jnp.bfloat16)
    grad_triple_low = attend_backward(triple_low, grad_mixed, logsum, allowed, heads)
    grad_triple = jnp.einsum(
        "nd,nt->dt", first_rows, grad_triple_low, preferred_element_type=jnp.float32
    )
    part = grad_triple_low
    grad_first = lax.psum_scatter(
        jnp.einsum("nt,dt->nd", part, triple_use, preferred_element_type=jnp.float32),
        "head",
        scatter_dimension=0,
        tiled=True,
    )
    first_back = jax.vjp(normalize, residual_in, first_gain, first_shift)[1]
    input_rows, first_gain_part, first_shift_part = first_back(grad_first)
    grad_input = grad_middle + input_rows
    grad_triple, grad_proj, grad_up, grad_upbias, grad_down = lax.psum(
        (grad_triple, grad_proj, grad_up, grad_upbias, grad_down), "dp"
    )
    sums = lax.psum(
        (
            first_gain_part,
            first_shift_part,
            second_gain_part,
            second_shift_part,
            jnp.sum(grad_middle, axis=0),
            jnp.sum(cotangent, axis=0),
        ),
        ("dp", "head"),
    )
    return (
        block_out,
        grad_input,
        grad_triple,
        grad_proj,
        grad_up,
        grad_upbias,
        grad_down,
        sums[4],
        sums[5],
        sums[0],
        sums[1],
        sums[2],
        sums[3],
    )


def solution(mesh):
    in_specs = (
        P(("dp", "head"), None),
        P(("dp", "head"), None),
        P(None, "head"),
        P("head", None),
        P(None, "head"),
        P("head"),
        P("head", None),
        P(),
        P(),
        P(),
        P(),
        P(),
        P(),
        P("dp"),
        P("dp"),
        P("dp"),
    )
    out_specs = (
        P(("dp", "head"), None),
        P(("dp", "head"), None),
        P(None, "head"),
        P("head", None),
        P(None, "head"),
        P("head"),
        P("head", None),
        P(),
        P(),
        P(),
        P(),
        P(),
        P(),
    )
    return jax.shard_map(shards, mesh=mesh, in_specs=in_specs, out_specs=out_specs, check_vma=False)
```

profile of v0, /device:TPU:0, one launch (start us, length us, event | category | flops | bytes accessed | tf_op | source)
XLA Modules:
  0.0 483.2 jit_solution(15964535945136883536)
XLA Ops:
  7.3 1.5 reduce_sum.148
  8.8 1.5 multiply_reduce_fusion.6
  10.3 1.0 add_convert_fusion.1
  11.7 1.2 or_and_fusion
  12.8 24.0 %all-gather.5.cloned.1.call-done = bf16[2048,512]{1,0:T(8,128)(2,1)} async-done(((bf16[512,512]{1,0:T(8,128)(2,1)}), bf16[2048,512]{1,0:T(8,128)(2,1)}) %all-gather.5.cloned.1.call-update) | async-done | bytes 2097168 | tf_op jit(solution)/shard_map/all_gather | solution.py:115
  36.8 4.0 convolution_convert_fusion
  40.8 1.7 copy.38
  45.6 0.8 copy-done.10
  46.4 2.7 fusion.25
  49.2 44.6 %reduce-scatter.5.cloned.1.call-done = f32[512,512]{1,0:T(8,128)} async-done(((f32[2048,512]{1,0:T(8,128)}), f32[512,512]{1,0:T(8,128)}) %reduce-scatter.5.cloned.1.call-update) | async-done | bytes 1048592 | tf_op jit(solution)/shard_map/reduce_scatter | solution.py:121
  93.8 2.9 fusion.36
  97.0 1.0 add_convert_fusion
  98.7 22.1 %all-gather.7.cloned.1.call-done = bf16[2048,512]{1,0:T(8,128)(2,1)} async-done(((bf16[512,512]{1,0:T(8,128)(2,1)}), bf16[2048,512]{1,0:T(8,128)(2,1)}) %all-gather.7.cloned.1.call-update) | async-done | bytes 2097168 | tf_op jit(solution)/shard_map/all_gather | solution.py:129
  120.8 4.8 fusion.40
  125.5 19.9 %all-gather.9.cloned.1.call-done = bf16[2048,512]{1,0:T(8,128)(2,1)} async-done(((bf16[512,512]{1,0:T(8,128)(2,1)}), bf16[2048,512]{1,0:T(8,128)(2,1)}) %all-gather.9.cloned.1.call-update) | async-done | bytes 2097168 | tf_op jit(solution)/shard_map/all_gather | solution.py:143
  145.4 7.1 %convert_reduce_fusion = (f32[512]{0:T(512)S(1)}, bf16[2048,512]{1,0:T(8,128)(2,1)S(1)}, bf16[2048,512]{1,0:T(8,128)(2,1)}) fusion(f32[2048,512]{1,0:T(8,128)} %fusion.40, f32[512]{0:T(512)S(1)} %convert_element_type.59, bf16[2048,512]{1,0:T(8,128)(2,1)} %all-gather.9.cloned.1.call-done, bf16[512,512]{1,0:T(8,128)(2,1)S(1)} %copy-done), kind=kOutput, calls=%fused_computation.9 | convolution fusion | flops 1099955712 | bytes 11014144 | tf_op jit(solution)/shard_map/nd,fd->nf/dot_general | solution.py:145
  152.5 1.3 copy-done.8
  153.9 3.2 fusion.42
  157.1 4.8 fusion.41
  162.2 39.5 %reduce-scatter.9.cloned.1.call-done = f32[512,512]{1,0:T(8,128)} async-done(((f32[2048,512]{1,0:T(8,128)}), f32[512,512]{1,0:T(8,128)}) %reduce-scatter.9.cloned.1.call-update) | async-done | bytes 1048592 | tf_op jit(solution)/shard_map/reduce_scatter | solution.py:151
  201.7 1.6 multiply_reduce_fusion.1
  203.4 45.2 %reduce-scatter.7.cloned.1.call-done = f32[512,512]{1,0:T(8,128)} async-done(((f32[2048,512]{1,0:T(8,128)}), f32[512,512]{1,0:T(8,128)}) %reduce-scatter.7.cloned.1.call-update) | async-done | bytes 1048592 | tf_op jit(solution)/shard_map/reduce_scatter | solution.py:135
  248.7 3.0 fusion.35
  251.9 1.0 copy-done.5
  252.9 0.9 convert_element_type.63
  253.8 22.7 %all-gather.11.cloned.1.call-done = bf16[2048,512]{1,0:T(8,128)(2,1)} async-done(((bf16[512,512]{1,0:T(8,128)(2,1)}), bf16[2048,512]{1,0:T(8,128)(2,1)}) %all-gather.11.cloned.1.call-update) | async-done | bytes 2097168 | tf_op jit(solution)/shard_map/all_gather | solution.py:161
  276.5 2.3 convolution_convert_fusion.1
  279.9 2.6 fusion.18
  282.5 0.7 multiply_reduce_fusion
  284.3 0.8 fusion.19
  285.9 1.0 copy.50
  286.9 3.3 fusion.11
  290.3 4.6 fusion.44
  294.9 2.2 fusion.43
  297.3 1.2 fusion.23
  298.4 1.0 copy-done.36
  299.5 2.2 fusion.9
  301.7 21.7 %psum.80 = f32[512]{0:T(512)} all-reduce(f32[512]{0:T(512)S(1)} %get-tuple-element.31), channel_id=1, replica_groups=mesh['dp'=8,'head'=4] {'dp'}, use_global_device_ids=true, to_apply=%region_19.20 | all-reduce | flops 512 | bytes 4096 | tf_op jit(solution)/shard_map/psum | solution.py:180
  323.4 11.5 %reduce-scatter.11.cloned.1.call-done = f32[512,512]{1,0:T(8,128)} async-done(((f32[2048,512]{1,0:T(8,128)}), f32[512,512]{1,0:T(8,128)}) %reduce-scatter.11.cloned.1.call-update) | async-done | bytes 1048592 | tf_op jit(solution)/shard_map/reduce_scatter | solution.py:171
  334.9 1.6 multiply_reduce_fusion.2
  336.6 42.7 %all-reduce = (f32[512]{0:T(512)}, f32[512]{0:T(512)}, f32[512]{0:T(512)}, f32[512]{0:T(512)}, f32[512]{0:T(512)}, /*index=5*/f32[512]{0:T(512)}) all-reduce(f32[512]{0:T(512)S(1)} %get-tuple-element.29, f32[512]{0:T(512)S(1)} %get-tuple-element.51, f32[512]{0:T(512)S(1)} %get-tuple-element.15, ...), channel_id=1, replica_groups=mesh['dp'=8,'head'=4] {'dp','head'}, use_global_device_ids=true, to_apply=%region_22.23 | all-reduce | flops 3072 | bytes 24576 | tf_op jit(solution)/shard_map/psum | solution.py:183
  379.2 1.6 fusion.34
  380.9 1.2 add_add_fusion.2
  382.1 88.7 %all-reduce.4.cloned.1.call-done = (f32[512,384]{1,0:T(8,128)}, f32[128,512]{1,0:T(8,128)}, f32[512,512]{1,0:T(8,128)}, f32[512,512]{1,0:T(8,128)}) async-done(((f32[512,384]{1,0:T(8,128)}, f32[128,512]{1,0:T(8,128)}, f32[512,512]{1,0:T(8,128)}, f32[512,512]{1,0:T(8,128)}), (f32[512,384]{1,0:T(8,128)}, f32[128,512]{1,0:T(8,128)}, f32[512,512]{1,0:T(8,128)}, ...) | async-done | bytes 3145744 | tf_op jit(solution)/shard_map/psum | solution.py:180
  470.8 2.2 copy.98
  473.0 1.7 copy.99
  474.7 1.0 copy.100
  475.7 1.0 copy.101
  (115 shorter events, 8.1 us)
Async XLA Ops:
  7.2 138.3 %copy-start = (bf16[512,512]{1,0:T(8,128)(2,1)S(1)}, bf16[512,512]{1,0:T(8,128)(2,1)}, u32[]{:S(2)}) copy-start(bf16[512,512]{1,0:T(8,128)(2,1)} %param.22) | copy-start | bytes 1572868
  7.2 3.1 copy-start.2
  7.2 3.1 copy-start.27
  7.2 3.1 copy-start.29
  7.2 4.2 copy-start.33
  7.2 4.3 copy-start.34
  7.2 4.4 copy-start.35
  7.3 29.6 %copy-start.24 = (bf16[512,384]{1,0:T(8,128)(2,1)S(1)}, bf16[512,384]{1,0:T(8,128)(2,1)}, u32[]{:S(2)}) copy-start(bf16[512,384]{1,0:T(8,128)(2,1)} %param.18) | copy-start | bytes 1179652
  7.3 29.6 %all-gather.5.cloned.1.call-start = ((), (), s32[]{:S(2)}) async-start(), calls=%async_computation.4 | async-start | bytes 2621440 | tf_op jit(solution)/shard_map/all_gather | solution.py:115
  11.4 82.4 %reduce-scatter.5.cloned.1.call-start = ((), (), s32[]{:S(2)}) async-start(), calls=%async_computation.5 | async-start | bytes 5242880 | tf_op jit(solution)/shard_map/reduce_scatter | solution.py:121
  43.3 1.1 copy-start.17
  43.3 1.1 copy-start.19
  43.3 1.1 copy-start.15
  43.9 1.3 copy-start.3
  44.4 2.0 copy-start.23
  45.6 0.8 copy-start.10
  49.1 44.7 %copy-start.28 = (f32[512]{0:T(512)S(1)}, f32[512]{0:T(512)}, u32[]{:S(2)}) copy-start(f32[512]{0:T(512)} %param.23) | copy-start | bytes 6148
  49.1 47.8 %copy-start.26 = (f32[512]{0:T(512)S(1)}, f32[512]{0:T(512)}, u32[]{:S(2)}) copy-start(f32[512]{0:T(512)} %param.27) | copy-start | bytes 6148
  49.1 47.8 %copy-start.30 = (f32[512]{0:T(512)S(1)}, f32[512]{0:T(512)}, u32[]{:S(2)}) copy-start(f32[512]{0:T(512)} %param.28) | copy-start | bytes 6148
  49.1 71.6 %all-gather.7.cloned.1.call-start = ((), (), s32[]{:S(2)}) async-start(), calls=%async_computation.6 | async-start | bytes 2621440 | tf_op jit(solution)/shard_map/all_gather | solution.py:129
  96.7 2.0 copy-start.32
  96.7 24.1 %copy-start.14 = (bf16[512,512]{1,0:T(8,128)(2,1)S(1)}, bf16[512,512]{1,0:T(8,128)(2,1)}, u32[]{:S(2)}) copy-start(bf16[512,512]{1,0:T(8,128)(2,1)} %param.20) | copy-start | bytes 1572868
  98.0 47.4 %all-gather.9.cloned.1.call-start = ((), (), s32[]{:S(2)}) async-start(), calls=%async_computation.8 | async-start | bytes 2621440 | tf_op jit(solution)/shard_map/all_gather | solution.py:143
  98.6 103.2 %reduce-scatter.9.cloned.1.call-start = ((), (), s32[]{:S(2)}) async-start(), calls=%async_computation.9 | async-start | bytes 5242880 | tf_op jit(solution)/shard_map/reduce_scatter | solution.py:151
  152.5 1.3 copy-start.8
  157.1 91.6 %reduce-scatter.7.cloned.1.call-start = ((), (), s32[]{:S(2)}) async-start(), calls=%async_computation.7 | async-start | bytes 5242880 | tf_op jit(solution)/shard_map/reduce_scatter | solution.py:135
  162.0 86.7 %copy-start.31 = (f32[512]{0:T(512)S(1)}, f32[512]{0:T(512)}, u32[]{:S(2)}) copy-start(f32[512]{0:T(512)} %param.24) | copy-start | bytes 6148
  162.0 114.5 %all-gather.11.cloned.1.call-start = ((), (), s32[]{:S(2)}) async-start(), calls=%async_computation.10 | async-start | bytes 2621440 | tf_op jit(solution)/shard_map/all_gather | solution.py:161
  248.7 3.1 copy-start.12
  251.9 1.0 copy-start.5
  253.8 81.1 %reduce-scatter.11.cloned.1.call-start = ((), (), s32[]{:S(2)}) async-start(), calls=%async_computation.11 | async-start | bytes 5242880 | tf_op jit(solution)/shard_map/reduce_scatter | solution.py:171
  279.2 3.3 copy-start.16
  279.9 2.6 copy-start.4
  283.2 1.0 copy-start.20
  284.3 1.0 copy-start.18
  285.9 1.0 copy-start.25
  290.2 180.5 %all-reduce.4.cloned.1.call-start = ((), (), s32[]{:S(2)}) async-start(), calls=%async_computation.12 | async-start | bytes 6291456 | tf_op jit(solution)/shard_map/psum | solution.py:180
  290.3 4.7 copy-start.9
  290.3 4.6 copy-start.13
  294.9 2.3 copy-start.7
  294.9 2.4 copy-start.11
  297.3 2.2 copy-start.36
  336.5 44.4 %copy-start.6 = (f32[512,512]{1,0:T(8,128)S(1)}, f32[512,512]{1,0:T(8,128)}, u32[]{:S(2)}) copy-start(f32[512,512]{1,0:T(8,128)} %copy-done.5) | copy-start | bytes 3145732
  470.7 3.9 copy-start.22
  470.7 4.9 %copy-start.21 = (f32[512,512]{1,0:T(8,128)S(1)}, f32[512,512]{1,0:T(8,128)}, u32[]{:S(2)}) copy-start(f32[512,512]{1,0:T(8,128)} %get-tuple-element.58) | copy-start | bytes 3145732
  473.0 3.7 copy-start.1
Sparse Core Ops, SparseCore 0:
  11.5 25.2 all-gather.4
  49.2 44.4 reduce-scatter.4
  98.1 22.5 all-gather.6
  122.8 22.5 all-gather.8
  157.2 44.4 reduce-scatter.8
  204.1 44.4 reduce-scatter.6
  253.9 22.5 all-gather.10
  290.3 44.5 reduce-scatter.10
  339.3 131.3 all-reduce.3
where the time goes:
time: 484 us; the launch traced here: 483 us
  waiting for transfers between devices  319 us (66%)
  blocking collectives  64.4 us (13%)
  matrix products  48 us (10%)
  other arithmetic  21 us (4%)
  local copies, waits for them, and re-layouts  16.1 us (3%)
  between operations  14.3 us (3%)
    psum x1, waiting for transfers between devices, shards(): lax.psum((grad_triple, grad_proj, grad_up, grad_upbias, grad_down), 'dp')  88.7 us
    reduce_scatter x1, waiting for transfers between devices, shards(): lax.psum_scatter(jnp.dot(part, down_use, preferred_element_type=jnp.float...  45.2 us
    reduce_scatter x1, waiting for transfers between devices, shards(): lax.psum_scatter(jnp.dot(part, proj_use, preferred_element_type=jnp.float...  44.6 us
    psum x1, blocking collectives, shards(): lax.psum((first_gain_part, first_shift_part, second_gain_part, second_shi...  42.7 us
    reduce_scatter x1, waiting for transfers between devices, shards(): lax.psum_scatter(jnp.einsum('nf,df->nd', part, up_use, preferred_element_...  39.5 us
    all_gather x1, waiting for transfers between devices, shards(): first_rows = lax.all_gather(first_low, 'head', axis=0, tiled=True)  24 us
    all_gather x1, waiting for transfers between devices, shards(): middle_all = lax.all_gather(middle_low, 'head', axis=0, tiled=True)  22.7 us
    all_gather x1, waiting for transfers between devices, shards(): second_rows = lax.all_gather(second_low, 'head', axis=0, tiled=True)  22.1 us
  transfers between devices with their start and end apart: 9, of which 9 were waited for; matrix products, arithmetic and copies ran while one was open for 6% of the time, Pallas kernels for 0%

commit v1 on v0

v1 whole, which is shorter than its diff:
```python
import jax
import jax.numpy as jnp
from jax import lax
from jax.sharding import PartitionSpec as P

HEAD_DIM = 64
SEQ = 128
STEP_TOKENS = 6
EPSILON = 1e-05
NEG_FILL = -1e30
BF = jnp.bfloat16
F32 = jnp.float32
AXES = ("dp", "head")


def normalize(rows, gain, shift):
    centre = rows - jnp.mean(rows, axis=-1, keepdims=True)
    spread = jnp.mean(centre * centre, axis=-1, keepdims=True)
    return centre * lax.rsqrt(spread + EPSILON) * gain + shift


def visible(starts, counts, lengths):
    places = jnp.arange(SEQ, dtype=jnp.int32)
    groups = jnp.maximum((places // STEP_TOKENS)[None, :], starts[:, None])
    causal = groups[:, None, :] <= groups[:, :, None]
    prefix = places[None, None, :] < counts[:, None, None]
    present = places[None, None, :] < lengths[:, None, None]
    return present & (causal | prefix)


def split_triple(triple_low, heads):
    shaped = triple_low.reshape(triple_low.shape[0] // SEQ, SEQ, heads, 3, HEAD_DIM)
    return (shaped[:, :, :, 0], shaped[:, :, :, 1], shaped[:, :, :, 2])


def masked_scores(queries, keys_all, allowed):
    scores = jnp.einsum(
        "snhe,smhe->shnm", queries, keys_all, preferred_element_type=F32
    ) * HEAD_DIM ** (-0.5)
    return jnp.where(allowed[:, None], scores, NEG_FILL)


def attend_forward(triple_low, allowed, heads):
    queries, keys_all, values = split_triple(triple_low, heads)
    scores = masked_scores(queries, keys_all, allowed)
    top = jnp.max(scores, axis=-1, keepdims=True)
    weights = jnp.exp(scores - top)
    total = jnp.sum(weights, axis=-1, keepdims=True)
    probs = weights / total
    mixed = jnp.einsum("shnm,smhe->snhe", probs.astype(BF), values, preferred_element_type=F32)
    return mixed.reshape(triple_low.shape[0], heads * HEAD_DIM).astype(BF), probs


def attend_backward(triple_low, grad_mixed, probs, heads):
    queries, keys_all, values = split_triple(triple_low, heads)
    grad_heads = grad_mixed.reshape(queries.shape)
    grad_probs = jnp.einsum("snhe,smhe->shnm", grad_heads, values, preferred_element_type=F32)
    inner = jnp.sum(grad_probs * probs, axis=-1, keepdims=True)
    grad_scores = (probs * (grad_probs - inner)).astype(BF)
    factor = HEAD_DIM ** (-0.5)
    grad_queries = (
        jnp.einsum("shnm,smhe->snhe", grad_scores, keys_all, preferred_element_type=F32) * factor
    )
    grad_keys = (
        jnp.einsum("shnm,snhe->smhe", grad_scores, queries, preferred_element_type=F32) * factor
    )
    grad_values = jnp.einsum(
        "shnm,snhe->smhe", probs.astype(BF), grad_heads, preferred_element_type=F32
    )
    stacked = jnp.stack([grad_queries, grad_keys, grad_values], axis=3)
    return stacked.reshape(triple_low.shape[0], heads * 3 * HEAD_DIM).astype(BF)


class Links:
    def __init__(self, mesh):
        self.dp, self.head = mesh.shape["dp"], mesh.shape["head"]

    def swap(self, value, bit):
        total = self.dp * self.head
        return lax.ppermute(value, AXES, [(i, i ^ bit) for i in range(total)])

    def gather(self, shard):
        slots = shard[None]
        bit = self.head // 2
        while bit:
            slots = jnp.concatenate([slots, self.swap(slots, bit)], 0)
            bit //= 2
        return slots

    def scatter(self, slots):
        bit = 1
        while bit < self.head:
            half = slots.shape[0] // 2
            got = self.swap(slots[half:].astype(BF), bit)
            slots = slots[:half] + got.astype(F32)
            bit *= 2
        return slots[0]

    def total(self, part):
        place = lax.axis_index("dp")
        bit, kept = 1, []
        while bit < self.dp:
            half = part.shape[0] // 2
            mine = (place // bit) % 2
            keep = lax.dynamic_slice_in_dim(part, mine * half, half, 0)
            send = lax.dynamic_slice_in_dim(part, (1 - mine) * half, half, 0)
            part = keep + self.swap(send.astype(BF), bit * self.head).astype(F32)
            bit *= 2
        low = part.astype(BF)
        while bit > 1:
            bit //= 2
            mine = (place // bit) % 2
            other = self.swap(low, bit * self.head)
            low = jnp.where(
                mine == 0, jnp.concatenate([low, other], 0), jnp.concatenate([other, low], 0)
            )
        return low.astype(F32)

    def everywhere(self, vec, axes_bits):
        for bit in axes_bits:
            vec = vec + self.swap(vec, bit)
        return vec


def make(mesh):
    links = Links(mesh)

    def columns(slots):
        return jnp.concatenate(list(slots), 1)

    def rows_of(slots):
        return slots.reshape(-1, slots.shape[-1])

    def shards(
        residual_in,
        cotangent,
        triple_weight,
        proj_weight,
        up_weight,
        up_bias,
        down_weight,
        proj_bias,
        down_bias,
        first_gain,
        first_shift,
        second_gain,
        second_shift,
        start_steps,
        cond_counts,
        valid_lengths,
    ):
        rows = residual_in.shape[0]
        seqs = rows // SEQ
        nslots = links.head
        place = lax.axis_index("head")
        pick = lambda a: lax.dynamic_slice_in_dim(a, place * seqs, seqs, 0)
        allowed = visible(pick(start_steps), pick(cond_counts), pick(valid_lengths))
        triple_use = columns(links.gather(triple_weight))
        proj_use = rows_of(links.gather(proj_weight))
        up_use = columns(links.gather(up_weight))
        upbias_use = links.gather(up_bias[None]).reshape(-1)
        down_use = rows_of(links.gather(down_weight))
        heads = triple_use.shape[1] // (3 * HEAD_DIM)
        first_rows = normalize(residual_in, first_gain, first_shift).astype(BF)
        triple_low = jnp.dot(first_rows, triple_use, preferred_element_type=F32).astype(BF)
        mixed_low, probs = attend_forward(triple_low, allowed, heads)
        attn_out = jnp.dot(mixed_low, proj_use, preferred_element_type=F32)
        middle = residual_in + attn_out + proj_bias
        second_rows = normalize(middle, second_gain, second_shift).astype(BF)
        up_pre = jnp.dot(second_rows, up_use, preferred_element_type=F32) + upbias_use.astype(F32)
        act_low = jax.nn.gelu(up_pre).astype(BF)
        out_rows = cotangent.astype(BF)
        grad_down = jnp.einsum("nf,nd->fd", act_low, out_rows, preferred_element_type=F32)
        grad_down = links.total(links.scatter(grad_down.reshape(nslots, -1, grad_down.shape[1])))
        grad_act = jnp.einsum("nd,fd->nf", out_rows, down_use, preferred_element_type=F32)
        gelu_back = jax.vjp(jax.nn.gelu, up_pre)[1]
        grad_pre = gelu_back(grad_act)[0].astype(BF)
        grad_upbias = jnp.sum(grad_pre.astype(F32), axis=0)
        grad_up = jnp.einsum("nd,nf->df", second_rows, grad_pre, preferred_element_type=F32)
        split = lambda g: jnp.stack(jnp.split(g, nslots, axis=1))
        grad_up = links.total(links.scatter(split(grad_up)))
        grad_upbias = links.everywhere(
            links.scatter(grad_upbias.reshape(nslots, 1, -1)),
            [links.head * 2**k for k in range(links.dp.bit_length() - 1)],
        )[0]
        grad_second = jnp.einsum("nf,df->nd", grad_pre, up_use, preferred_element_type=F32)
        mlp_out = jnp.dot(act_low, down_use, preferred_element_type=F32)
        block_out = middle + mlp_out + down_bias
        second_back = jax.vjp(normalize, middle, second_gain, second_shift)[1]
        middle_rows, second_gain_part, second_shift_part = second_back(grad_second)
        grad_middle = cotangent + middle_rows
        middle_low = grad_middle.astype(BF)
        grad_proj = jnp.einsum("nh,nd->hd", mixed_low, middle_low, preferred_element_type=F32)
        grad_proj = links.total(links.scatter(grad_proj.reshape(nslots, -1, grad_proj.shape[1])))
        grad_mixed = jnp.einsum(
            "nd,hd->nh", middle_low, proj_use, preferred_element_type=F32
        ).astype(BF)
        grad_triple_low = attend_backward(triple_low, grad_mixed, probs, heads)
        grad_triple = jnp.einsum(
            "nd,nt->dt", first_rows, grad_triple_low, preferred_element_type=F32
        )
        grad_triple = links.total(links.scatter(split(grad_triple)))
        grad_first = jnp.einsum(
            "nt,dt->nd", grad_triple_low, triple_use, preferred_element_type=F32
        )
        first_back = jax.vjp(normalize, residual_in, first_gain, first_shift)[1]
        input_rows, first_gain_part, first_shift_part = first_back(grad_first)
        grad_input = grad_middle + input_rows
        sums = jnp.stack(
            [
                jnp.sum(grad_middle, axis=0),
                jnp.sum(cotangent, axis=0),
                first_gain_part,
                first_shift_part,
                second_gain_part,
                second_shift_part,
                jnp.zeros_like(first_gain_part),
                jnp.zeros_like(first_gain_part),
            ]
        )
        sums = links.everywhere(
            sums, [2**k for k in range((links.dp * links.head).bit_length() - 1)]
        )
        return (
            block_out,
            grad_input,
            grad_triple,
            grad_proj,
            grad_up,
            grad_upbias,
            grad_down,
            sums[0],
            sums[1],
            sums[2],
            sums[3],
            sums[4],
            sums[5],
        )

    return shards


def solution(mesh):
    in_specs = (
        P(("dp", "head"), None),
        P(("dp", "head"), None),
        P(None, "head"),
        P("head", None),
        P(None, "head"),
        P("head"),
        P("head", None),
        P(),
        P(),
        P(),
        P(),
        P(),
        P(),
        P("dp"),
        P("dp"),
        P("dp"),
    )
    out_specs = (
        P(("dp", "head"), None),
        P(("dp", "head"), None),
        P(None, "head"),
        P("head", None),
        P(None, "head"),
        P("head"),
        P("head", None),
        P(),
        P(),
        P(),
        P(),
        P(),
        P(),
    )
    return jax.shard_map(
        make(mesh), mesh=mesh, in_specs=in_specs, out_specs=out_specs, check_vma=False
    )
```

time: 484 us -> 235 us (0.49)
  waiting for transfers between devices: 319 us -> 61.4 us
  blocking collectives: 64.4 us -> 0 us
  starting transfers between devices: 0.55 us -> 57.3 us
  local copies, waits for them, and re-layouts: 16.1 us -> 39 us
  between operations: 14.3 us -> 1.92 us
  other arithmetic: 21 us -> 29.9 us
    reduce_scatter x4 -> x0, waiting for transfers between devices: 141 us -> none  [the longest x1 45.2 us: shards(): lax.psum_scatter(jnp.dot(part, down_use, preferred_element_type=jnp.float...]
    all_gather x4 -> x0, waiting for transfers between devices: 88.7 us -> none  [the longest x1 24 us: shards(): first_rows = lax.all_gather(first_low, 'head', axis=0, tiled=True)]
    psum x1 -> x0, waiting for transfers between devices: 88.7 us -> none  [shards(): lax.psum((grad_triple, grad_proj, grad_up, grad_upbias, grad_down), 'dp')]
    psum x2 -> x0, blocking collectives: 64.4 us -> none  [the longest x1 42.7 us: shards(): lax.psum((first_gain_part, first_shift_part, second_gain_part, second_shi...]
    ppermute x0 -> x52, waiting for transfers between devices: none -> 61.4 us  [swap(): return lax.ppermute(value, AXES, [(i, i ^ bit) for i in range(total)])]
    ppermute x0 -> x52, starting transfers between devices: none -> 57.3 us  [swap(): return lax.ppermute(value, AXES, [(i, i ^ bit) for i in range(total)])]
    concatenate x0 -> x7, other arithmetic: none -> 11.1 us  [gather(): slots = jnp.concatenate([slots, self.swap(slots, bit)], 0)]
    reduce_sum x4 -> x1, other arithmetic: 9.05 us -> 0.15 us  [normalize(): centre = rows - jnp.mean(rows, axis=-1, keepdims=True)]
  transfers between devices with their start and end apart: 9 -> 52, of which waited for: 9 -> 21; matrix products, arithmetic and copies ran while one was open for 6% -> 23% of each run, Pallas kernels for 0% -> 0%
where the time goes in v1:
time: 235 us; the launch traced here: 234 us
  waiting for transfers between devices  61.4 us (26%)
  starting transfers between devices  57.3 us (24%)
  matrix products  44.8 us (19%)
  local copies, waits for them, and re-layouts  39 us (17%)
  other arithmetic  29.9 us (13%)
    ppermute x52, waiting for transfers between devices, swap(): return lax.ppermute(value, AXES, [(i, i ^ bit) for i in range(total)])  61.4 us
    ppermute x52, starting transfers between devices, swap(): return lax.ppermute(value, AXES, [(i, i ^ bit) for i in range(total)])  57.3 us
    unnamed x146, local copies, waits for them, and re-layouts  13.2 us
    concatenate x7, other arithmetic, gather(): slots = jnp.concatenate([slots, self.swap(slots, bit)], 0)  11.1 us
  transfers between devices with their start and end apart: 52, of which 21 were waited for; matrix products, arithmetic and copies ran while one was open for 23% of the time, Pallas kernels for 0%

profile of v1, /device:TPU:0, one launch (start us, length us, event | category | flops | bytes accessed | tf_op | source)
XLA Modules:
  0.0 234.4 jit_solution(16153811160725900283)
XLA Ops:
  0.7 3.0 %collective-permute-start.2 = (bf16[1,128,512]{2,1,0:T(8,128)(2,1)}, bf16[1,128,512]{2,1,0:T(8,128)(2,1)S(1)}, u32[]{:S(2)}, u32[]{:S(2)}) collective-permute-start(bf16[1,128,512]{2,1,0:T(8,128)(2,1)} %bitcast.177), channel_id=1, source_target_pairs={{0,2},{1,3},{2,0},{3,1},{4,6},{5,7},{6,4},{7,5},{8,10},{9,11},{10,... | collective-permute-start | bytes 393224 | tf_op jit(solution)/shard_map/ppermute | solution.py:80
  3.8 1.9 collective-permute-start.8
  6.5 1.9 collective-permute-start.6
  12.5 4.3 %collective-permute-done = bf16[1,512,384]{2,1,0:T(8,128)(2,1)} collective-permute-done((bf16[1,512,384]{2,1,0:T(8,128)(2,1)}, bf16[1,512,384]{2,1,0:T(8,128)(2,1)}, u32[]{:S(2)}, u32[]{:S(2)}) %collective-permute-start) | collective-permute-done | bytes 393248 | tf_op jit(solution)/shard_map/ppermute | solution.py:80
  16.8 2.1 pad_maximum_fusion.7
  19.0 19.5 %collective-permute-done.6 = bf16[1,1,512]{2,1,0:T(2,128)(2,1)S(1)} collective-permute-done((bf16[1,1,512]{2,1,0:T(2,128)(2,1)S(1)}, bf16[1,1,512]{2,1,0:T(2,128)(2,1)S(1)}, u32[]{:S(2)}, u32[]{:S(2)}) %collective-permute-start.6) | collective-permute-done | bytes 1056 | tf_op jit(solution)/shard_map/ppermute | solution.py:80
  42.3 2.3 pad_maximum_fusion.5
  45.0 2.1 pad_maximum_fusion.4
  49.4 2.1 convolution_convert_fusion
  51.5 1.8 copy.49
  53.3 2.4 %reshape.279 = bf16[4,128,8,3,64]{1,0,4,3,2:T(4,128)(2,1)S(1)} reshape(bf16[512,1536]{0,1:T(8,128)(2,1)} %copy.49) | data formatting | bytes 3145728 | tf_op jit(solution)/shard_map/reshape | solution.py:32
  57.2 3.5 %fusion.68 = (f32[4,8,128]{2,1,0:T(8,128)S(1)}, f32[4,8,128,128]{2,3,1,0:T(8,128)}) fusion(pred[4,128,128]{1,2,0:T(8,128)(4,1)} %or_and_fusion, bf16[4,128,8,1,64]{1,0,4,3,2:T(4,128)(2,1)} %get-tuple-element.53, bf16[4,128,8,1,64]{1,0,4,3,2:T(4,128)(2,1)} %get-tuple-element.54), kind=kOutput, calls=%fused_computation.197 | convolution fusion | flops 69206144 | bytes 3227648 | tf_op jit(solution)/shard_map/sub | solution.py:47
  60.7 2.0 fusion.22
  65.3 2.5 %fusion.42 = f32[512,2048]{1,0:T(8,128)S(1)} fusion(bf16[512,512]{1,0:T(8,128)(2,1)S(1)} %get-tuple-element.57, bf16[512,512]{1,0:T(8,128)(2,1)S(1)} %get-tuple-element.56, bf16[512,512]{1,0:T(8,128)(2,1)} %bitcast.11, bf16[512,512]{1,0:T(8,128)(2,1)S(1)} %copy-done.30, f32[512,512]{0,1:T(8,128)S(1)} %get-tuple-element.69, f32[512]{0:T(512)S(1)} %copy-done.46, ...), kind=kOutput, calls=%fused_computation.119 | convolution fusion | flops 1083441152 | bytes 7348224 | tf_op jit(solution)/shard_map/dot_general | solution.py:170
  67.9 2.9 %pad_maximum_fusion.1 = bf16[4,512,512]{2,1,0:T(8,128)(2,1)S(1)} fusion(bf16[2,512,512]{2,1,0:T(8,128)(2,1)} %collective-permute-done.9, bf16[1,512,512]{2,1,0:T(8,128)(2,1)} %collective-permute-done.8, bf16[1,512,512]{2,1,0:T(8,128)(2,1)S(1)} %bitcast.173), kind=kLoop, calls=%fused_computation.20 | loop fusion | flops 2097152 | bytes 4194304 | tf_op jit(solution)/shard_map/concatenate | solution.py:86
  71.0 4.4 %convert_reduce_fusion = (f32[2048]{0:T(1024)}, bf16[512,2048]{1,0:T(8,128)(2,1)S(1)}) fusion(f32[512,2048]{1,0:T(8,128)S(1)} %fusion.42, f32[2048]{0:T(1024)S(1)} %bitcast.184, bf16[2048,512]{1,0:T(8,128)(2,1)S(1)} %bitcast.168, f32[512,512]{1,0:T(8,128)S(1)} %copy-done.12), kind=kOutput, calls=%fused_computation.15 | convolution fusion | flops 1098119168 | bytes 9453568 | tf_op jit(solution)/shard_map/nd,fd->nf/dot_general | solution.py:175
  75.4 4.2 %fusion.73 = (f32[512]{0:T(512)}, f32[512,512]{1,0:T(8,128)}) fusion(bf16[512,2048]{1,0:T(8,128)(2,1)S(1)} %get-tuple-element.77, bf16[512,512]{1,0:T(8,128)(2,1)S(1)} %get-tuple-element.57, bf16[512,512]{1,0:T(8,128)(2,1)S(1)} %get-tuple-element.56, bf16[512,512]{1,0:T(8,128)(2,1)} %bitcast.11, bf16[512,512]{1,0:T(8,128)(2,1)S(1)} %copy-done.30), kind=kOutput, calls=%fused_computation.202 | convolution fusion | flops 1082392064 | bytes 5244928 | tf_op jit(solution)/shard_map/nf,df->nd/dot_general | solution.py:186
  86.3 1.9 reshape.288
  89.6 2.7 %fusion.23 = bf16[4,128,8,1,64]{1,4,2,0,3:T(8,128)(2,1)S(1)} fusion(bf16[4,128,8,64]{1,3,2,0:T(8,128)(2,1)} %copy.60, f32[4,8,128,128]{2,3,1,0:T(8,128)} %get-tuple-element.67, f32[4,8,128]{2,1,0:T(8,128)} %copy-done.52), kind=kOutput, calls=%fused_computation.51 | convolution fusion | flops 68419584 | bytes 3162112 | tf_op jit(solution)/shard_map/shnm,snhe->smhe/dot_general | solution.py:67
  97.1 3.6 %fusion.72 = (f32[512]{0:T(512)}, f32[512,512]{1,0:T(8,128)}) fusion(bf16[512,384]{1,0:T(8,128)(2,1)S(1)} %copy-done.38, bf16[512,384]{1,0:T(8,128)(2,1)S(1)} %copy-done.36, bf16[512,384]{1,0:T(8,128)(2,1)} %bitcast.1, bf16[512,384]{1,0:T(8,128)(2,1)S(1)} %copy-done.34, bf16[192,8,4,128]{3,2,1,0:T(4,128)(2,1)S(1)} %bitcast.162), kind=kOutput, calls=%fused_computation.201 | convolution fusion | flops 811859456 | bytes 4196352 | tf_op jit(solution)/shard_map/nt,dt->nd/dot_general | solution.py:203
  100.7 3.3 %fusion.70 = (bf16[512,1536]{1,0:T(8,128)(2,1)}, f32[512,1536]{1,0:T(8,128)}) fusion(bf16[192,8,4,128]{3,2,1,0:T(4,128)(2,1)S(1)} %bitcast.163, f32[512,512]{0,1:T(8,128)S(1)} %copy.55, f32[512]{0:T(512)S(1)} %copy-done.62, f32[512]{0:T(512)S(1)} %copy-done.41, f32[512]{0:T(512)S(1)} %copy-done.44, f32[512]{0:T(512)S(1)} %broadcast_multiply_fusion.1), kind=kOutput, calls=%fused_computation.199 | convolution fusion | flops 807403520 | bytes 7348224 | tf_op jit(solution)/shard_map/nd,nt->dt/dot_general | solution.py:199
  106.0 4.1 %fusion.71 = (bf16[512,2048]{1,0:T(8,128)(2,1)}, f32[512,2048]{1,0:T(8,128)}) fusion(bf16[512,2048]{1,0:T(8,128)(2,1)S(1)} %copy-done.23, f32[512,512]{0,1:T(8,128)S(1)} %get-tuple-element.69, f32[512]{0:T(512)S(1)} %copy-done.47, f32[512]{0:T(512)S(1)} %copy-done.39, f32[512]{0:T(512)S(1)} %fusion.55, f32[512]{0:T(512)S(1)} %broadcast_multiply_fusion), kind=kOutput, calls=%fused_computation.200 | convolution fusion | flops 1076101120 | bytes 9445376 | tf_op jit(solution)/shard_map/nd,nf->df/dot_general | solution.py:179
  110.1 4.3 %fusion.47 = f32[2048,512]{1,0:T(8,128)} fusion(f32[512,512]{1,0:T(8,128)S(1)} %copy-done.13, f32[512,2048]{1,0:T(8,128)S(1)} %copy-done.70, f32[2048]{0:T(1024)S(1)} %bitcast.185), kind=kOutput, calls=%fused_computation.133 | convolution fusion | flops 1084489728 | bytes 9445376 | tf_op jit(solution)/shard_map/nf,nd->fd/dot_general | solution.py:173
  114.4 3.0 %fusion.19 = f32[512,512]{0,1:T(8,128)} fusion(f32[512,512]{0,1:T(8,128)S(1)} %get-tuple-element.69, bf16[2048,512]{1,0:T(8,128)(2,1)S(1)} %bitcast.169, f32[512]{0:T(512)S(1)} %copy-done.65, f32[512,2048]{1,0:T(8,128)S(1)} %copy-done.70, f32[2048]{0:T(1024)S(1)} %bitcast.186), kind=kOutput, calls=%fused_computation.44 | convolution fusion | flops 1084751872 | bytes 8398848 | tf_op jit(solution)/shard_map/dot_general | solution.py:187
  117.4 1.8 copy.66
  123.1 1.8 slice.194
  125.5 3.1 %slice_bitcast_fusion.1 = (f32[1,512,512]{2,1,0:T(8,128)}, f32[1,512,512]{2,1,0:T(8,128)}) fusion(f32[512,2048]{1,0:T(8,128)} %get-tuple-element.75), kind=kLoop, calls=%fused_computation.59 | loop fusion | bytes 4194304 | tf_op jit(solution)/shard_map/stack | solution.py:180
  129.8 1.8 collective-permute-start.35
  137.1 2.0 collective-permute-done.19
  145.2 2.7 %collective-permute-start.38 = (f32[1,512]{1,0:T(1,128)S(1)}, f32[1,512]{1,0:T(1,128)S(1)}, u32[]{:S(2)}, u32[]{:S(2)}) collective-permute-start(f32[1,512]{1,0:T(1,128)S(1)} %add.317), channel_id=1, source_target_pairs={{0,16},{1,17},{2,18},{3,19},{4,20},{5,21},{6,22},{7,23},{8,24},{9,... | collective-permute-start | bytes 6152 | tf_op jit(solution)/shard_map/ppermute | solution.py:80
  151.3 2.1 collective-permute-start.22
  154.4 2.2 copy-done.3
  157.7 2.5 %copy.69 = f32[512,512]{1,0:T(8,128)} copy(f32[512,512]{0,1:T(8,128)} %fusion.19) | data formatting | bytes 2097152
  165.4 2.0 collective-permute-done.23
  168.2 2.2 collective-permute-done.12
  172.5 2.7 %collective-permute-done.13 = bf16[128,384]{1,0:T(8,128)(2,1)S(1)} collective-permute-done((bf16[128,384]{1,0:T(8,128)(2,1)S(1)}, bf16[128,384]{1,0:T(8,128)(2,1)S(1)}, u32[]{:S(2)}, u32[]{:S(2)}) %collective-permute-start.13) | collective-permute-done | bytes 98336 | tf_op jit(solution)/shard_map/ppermute | solution.py:80
  175.2 2.4 %collective-permute-start.14 = (bf16[64,384]{1,0:T(8,128)(2,1)S(1)}, bf16[64,384]{1,0:T(8,128)(2,1)S(1)}, u32[]{:S(2)}, u32[]{:S(2)}) collective-permute-start(bf16[64,384]{1,0:T(8,128)(2,1)S(1)} %dynamic-slice_convert_fusion.9), channel_id=1, source_target_pairs={{0,16},{1,17},{2,18},{3,19},{4,20},{5,21},{6,22},{7,23},{8,24},{9,... | collective-permute-start | bytes 147464 | tf_op jit(solution)/shard_map/ppermute | solution.py:80
  180.7 2.2 collective-permute-start.15
  182.9 1.9 collective-permute-start.25
  187.9 7.3 %collective-permute-done.40 = bf16[1,512,512]{2,1,0:T(8,128)(2,1)S(1)} collective-permute-done((bf16[1,512,512]{2,1,0:T(8,128)(2,1)S(1)}, bf16[1,512,512]{2,1,0:T(8,128)(2,1)S(1)}, u32[]{:S(2)}, u32[]{:S(2)}) %collective-permute-start.40) | collective-permute-done | bytes 524320 | tf_op jit(solution)/shard_map/ppermute | solution.py:80
  198.2 3.7 %collective-permute-done.41 = bf16[256,512]{1,0:T(8,128)(2,1)S(1)} collective-permute-done((bf16[256,512]{1,0:T(8,128)(2,1)S(1)}, bf16[256,512]{1,0:T(8,128)(2,1)S(1)}, u32[]{:S(2)}, u32[]{:S(2)}) %collective-permute-start.41) | collective-permute-done | bytes 262176 | tf_op jit(solution)/shard_map/ppermute | solution.py:80
  203.7 2.1 collective-permute-start.30
  205.8 1.9 collective-permute-done.42
  207.8 2.4 %collective-permute-start.43 = (bf16[64,512]{1,0:T(8,128)(2,1)S(1)}, bf16[64,512]{1,0:T(8,128)(2,1)S(1)}, u32[]{:S(2)}, u32[]{:S(2)}) collective-permute-start(bf16[64,512]{1,0:T(8,128)(2,1)S(1)} %dynamic-slice_convert_fusion.6), channel_id=1, source_target_pairs={{0,16},{1,17},{2,18},{3,19},{4,20},{5,21},{6,22},{7,23},{8,24},{9,... | collective-permute-start | bytes 196616 | tf_op jit(solution)/shard_map/ppermute | solution.py:80
  211.8 2.0 collective-permute-done.43
  220.1 2.1 collective-permute-done.32
  224.8 1.7 collective-permute-start.46
  227.5 2.9 %collective-permute-done.33 = bf16[256,512]{1,0:T(8,128)(2,1)S(1)} collective-permute-done((bf16[256,512]{1,0:T(8,128)(2,1)S(1)}, bf16[256,512]{1,0:T(8,128)(2,1)S(1)}, u32[]{:S(2)}, u32[]{:S(2)}) %collective-permute-start.33) | collective-permute-done | bytes 262176 | tf_op jit(solution)/shard_map/ppermute | solution.py:80
  (344 shorter events, 87.2 us)
Async XLA Ops:
  0.7 11.0 %collective-permute-start.2 = (bf16[1,128,512]{2,1,0:T(8,128)(2,1)}, bf16[1,128,512]{2,1,0:T(8,128)(2,1)S(1)}, u32[]{:S(2)}, u32[]{:S(2)}) collective-permute-start(bf16[1,128,512]{2,1,0:T(8,128)(2,1)} %bitcast.177), channel_id=1, source_target_pairs={{0,2},{1,3},{2,0},{3,1},{4,6},{5,7},{6,4},{7,5},{8,10},{9,11},{10,... | collective-permute-start | bytes 393224 | tf_op jit(solution)/shard_map/ppermute | solution.py:80
  3.7 13.1 %collective-permute-start = (bf16[1,512,384]{2,1,0:T(8,128)(2,1)}, bf16[1,512,384]{2,1,0:T(8,128)(2,1)}, u32[]{:S(2)}, u32[]{:S(2)}) collective-permute-start(bf16[1,512,384]{2,1,0:T(8,128)(2,1)} %bitcast.180), channel_id=1, source_target_pairs={{0,2},{1,3},{2,0},{3,1},{4,6},{5,7},{6,4},{7,5},{8,10},{9,11},{10,... | collective-permute-start | bytes 1179656 | tf_op jit(solution)/shard_map/ppermute | solution.py:80
  3.8 38.4 %collective-permute-start.8 = (bf16[1,512,512]{2,1,0:T(8,128)(2,1)}, bf16[1,512,512]{2,1,0:T(8,128)(2,1)}, u32[]{:S(2)}, u32[]{:S(2)}) collective-permute-start(bf16[1,512,512]{2,1,0:T(8,128)(2,1)} %bitcast.171), channel_id=1, source_target_pairs={{0,2},{1,3},{2,0},{3,1},{4,6},{5,7},{6,4},{7,5},{8,10},{9,11},{10,... | collective-permute-start | bytes 1572872 | tf_op jit(solution)/shard_map/ppermute | solution.py:80
  5.7 39.2 %collective-permute-start.4 = (bf16[1,512,512]{2,1,0:T(8,128)(2,1)}, bf16[1,512,512]{2,1,0:T(8,128)(2,1)}, u32[]{:S(2)}, u32[]{:S(2)}) collective-permute-start(bf16[1,512,512]{2,1,0:T(8,128)(2,1)} %bitcast.175), channel_id=1, source_target_pairs={{0,2},{1,3},{2,0},{3,1},{4,6},{5,7},{6,4},{7,5},{8,10},{9,11},{10,... | collective-permute-start | bytes 1572872 | tf_op jit(solution)/shard_map/ppermute | solution.py:80
  6.5 31.9 %collective-permute-start.6 = (bf16[1,1,512]{2,1,0:T(2,128)(2,1)S(1)}, bf16[1,1,512]{2,1,0:T(2,128)(2,1)S(1)}, u32[]{:S(2)}, u32[]{:S(2)}) collective-permute-start(bf16[1,1,512]{2,1,0:T(2,128)(2,1)S(1)} %broadcast_in_dim_broadcast_in_dim.3), channel_id=1, source_target_pairs={{0,2},{1,3},{2,0},{3,1},{4,6},{5,7},{6,4},{7,5},{8,10},{9,11},{10,... | collective-permute-start | bytes 3080 | tf_op jit(solution)/shard_map/ppermute | solution.py:80
  12.5 28.8 %collective-permute-start.3 = (bf16[2,128,512]{2,1,0:T(8,128)(2,1)}, bf16[2,128,512]{2,1,0:T(8,128)(2,1)}, u32[]{:S(2)}, u32[]{:S(2)}) collective-permute-start(bf16[2,128,512]{2,1,0:T(8,128)(2,1)} %pad_maximum_fusion.14), channel_id=1, source_target_pairs={{0,1},{1,0},{2,3},{3,2},{4,5},{5,4},{6,7},{7,6},{8,9},{9,8},{10,11... | collective-permute-start | bytes 786440 | tf_op jit(solution)/shard_map/ppermute | solution.py:80
  18.9 28.4 %collective-permute-start.1 = (bf16[2,512,384]{2,1,0:T(8,128)(2,1)}, bf16[2,512,384]{2,1,0:T(8,128)(2,1)}, u32[]{:S(2)}, u32[]{:S(2)}) collective-permute-start(bf16[2,512,384]{2,1,0:T(8,128)(2,1)} %pad_maximum_fusion.7), channel_id=1, source_target_pairs={{0,1},{1,0},{2,3},{3,2},{4,5},{5,4},{6,7},{7,6},{8,9},{9,8},{10,11... | collective-permute-start | bytes 2359304 | tf_op jit(solution)/shard_map/ppermute | solution.py:80
  44.6 23.3 %collective-permute-start.9 = (bf16[2,512,512]{2,1,0:T(8,128)(2,1)}, bf16[2,512,512]{2,1,0:T(8,128)(2,1)}, u32[]{:S(2)}, u32[]{:S(2)}) collective-permute-start(bf16[2,512,512]{2,1,0:T(8,128)(2,1)} %pad_maximum_fusion.5), channel_id=1, source_target_pairs={{0,1},{1,0},{2,3},{3,2},{4,5},{5,4},{6,7},{7,6},{8,9},{9,8},{10,11... | collective-permute-start | bytes 3145736 | tf_op jit(solution)/shard_map/ppermute | solution.py:80
  47.1 16.8 %collective-permute-start.5 = (bf16[2,512,512]{2,1,0:T(8,128)(2,1)}, bf16[2,512,512]{2,1,0:T(8,128)(2,1)}, u32[]{:S(2)}, u32[]{:S(2)}) collective-permute-start(bf16[2,512,512]{2,1,0:T(8,128)(2,1)} %pad_maximum_fusion.4), channel_id=1, source_target_pairs={{0,1},{1,0},{2,3},{3,2},{4,5},{5,4},{6,7},{7,6},{8,9},{9,8},{10,11... | collective-permute-start | bytes 3145736 | tf_op jit(solution)/shard_map/ppermute | solution.py:80
  122.7 26.1 %collective-permute-start.10 = (bf16[2,512,384]{2,1,0:T(8,128)(2,1)}, bf16[2,512,384]{2,1,0:T(8,128)(2,1)}, u32[]{:S(2)}, u32[]{:S(2)}) collective-permute-start(bf16[2,512,384]{2,1,0:T(8,128)(2,1)} %pad_maximum_fusion.8), channel_id=1, source_target_pairs={{0,1},{1,0},{2,3},{3,2},{4,5},{5,4},{6,7},{7,6},{8,9},{9,8},{10,11... | collective-permute-start | bytes 2359304 | tf_op jit(solution)/shard_map/ppermute | solution.py:80
  124.9 7.7 %collective-permute-start.18 = (bf16[2,128,512]{2,1,0:T(8,128)(2,1)}, bf16[2,128,512]{2,1,0:T(8,128)(2,1)S(1)}, u32[]{:S(2)}, u32[]{:S(2)}) collective-permute-start(bf16[2,128,512]{2,1,0:T(8,128)(2,1)} %bitcast.31), channel_id=1, source_target_pairs={{0,1},{1,0},{2,3},{3,2},{4,5},{5,4},{6,7},{7,6},{8,9},{9,8},{10,11... | collective-permute-start | bytes 786440 | tf_op jit(solution)/shard_map/ppermute | solution.py:80
  125.0 4.7 %collective-permute-start.34 = (bf16[2,1,512]{2,0,1:T(2,128)(2,1)S(1)}, bf16[2,1,512]{2,0,1:T(2,128)(2,1)S(1)}, u32[]{:S(2)}, u32[]{:S(2)}) collective-permute-start(bf16[2,1,512]{2,0,1:T(2,128)(2,1)S(1)} %convert_element_type.268), channel_id=1, source_target_pairs={{0,1},{1,0},{2,3},{3,2},{4,5},{5,4},{6,7},{7,6},{8,9},{9,8},{10,11... | collective-permute-start | bytes 6152 | tf_op jit(solution)/shard_map/ppermute | solution.py:80
  129.8 5.1 %collective-permute-start.35 = (bf16[1,1,512]{2,0,1:T(2,128)(2,1)S(1)}, bf16[1,1,512]{2,0,1:T(2,128)(2,1)S(1)}, u32[]{:S(2)}, u32[]{:S(2)}) collective-permute-start(bf16[1,1,512]{2,0,1:T(2,128)(2,1)S(1)} %slice.197), channel_id=1, source_target_pairs={{0,2},{1,3},{2,0},{3,1},{4,6},{5,7},{6,4},{7,5},{8,10},{9,11},{10,... | collective-permute-start | bytes 3080 | tf_op jit(solution)/shard_map/ppermute | solution.py:80
  131.6 4.9 %collective-permute-start.48 = (f32[8,512]{1,0:T(8,128)S(1)}, f32[8,512]{1,0:T(8,128)S(1)}, u32[]{:S(2)}, u32[]{:S(2)}) collective-permute-start(f32[8,512]{1,0:T(8,128)S(1)} %add.324), channel_id=1, source_target_pairs={{0,2},{1,3},{2,0},{3,1},{4,6},{5,7},{6,4},{7,5},{8,10},{9,11},{10,... | collective-permute-start | bytes 49160 | tf_op jit(solution)/shard_map/ppermute | solution.py:80
  133.7 5.4 %collective-permute-start.19 = (bf16[1,128,512]{2,1,0:T(8,128)(2,1)S(1)}, bf16[1,128,512]{2,1,0:T(8,128)(2,1)S(1)}, u32[]{:S(2)}, u32[]{:S(2)}) collective-permute-start(bf16[1,128,512]{2,1,0:T(8,128)(2,1)S(1)} %slice.195), channel_id=1, source_target_pairs={{0,2},{1,3},{2,0},{3,1},{4,6},{5,7},{6,4},{7,5},{8,10},{9,11},{10,... | collective-permute-start | bytes 393224 | tf_op jit(solution)/shard_map/ppermute | solution.py:80
  134.9 5.9 %collective-permute-start.36 = (f32[1,512]{1,0:T(1,128)S(1)}, f32[1,512]{1,0:T(1,128)S(1)}, u32[]{:S(2)}, u32[]{:S(2)}) collective-permute-start(f32[1,512]{1,0:T(1,128)S(1)} %fusion.53), channel_id=1, source_target_pairs={{0,4},{1,5},{2,6},{3,7},{4,0},{5,1},{6,2},{7,3},{8,12},{9,13},{10,... | collective-permute-start | bytes 6152 | tf_op jit(solution)/shard_map/ppermute | solution.py:80
  136.4 6.0 %collective-permute-start.49 = (f32[8,512]{1,0:T(8,128)S(1)}, f32[8,512]{1,0:T(8,128)S(1)}, u32[]{:S(2)}, u32[]{:S(2)}) collective-permute-start(f32[8,512]{1,0:T(8,128)S(1)} %add.325), channel_id=1, source_target_pairs={{0,4},{1,5},{2,6},{3,7},{4,0},{5,1},{6,2},{7,3},{8,12},{9,13},{10,... | collective-permute-start | bytes 49160 | tf_op jit(solution)/shard_map/ppermute | solution.py:80
  142.4 5.5 %collective-permute-start.50 = (f32[8,512]{1,0:T(8,128)S(1)}, f32[8,512]{1,0:T(8,128)S(1)}, u32[]{:S(2)}, u32[]{:S(2)}) collective-permute-start(f32[8,512]{1,0:T(8,128)S(1)} %add.326), channel_id=1, source_target_pairs={{0,8},{1,9},{2,10},{3,11},{4,12},{5,13},{6,14},{7,15},{8,0},{9,1},... | collective-permute-start | bytes 49160 | tf_op jit(solution)/shard_map/ppermute | solution.py:80
  143.5 5.4 %collective-permute-start.21 = (bf16[32,512]{1,0:T(8,128)(2,1)S(1)}, bf16[32,512]{1,0:T(8,128)(2,1)S(1)}, u32[]{:S(2)}, u32[]{:S(2)}) collective-permute-start(bf16[32,512]{1,0:T(8,128)(2,1)S(1)} %dynamic-slice_convert_fusion.10), channel_id=1, source_target_pairs={{0,8},{1,9},{2,10},{3,11},{4,12},{5,13},{6,14},{7,15},{8,0},{9,1},... | collective-permute-start | bytes 98312 | tf_op jit(solution)/shard_map/ppermute | solution.py:80
  145.2 16.4 %collective-permute-start.38 = (f32[1,512]{1,0:T(1,128)S(1)}, f32[1,512]{1,0:T(1,128)S(1)}, u32[]{:S(2)}, u32[]{:S(2)}) collective-permute-start(f32[1,512]{1,0:T(1,128)S(1)} %add.317), channel_id=1, source_target_pairs={{0,16},{1,17},{2,18},{3,19},{4,20},{5,21},{6,22},{7,23},{8,24},{9,... | collective-permute-start | bytes 6152 | tf_op jit(solution)/shard_map/ppermute | solution.py:80
  147.9 14.8 %collective-permute-start.51 = (f32[8,512]{1,0:T(8,128)S(1)}, f32[8,512]{1,0:T(8,128)S(1)}, u32[]{:S(2)}, u32[]{:S(2)}) collective-permute-start(f32[8,512]{1,0:T(8,128)S(1)} %add.327), channel_id=1, source_target_pairs={{0,16},{1,17},{2,18},{3,19},{4,20},{5,21},{6,22},{7,23},{8,24},{9,... | collective-permute-start | bytes 49160 | tf_op jit(solution)/shard_map/ppermute | solution.py:80
  150.2 13.5 %collective-permute-start.11 = (bf16[1,512,384]{2,1,0:T(8,128)(2,1)S(1)}, bf16[1,512,384]{2,1,0:T(8,128)(2,1)S(1)}, u32[]{:S(2)}, u32[]{:S(2)}) collective-permute-start(bf16[1,512,384]{2,1,0:T(8,128)(2,1)S(1)} %slice.193), channel_id=1, source_target_pairs={{0,2},{1,3},{2,0},{3,1},{4,6},{5,7},{6,4},{7,5},{8,10},{9,11},{10,... | collective-permute-start | bytes 1179656 | tf_op jit(solution)/shard_map/ppermute | solution.py:80
  151.3 11.4 %collective-permute-start.22 = (bf16[16,512]{1,0:T(8,128)(2,1)S(1)}, bf16[16,512]{1,0:T(8,128)(2,1)S(1)}, u32[]{:S(2)}, u32[]{:S(2)}) collective-permute-start(bf16[16,512]{1,0:T(8,128)(2,1)S(1)} %dynamic-slice_convert_fusion.11), channel_id=1, source_target_pairs={{0,16},{1,17},{2,18},{3,19},{4,20},{5,21},{6,22},{7,23},{8,24},{9,... | collective-permute-start | bytes 49160 | tf_op jit(solution)/shard_map/ppermute | solution.py:80
  161.6 9.4 %collective-permute-start.26 = (bf16[2,512,512]{2,1,0:T(8,128)(2,1)}, bf16[2,512,512]{2,1,0:T(8,128)(2,1)S(1)}, u32[]{:S(2)}, u32[]{:S(2)}) collective-permute-start(bf16[2,512,512]{2,1,0:T(8,128)(2,1)} %pad_maximum_fusion.6), channel_id=1, source_target_pairs={{0,1},{1,0},{2,3},{3,2},{4,5},{5,4},{6,7},{7,6},{8,9},{9,8},{10,11... | collective-permute-start | bytes 3145736 | tf_op jit(solution)/shard_map/ppermute | solution.py:80
  161.6 16.0 %collective-permute-start.39 = (bf16[2,512,512]{2,1,0:T(8,128)(2,1)}, bf16[2,512,512]{2,1,0:T(8,128)(2,1)S(1)}, u32[]{:S(2)}, u32[]{:S(2)}) collective-permute-start(bf16[2,512,512]{2,1,0:T(8,128)(2,1)} %bitcast.174), channel_id=1, source_target_pairs={{0,1},{1,0},{2,3},{3,2},{4,5},{5,4},{6,7},{7,6},{8,9},{9,8},{10,11... | collective-permute-start | bytes 3145736 | tf_op jit(solution)/shard_map/ppermute | solution.py:80
  162.7 4.7 %collective-permute-start.23 = (bf16[16,512]{1,0:T(8,128)(2,1)S(1)}, bf16[16,512]{1,0:T(8,128)(2,1)S(1)}, u32[]{:S(2)}, u32[]{:S(2)}) collective-permute-start(bf16[16,512]{1,0:T(8,128)(2,1)S(1)} %add_convert_fusion.5), channel_id=1, source_target_pairs={{0,16},{1,17},{2,18},{3,19},{4,20},{5,21},{6,22},{7,23},{8,24},{9,... | collective-permute-start | bytes 49160 | tf_op jit(solution)/shard_map/ppermute | solution.py:80
  163.7 6.7 %collective-permute-start.12 = (bf16[256,384]{1,0:T(8,128)(2,1)S(1)}, bf16[256,384]{1,0:T(8,128)(2,1)S(1)}, u32[]{:S(2)}, u32[]{:S(2)}) collective-permute-start(bf16[256,384]{1,0:T(8,128)(2,1)S(1)} %fusion.50), channel_id=1, source_target_pairs={{0,4},{1,5},{2,6},{3,7},{4,0},{5,1},{6,2},{7,3},{8,12},{9,13},{10,... | collective-permute-start | bytes 589832 | tf_op jit(solution)/shard_map/ppermute | solution.py:80
  167.4 15.5 %collective-permute-start.24 = (bf16[32,512]{1,0:T(8,128)(2,1)S(1)}, bf16[32,512]{1,0:T(8,128)(2,1)S(1)}, u32[]{:S(2)}, u32[]{:S(2)}) collective-permute-start(bf16[32,512]{1,0:T(8,128)(2,1)S(1)} %maximum_select_fusion.11), channel_id=1, source_target_pairs={{0,8},{1,9},{2,10},{3,11},{4,12},{5,13},{6,14},{7,15},{8,0},{9,1},... | collective-permute-start | bytes 98312 | tf_op jit(solution)/shard_map/ppermute | solution.py:80
  170.5 4.7 %collective-permute-start.13 = (bf16[128,384]{1,0:T(8,128)(2,1)S(1)}, bf16[128,384]{1,0:T(8,128)(2,1)S(1)}, u32[]{:S(2)}, u32[]{:S(2)}) collective-permute-start(bf16[128,384]{1,0:T(8,128)(2,1)S(1)} %dynamic-slice_convert_fusion.5), channel_id=1, source_target_pairs={{0,8},{1,9},{2,10},{3,11},{4,12},{5,13},{6,14},{7,15},{8,0},{9,1},... | collective-permute-start | bytes 294920 | tf_op jit(solution)/shard_map/ppermute | solution.py:80
  171.5 14.9 %collective-permute-start.27 = (bf16[1,512,512]{2,1,0:T(8,128)(2,1)S(1)}, bf16[1,512,512]{2,1,0:T(8,128)(2,1)S(1)}, u32[]{:S(2)}, u32[]{:S(2)}) collective-permute-start(bf16[1,512,512]{2,1,0:T(8,128)(2,1)S(1)} %slice.192), channel_id=1, source_target_pairs={{0,2},{1,3},{2,0},{3,1},{4,6},{5,7},{6,4},{7,5},{8,10},{9,11},{10,... | collective-permute-start | bytes 1572872 | tf_op jit(solution)/shard_map/ppermute | solution.py:80
  175.2 5.5 %collective-permute-start.14 = (bf16[64,384]{1,0:T(8,128)(2,1)S(1)}, bf16[64,384]{1,0:T(8,128)(2,1)S(1)}, u32[]{:S(2)}, u32[]{:S(2)}) collective-permute-start(bf16[64,384]{1,0:T(8,128)(2,1)S(1)} %dynamic-slice_convert_fusion.9), channel_id=1, source_target_pairs={{0,16},{1,17},{2,18},{3,19},{4,20},{5,21},{6,22},{7,23},{8,24},{9,... | collective-permute-start | bytes 147464 | tf_op jit(solution)/shard_map/ppermute | solution.py:80
  178.0 17.2 %collective-permute-start.40 = (bf16[1,512,512]{2,1,0:T(8,128)(2,1)S(1)}, bf16[1,512,512]{2,1,0:T(8,128)(2,1)S(1)}, u32[]{:S(2)}, u32[]{:S(2)}) collective-permute-start(bf16[1,512,512]{2,1,0:T(8,128)(2,1)S(1)} %slice.191), channel_id=1, source_target_pairs={{0,2},{1,3},{2,0},{3,1},{4,6},{5,7},{6,4},{7,5},{8,10},{9,11},{10,... | collective-permute-start | bytes 1572872 | tf_op jit(solution)/shard_map/ppermute | solution.py:80
  180.7 5.2 %collective-permute-start.15 = (bf16[64,384]{1,0:T(8,128)(2,1)S(1)}, bf16[64,384]{1,0:T(8,128)(2,1)S(1)}, u32[]{:S(2)}, u32[]{:S(2)}) collective-permute-start(bf16[64,384]{1,0:T(8,128)(2,1)S(1)} %add_convert_fusion.4), channel_id=1, source_target_pairs={{0,16},{1,17},{2,18},{3,19},{4,20},{5,21},{6,22},{7,23},{8,24},{9,... | collective-permute-start | bytes 147464 | tf_op jit(solution)/shard_map/ppermute | solution.py:80
  182.9 39.7 %collective-permute-start.25 = (bf16[64,512]{1,0:T(8,128)(2,1)S(1)}, bf16[64,512]{1,0:T(8,128)(2,1)S(1)}, u32[]{:S(2)}, u32[]{:S(2)}) collective-permute-start(bf16[64,512]{1,0:T(8,128)(2,1)S(1)} %maximum_select_fusion.10), channel_id=1, source_target_pairs={{0,4},{1,5},{2,6},{3,7},{4,0},{5,1},{6,2},{7,3},{8,12},{9,13},{10,... | collective-permute-start | bytes 196616 | tf_op jit(solution)/shard_map/ppermute | solution.py:80
  185.9 31.7 %collective-permute-start.16 = (bf16[128,384]{1,0:T(8,128)(2,1)S(1)}, bf16[128,384]{1,0:T(8,128)(2,1)S(1)}, u32[]{:S(2)}, u32[]{:S(2)}) collective-permute-start(bf16[128,384]{1,0:T(8,128)(2,1)S(1)} %maximum_select_fusion.9), channel_id=1, source_target_pairs={{0,8},{1,9},{2,10},{3,11},{4,12},{5,13},{6,14},{7,15},{8,0},{9,1},... | collective-permute-start | bytes 294920 | tf_op jit(solution)/shard_map/ppermute | solution.py:80
  186.6 10.1 %collective-permute-start.28 = (bf16[256,512]{1,0:T(8,128)(2,1)S(1)}, bf16[256,512]{1,0:T(8,128)(2,1)S(1)}, u32[]{:S(2)}, u32[]{:S(2)}) collective-permute-start(bf16[256,512]{1,0:T(8,128)(2,1)S(1)} %fusion.43), channel_id=1, source_target_pairs={{0,4},{1,5},{2,6},{3,7},{4,0},{5,1},{6,2},{7,3},{8,12},{9,13},{10,... | collective-permute-start | bytes 786440 | tf_op jit(solution)/shard_map/ppermute | solution.py:80
  195.4 6.4 %collective-permute-start.41 = (bf16[256,512]{1,0:T(8,128)(2,1)S(1)}, bf16[256,512]{1,0:T(8,128)(2,1)S(1)}, u32[]{:S(2)}, u32[]{:S(2)}) collective-permute-start(bf16[256,512]{1,0:T(8,128)(2,1)S(1)} %fusion.44), channel_id=1, source_target_pairs={{0,4},{1,5},{2,6},{3,7},{4,0},{5,1},{6,2},{7,3},{8,12},{9,13},{10,... | collective-permute-start | bytes 786440 | tf_op jit(solution)/shard_map/ppermute | solution.py:80
  196.8 6.8 %collective-permute-start.29 = (bf16[128,512]{1,0:T(8,128)(2,1)S(1)}, bf16[128,512]{1,0:T(8,128)(2,1)S(1)}, u32[]{:S(2)}, u32[]{:S(2)}) collective-permute-start(bf16[128,512]{1,0:T(8,128)(2,1)S(1)} %dynamic-slice_convert_fusion.4), channel_id=1, source_target_pairs={{0,8},{1,9},{2,10},{3,11},{4,12},{5,13},{6,14},{7,15},{8,0},{9,1},... | collective-permute-start | bytes 393224 | tf_op jit(solution)/shard_map/ppermute | solution.py:80
  202.0 5.7 %collective-permute-start.42 = (bf16[128,512]{1,0:T(8,128)(2,1)S(1)}, bf16[128,512]{1,0:T(8,128)(2,1)S(1)}, u32[]{:S(2)}, u32[]{:S(2)}) collective-permute-start(bf16[128,512]{1,0:T(8,128)(2,1)S(1)} %dynamic-slice_convert_fusion.3), channel_id=1, source_target_pairs={{0,8},{1,9},{2,10},{3,11},{4,12},{5,13},{6,14},{7,15},{8,0},{9,1},... | collective-permute-start | bytes 393224 | tf_op jit(solution)/shard_map/ppermute | solution.py:80
  203.7 6.8 %collective-permute-start.30 = (bf16[64,512]{1,0:T(8,128)(2,1)S(1)}, bf16[64,512]{1,0:T(8,128)(2,1)S(1)}, u32[]{:S(2)}, u32[]{:S(2)}) collective-permute-start(bf16[64,512]{1,0:T(8,128)(2,1)S(1)} %dynamic-slice_convert_fusion.7), channel_id=1, source_target_pairs={{0,16},{1,17},{2,18},{3,19},{4,20},{5,21},{6,22},{7,23},{8,24},{9,... | collective-permute-start | bytes 196616 | tf_op jit(solution)/shard_map/ppermute | solution.py:80
  207.8 6.0 %collective-permute-start.43 = (bf16[64,512]{1,0:T(8,128)(2,1)S(1)}, bf16[64,512]{1,0:T(8,128)(2,1)S(1)}, u32[]{:S(2)}, u32[]{:S(2)}) collective-permute-start(bf16[64,512]{1,0:T(8,128)(2,1)S(1)} %dynamic-slice_convert_fusion.6), channel_id=1, source_target_pairs={{0,16},{1,17},{2,18},{3,19},{4,20},{5,21},{6,22},{7,23},{8,24},{9,... | collective-permute-start | bytes 196616 | tf_op jit(solution)/shard_map/ppermute | solution.py:80
  210.5 6.6 %collective-permute-start.31 = (bf16[64,512]{1,0:T(8,128)(2,1)S(1)}, bf16[64,512]{1,0:T(8,128)(2,1)S(1)}, u32[]{:S(2)}, u32[]{:S(2)}) collective-permute-start(bf16[64,512]{1,0:T(8,128)(2,1)S(1)} %add_convert_fusion.3), channel_id=1, source_target_pairs={{0,16},{1,17},{2,18},{3,19},{4,20},{5,21},{6,22},{7,23},{8,24},{9,... | collective-permute-start | bytes 196616 | tf_op jit(solution)/shard_map/ppermute | solution.py:80
  213.8 5.9 %collective-permute-start.44 = (bf16[64,512]{1,0:T(8,128)(2,1)S(1)}, bf16[64,512]{1,0:T(8,128)(2,1)S(1)}, u32[]{:S(2)}, u32[]{:S(2)}) collective-permute-start(bf16[64,512]{1,0:T(8,128)(2,1)S(1)} %add_convert_fusion.2), channel_id=1, source_target_pairs={{0,16},{1,17},{2,18},{3,19},{4,20},{5,21},{6,22},{7,23},{8,24},{9,... | collective-permute-start | bytes 196616 | tf_op jit(solution)/shard_map/ppermute | solution.py:80
  217.1 5.0 %collective-permute-start.32 = (bf16[128,512]{1,0:T(8,128)(2,1)S(1)}, bf16[128,512]{1,0:T(8,128)(2,1)S(1)}, u32[]{:S(2)}, u32[]{:S(2)}) collective-permute-start(bf16[128,512]{1,0:T(8,128)(2,1)S(1)} %maximum_select_fusion.7), channel_id=1, source_target_pairs={{0,8},{1,9},{2,10},{3,11},{4,12},{5,13},{6,14},{7,15},{8,0},{9,1},... | collective-permute-start | bytes 393224 | tf_op jit(solution)/shard_map/ppermute | solution.py:80
  217.7 8.9 %collective-permute-start.17 = (bf16[256,384]{1,0:T(8,128)(2,1)S(1)}, bf16[256,384]{1,0:T(8,128)(2,1)S(1)}, u32[]{:S(2)}, u32[]{:S(2)}) collective-permute-start(bf16[256,384]{1,0:T(8,128)(2,1)S(1)} %maximum_select_fusion.5), channel_id=1, source_target_pairs={{0,4},{1,5},{2,6},{3,7},{4,0},{5,1},{6,2},{7,3},{8,12},{9,13},{10,... | collective-permute-start | bytes 589832 | tf_op jit(solution)/shard_map/ppermute | solution.py:80
  219.7 5.0 %collective-permute-start.45 = (bf16[128,512]{1,0:T(8,128)(2,1)S(1)}, bf16[128,512]{1,0:T(8,128)(2,1)S(1)}, u32[]{:S(2)}, u32[]{:S(2)}) collective-permute-start(bf16[128,512]{1,0:T(8,128)(2,1)S(1)} %maximum_select_fusion.8), channel_id=1, source_target_pairs={{0,8},{1,9},{2,10},{3,11},{4,12},{5,13},{6,14},{7,15},{8,0},{9,1},... | collective-permute-start | bytes 393224 | tf_op jit(solution)/shard_map/ppermute | solution.py:80
  222.2 8.2 %collective-permute-start.33 = (bf16[256,512]{1,0:T(8,128)(2,1)S(1)}, bf16[256,512]{1,0:T(8,128)(2,1)S(1)}, u32[]{:S(2)}, u32[]{:S(2)}) collective-permute-start(bf16[256,512]{1,0:T(8,128)(2,1)S(1)} %maximum_select_fusion.3), channel_id=1, source_target_pairs={{0,4},{1,5},{2,6},{3,7},{4,0},{5,1},{6,2},{7,3},{8,12},{9,13},{10,... | collective-permute-start | bytes 786440 | tf_op jit(solution)/shard_map/ppermute | solution.py:80
  224.8 8.4 %collective-permute-start.46 = (bf16[256,512]{1,0:T(8,128)(2,1)S(1)}, bf16[256,512]{1,0:T(8,128)(2,1)S(1)}, u32[]{:S(2)}, u32[]{:S(2)}) collective-permute-start(bf16[256,512]{1,0:T(8,128)(2,1)S(1)} %maximum_select_fusion.4), channel_id=1, source_target_pairs={{0,4},{1,5},{2,6},{3,7},{4,0},{5,1},{6,2},{7,3},{8,12},{9,13},{10,... | collective-permute-start | bytes 786440 | tf_op jit(solution)/shard_map/ppermute | solution.py:80
  (76 other events, 374.8 us)

commit v2 on v1

v2 whole, which is shorter than its diff:
```python
import functools

import jax
import jax.numpy as jnp
from jax import lax
from jax.experimental import pallas as pl
from jax.experimental.pallas import tpu as pltpu
from jax.sharding import PartitionSpec as P

HEAD_DIM = 64
SEQ = 128
EPSILON = 1e-05
NEG_FILL = -1e30
BF = jnp.bfloat16
F32 = jnp.float32
AXES = ("dp", "head")
CHUNK = 128
VMEM_LIMIT = 8 * 2**20


def nn(a, b):
    return lax.dot_general(a, b, (((1,), (0,)), ((), ())), preferred_element_type=F32)


def nt(a, b):
    return lax.dot_general(a, b, (((1,), (1,)), ((), ())), preferred_element_type=F32)


def tn(a, b):
    return lax.dot_general(a, b, (((0,), (0,)), ((), ())), preferred_element_type=F32)


class Kernels:
    def __init__(self):
        self.token = jnp.zeros((8, 128), F32)

    def call(self, body, outs, *args, scalars=0, scratch=(), name=None):
        vmem = pl.BlockSpec(memory_space=pltpu.VMEM)
        smem = pl.BlockSpec(memory_space=pltpu.SMEM)
        plain, count = len(args) - scalars, len(args)

        last = count + 1 + len(outs)

        def ordered(*refs):
            refs[last][...] = refs[count][...]
            body(*refs[:count], *refs[count + 1 : last], *refs[last + 1 :])

        got = pl.pallas_call(
            ordered,
            out_shape=[jax.ShapeDtypeStruct(*out[:2]) for out in outs]
            + [jax.ShapeDtypeStruct((8, 128), F32)],
            in_specs=[vmem] * plain + [smem] * scalars + [vmem],
            out_specs=[vmem] * (len(outs) + 1),
            compiler_params=pltpu.CompilerParams(vmem_limit_bytes=VMEM_LIMIT),
            scratch_shapes=[pltpu.VMEM(*s) for s in scratch],
            cost_estimate=pl.CostEstimate(flops=0, bytes_accessed=0, transcendentals=0),
            name=name,
        )(*args, self.token)
        self.token = got[-1]
        return got[:-1]


def centred(rows):
    centre = rows - jnp.mean(rows, axis=-1, keepdims=True)
    spread = jnp.mean(centre * centre, axis=-1, keepdims=True)
    rstd = lax.rsqrt(spread + EPSILON)
    return centre * rstd, rstd


def norm_back(grad, rows, gain):
    xhat, rstd = centred(rows)
    q = grad * gain
    inner = jnp.mean(q * xhat, axis=-1, keepdims=True)
    row = rstd * (q - jnp.mean(q, axis=-1, keepdims=True) - xhat * inner)
    return row, jnp.sum(grad * xhat, axis=0, keepdims=True), jnp.sum(grad, axis=0, keepdims=True)


def prep_kernel(res, cot, gain, shift, first, first_t, out_low, out_t):
    for r in range(0, res.shape[0], CHUNK):
        xhat, _ = centred(res[r : r + CHUNK, :])
        low = (xhat * gain[...] + shift[...]).astype(BF)
        first[r : r + CHUNK, :] = low
        first_t[:, r : r + CHUNK] = low.T
        low = cot[r : r + CHUNK, :].astype(BF)
        out_low[r : r + CHUNK, :] = low
        out_t[:, r : r + CHUNK] = low.T


def lanes_low(shape):
    return lax.broadcasted_iota(jnp.int32, shape, 1) < HEAD_DIM


def half_turn(block):
    return jnp.concatenate([block[:, HEAD_DIM:], block[:, :HEAD_DIM]], 1)


def mask_of(start, count, length):
    m = lax.broadcasted_iota(jnp.int32, (SEQ, SEQ), 0)
    n = lax.broadcasted_iota(jnp.int32, (SEQ, SEQ), 1)
    group_m = jnp.maximum((m * 43) >> 8, start)
    group_n = jnp.maximum((n * 43) >> 8, start)
    return (m < length) & ((group_m <= group_n) | (m < count))


def attend(first, weight, triple, probs, mixed, scalars, seqs):
    low = lanes_low((SEQ, 2 * HEAD_DIM))
    zero = jnp.zeros((SEQ, 2 * HEAD_DIM), BF)
    triple[...] = nn(first[...], weight[...]).astype(BF)
    base, starts, counts, lengths = scalars
    for s in range(seqs):
        at = slice(s * SEQ, (s + 1) * SEQ)
        b0, b1, b2 = (triple[at, c * 128 : (c + 1) * 128] for c in range(3))
        seen = mask_of(*(ref[base + s] for ref in (starts, counts, lengths)))
        pairs = (
            (jnp.where(low, half_turn(b0), zero), b0, jnp.where(low, b1, zero)),
            (jnp.where(low, b2, zero), half_turn(b1), jnp.where(low, zero, b2)),
        )
        out = None
        for h, (keys, queries, values) in enumerate(pairs):
            score = jnp.where(seen, nt(keys, queries) * HEAD_DIM**-0.5, NEG_FILL)
            weights = jnp.exp(score - jnp.max(score, axis=0, keepdims=True))
            prob = weights * (1.0 / jnp.sum(weights, axis=0, keepdims=True))
            probs[2 * s + h] = prob
            part = tn(prob.astype(BF), values)
            out = part if out is None else out + part
        mixed[at, :] = out.astype(BF)


def attend_back(middle_low, proj, triple, probs, seqs, gtl, grad_mixed):
    low = lanes_low((SEQ, 2 * HEAD_DIM))
    zero = jnp.zeros((SEQ, 2 * HEAD_DIM), BF)
    factor = HEAD_DIM**-0.5
    grad_mixed[...] = nt(middle_low[...], proj[: 2 * HEAD_DIM, :]).astype(BF)
    for s in range(seqs):
        at = slice(s * SEQ, (s + 1) * SEQ)
        b0, b1, b2 = (triple[at, c * 128 : (c + 1) * 128] for c in range(3))
        r0, r1, r2 = (half_turn(b) for b in (b0, b1, b2))
        gm = grad_mixed[at, :]
        grads = []
        for h, values in enumerate((jnp.where(low, b1, zero), jnp.where(low, zero, b2))):
            prob = probs[2 * s + h]
            grad_prob = nt(values, gm)
            inner = jnp.sum(grad_prob * prob, axis=0, keepdims=True)
            grads.append(((prob * (grad_prob - inner)).astype(BF), prob.astype(BF)))
        (ds0, p0), (ds1, p1) = grads
        gtl[at, 0:128] = (jnp.where(low, tn(ds0, r0), nn(ds0, r0)) * factor).astype(BF)
        gtl[at, 128:256] = jnp.where(low, nn(p0, gm), tn(ds1, r2) * factor).astype(BF)
        gtl[at, 256:384] = jnp.where(low, nn(ds1, r1) * factor, nn(p1, gm)).astype(BF)


def gelu_parts(x):
    c0, c1 = 0.7978845608028654, 0.044715
    square = x * x
    t = jnp.tanh(x * (c0 + (c0 * c1) * square))
    h = 0.5 * (1.0 + t)
    slope = h + (0.5 * x) * (1.0 - t * t) * (c0 + (3.0 * c0 * c1) * square)
    return x * h, slope


def pack_kernel(proj, bias, place, base, out):
    rows, span = proj.shape[0], bias.shape[1]
    out[:rows, :] = proj[...]
    if span < out.shape[1]:
        out[rows:, :] = jnp.zeros((out.shape[0] - rows, out.shape[1]), out.dtype)
    out[rows:, :span] = jnp.broadcast_to(bias[...], (out.shape[0] - rows, span))


def pair_kernel(axis, span, *refs):
    out = refs[-1]
    for k, part in enumerate(refs[:-1]):
        if axis == 0:
            out[k * span : (k + 1) * span, :] = part[:span, :]
        else:
            out[:, k * span : (k + 1) * span] = part[:, :span]


def relay_kernel(value, out):
    out[...] = value[...]


def attend_kernel(units, seqs, *refs):
    refs = list(refs)
    take = lambda n: [refs.pop(0) for _ in range(n)]
    (first,) = take(1)
    weights = take(units)
    scalars = take(4)
    scalars = [scalars[0][0]] + scalars[1:]
    triples, probs, mixeds = take(units), take(units), take(units)
    for u in range(units):
        attend(first, weights[u], triples[u], probs[u], mixeds[u], scalars, seqs)


def project_kernel(units, *refs):
    mixeds, projs, acc = refs[:units], refs[units : 2 * units], refs[2 * units]
    acc[...] = sum(nn(mixeds[u][...], projs[u][: 2 * HEAD_DIM, :]) for u in range(units))


def second_kernel(units, *refs):
    refs = list(refs)
    take = lambda n: [refs.pop(0) for _ in range(n)]
    mixeds, projs = take(units), take(units)
    acc, residual, bias, gain, shift, middle, second, second_t = refs
    for r in range(0, acc.shape[0], CHUNK):
        at = slice(r, r + CHUNK)
        out = acc[at, :] + sum(
            nn(mixeds[u][at, :], projs[u][: 2 * HEAD_DIM, :]) for u in range(units)
        )
        out = residual[at, :] + out + bias[...]
        middle[at, :] = out
        xhat, _ = centred(out)
        low = (xhat * gain[...] + shift[...]).astype(BF)
        second[at, :] = low
        second_t[:, at] = low.T


def hidden_kernel(slots, *refs):
    refs = list(refs)
    take = lambda n: [refs.pop(0) for _ in range(n)]
    second, out_t = take(2)
    ups, biases = take(slots), take(slots)
    acts, slopes, grads = take(slots), take(slots), take(slots)
    for j in range(slots):
        bias = biases[j][-1:, : ups[j].shape[1]].astype(F32)
        for r in range(0, second.shape[0], 2 * CHUNK):
            at = slice(r, r + 2 * CHUNK)
            act, slope = gelu_parts(nn(second[at, :], ups[j][...]) + bias)
            acts[j][at, :] = act.astype(BF)
            slopes[j][at, :] = slope
        grads[j][...] = nn(out_t[...], acts[j][...]).astype(grads[j].dtype)


def hidden_back_kernel(slots, first_call, *refs):
    refs = list(refs)
    take = lambda n: [refs.pop(0) for _ in range(n)]
    out_low, second_t = take(2)
    ups, downs, slopes = take(slots), take(slots), take(slots)
    acc_in = None if first_call else take(1)[0]
    grads, biases = take(slots), take(slots)
    (acc,) = take(1)
    pre = take(slots)
    for j in range(slots):
        total = 0.0
        for r in range(0, out_low.shape[0], 2 * CHUNK):
            at = slice(r, r + 2 * CHUNK)
            low = (nt(out_low[at, :], downs[j][...]) * slopes[j][at, :]).astype(BF)
            pre[j][at, :] = low
            total = total + jnp.sum(low.astype(F32), axis=0, keepdims=True)
        biases[j][...] = total
        grads[j][...] = nn(second_t[...], pre[j][...]).astype(grads[j].dtype)
    for r in range(0, out_low.shape[0], 2 * CHUNK):
        at = slice(r, r + 2 * CHUNK)
        out = sum(nt(pre[j][at, :], ups[j][...]) for j in range(slots))
        acc[at, :] = out if first_call else acc_in[at, :] + out


def middle_kernel(grad_second, middle, gain, cot, grad_middle, middle_low, middle_t, sums):
    totals = [0.0, 0.0, 0.0]
    for r in range(0, cot.shape[0], CHUNK):
        at = slice(r, r + CHUNK)
        row, dgain, dshift = norm_back(grad_second[at, :], middle[at, :], gain[...])
        grad = cot[at, :] + row
        grad_middle[at, :] = grad
        low = grad.astype(BF)
        middle_low[at, :] = low
        middle_t[:, at] = low.T
        parts = (jnp.sum(grad, axis=0, keepdims=True), dgain, dshift)
        totals = [t + p for t, p in zip(totals, parts)]
    for i, t in enumerate(totals):
        sums[i : i + 1, :] = t


def attend_back_kernel(units, group, seqs, *refs):
    refs = list(refs)
    take = lambda n: [refs.pop(0) for _ in range(n)]
    middle_low, middle_t, first_t = take(3)
    projs, triples, probs, mixeds = take(units), take(units), take(units), take(units)
    gtls, grads, grad_mixed = take(units), take(units * group), take(units)
    heads = 2 // group
    for u in range(units):
        attend_back(middle_low, projs[u], triples[u], probs[u], seqs, gtls[u], grad_mixed[u])
        triple_grad = nn(first_t[...], gtls[u][...])
        proj_grad = nn(middle_t[...], mixeds[u][...])
        for k in range(group):
            out, span, small = grads[u * group + k], 3 * HEAD_DIM * heads, HEAD_DIM * heads
            out[:, :span] = triple_grad[:, k * span : (k + 1) * span].astype(out.dtype)
            out[:, span:] = proj_grad[:, k * small : (k + 1) * small].astype(out.dtype)


def input_kernel(units, *refs):
    refs = list(refs)
    take = lambda n: [refs.pop(0) for _ in range(n)]
    gtls, weights = take(units), take(units)
    residual, gain, grad_middle, cot = take(4)
    grad_input, sums = take(2)
    totals = [0.0, 0.0, 0.0]
    for r in range(0, cot.shape[0], CHUNK):
        at = slice(r, r + CHUNK)
        grad = sum(nt(gtls[u][at, :], weights[u][...]) for u in range(units))
        row, dgain, dshift = norm_back(grad, residual[at, :], gain[...])
        grad_input[at, :] = grad_middle[at, :] + row
        parts = (jnp.sum(cot[at, :], axis=0, keepdims=True), dgain, dshift)
        totals = [t + p for t, p in zip(totals, parts)]
    for i, t in enumerate(totals):
        sums[i : i + 1, :] = t


def output_kernel(slots, *refs):
    acts, downs = refs[:slots], refs[slots : 2 * slots]
    middle, bias, out = refs[2 * slots :]
    for r in range(0, middle.shape[0], 2 * CHUNK):
        at = slice(r, r + 2 * CHUNK)
        total = sum(nn(acts[j][at, :], downs[j][...]) for j in range(slots))
        out[at, :] = middle[at, :] + total + bias[...]


def total(terms):
    out = terms[0]
    for term in terms[1:]:
        out = out + term
    return out


def read(refs, spots, at):
    return total([refs[i][pl.ds(first + at[0], at[1]), :].astype(F32) for i, first in spots])


def send_kernel(spots, rows, *refs):
    out = refs[-1]
    for k, spot in enumerate(spots):
        out[k * rows : (k + 1) * rows, :] = read(refs, spot, (0, rows)).astype(out.dtype)


def halve_kernel(spots, rows, bit, *refs):
    count = len(refs) - len(spots) - 2
    place, stays, send = refs[count], refs[count + 1 : -1], refs[-1]
    half = rows // 2
    mine = (place[0] // bit) % 2
    for k, spot in enumerate(spots):
        stays[k][...] = read(refs, spot, (pl.multiple_of(mine * half, half), half))
        leave = read(refs, spot, (pl.multiple_of((1 - mine) * half, half), half))
        send[k * half : (k + 1) * half, :] = leave.astype(BF)


def whole_kernel(spots, rows, *refs):
    keep, send = refs[-2:]
    value = read(refs, spots[0], (0, rows))
    keep[...] = value
    send[...] = value.astype(BF)


def join_kernel(bit, own, other, place, out):
    half = own.shape[0]
    mine = (place[0] // bit) % 2
    out[pl.ds(pl.multiple_of(mine * half, half), half), :] = own[...].astype(out.dtype)
    out[pl.ds(pl.multiple_of((1 - mine) * half, half), half), :] = other[...].astype(out.dtype)


def finish_kernel(bit, turned, own, other, place, *refs):
    outs, low = refs[:-1], refs[-1]
    join_kernel(bit, own, other, place, low)
    col = 0
    for out, turn in zip(outs, turned):
        span = out.shape[0] if turn else out.shape[1]
        part = low[:, col : col + span]
        out[...] = part.T if turn else part
        col += span


def vector_kernel(parts, *refs):
    out = refs[-1]
    out[...] = jnp.zeros_like(out)
    row = 0
    for ref, n in zip(refs, parts):
        out[row : row + n, : ref.shape[1]] = ref[:n, :]
        row += n


def vector_add_kernel(bit, heads, fixed, mine, got, out):
    out[:fixed, :] = mine[:fixed, :] + got[:fixed, :]
    for k in range(heads):
        other = fixed + (k ^ bit if bit < heads else k)
        out[fixed + k : fixed + k + 1, :] = (
            mine[fixed + k : fixed + k + 1, :] + got[other : other + 1, :]
        )


class Links:
    def __init__(self, mesh):
        self.dp, self.head = mesh.shape["dp"], mesh.shape["head"]

    def swap(self, value, bit):
        total = self.dp * self.head
        return lax.ppermute(value, AXES, [(i, i ^ bit) for i in range(total)])


class Chain:
    def __init__(self, links, kernels, place):
        self.links, self.kernels, self.place = links, kernels, place
        self.slots, self.bit = {}, 2

    def give(self, slot, value):
        self.rows, self.cols = value.shape
        if slot % 2:
            got = self.links.swap(value, 1)
            self.slots.setdefault(slot - 1, []).append((got, 0))
        else:
            self.slots.setdefault(slot, []).append((value, 0))

    def spots(self, sums):
        arrays, spots = [], []
        for terms in sums:
            spots.append([])
            for value, first in terms:
                known = [i for i, a in enumerate(arrays) if a is value]
                if not known:
                    arrays.append(value)
                    known = [len(arrays) - 1]
                spots[-1].append((known[0], first))
        return arrays, spots

    def head(self):
        leave = [k for k in self.slots if k & self.bit]
        arrays, spots = self.spots([self.slots[k] for k in leave])
        (send,) = self.kernels.call(
            functools.partial(send_kernel, spots, self.rows),
            [((len(leave) * self.rows, self.cols), BF)],
            *arrays,
            name="send",
        )
        got = self.links.swap(send, self.bit)
        for i, k in enumerate(leave):
            del self.slots[k]
            self.slots[k ^ self.bit].append((got, i * self.rows))
        self.bit *= 2

    def fold(self, slot):
        arrays, spots = self.spots([self.slots[slot]])
        (value,) = self.kernels.call(
            functools.partial(send_kernel, spots, self.rows),
            [((self.rows, self.cols), F32)],
            *arrays,
            name="fold",
        )
        self.slots[slot] = [(value, 0)]

    def halve(self, bit):
        keys = list(self.slots)
        arrays, spots = self.spots([self.slots[k] for k in keys])
        half = self.rows // 2
        got = self.kernels.call(
            functools.partial(halve_kernel, spots, self.rows, bit),
            [((half, self.cols), F32)] * len(keys) + [((len(keys) * half, self.cols), BF)],
            *arrays,
            self.place,
            scalars=1,
            name="halve",
        )
        came = self.links.swap(got[-1], bit * self.links.head)
        self.slots = {k: [(got[i], 0), (came, i * half)] for i, k in enumerate(keys)}
        self.rows = half

    def whole(self, bit):
        arrays, spots = self.spots([self.slots[0]])
        keep, send = self.kernels.call(
            functools.partial(whole_kernel, spots, self.rows),
            [((self.rows, self.cols), F32), ((self.rows, self.cols), BF)],
            *arrays,
            name="whole",
        )
        self.slots = {0: [(keep, 0), (self.links.swap(send, bit * self.links.head), 0)]}

    def settle(self, bit):
        arrays, spots = self.spots([self.slots[0]])
        (self.own,) = self.kernels.call(
            functools.partial(send_kernel, spots, self.rows),
            [((self.rows, self.cols), BF)],
            *arrays,
            name="settle",
        )
        self.got, self.last = self.links.swap(self.own, bit * self.links.head), bit

    def double(self, bit):
        self.rows *= 2
        (self.own,) = self.kernels.call(
            functools.partial(join_kernel, self.last),
            [((self.rows, self.cols), BF)],
            self.own,
            self.got,
            self.place,
            scalars=1,
            name="join",
        )
        self.got, self.last = self.links.swap(self.own, bit * self.links.head), bit

    def finish(self, outs, turned):
        return self.kernels.call(
            functools.partial(finish_kernel, self.last, turned),
            [(o, F32, True) for o in outs],
            self.own,
            self.got,
            self.place,
            scalars=1,
            scratch=[((2 * self.rows, self.cols), F32)],
            name="finish",
        )


def make(mesh):
    links = Links(mesh)
    nslots = links.head
    bits = [2**k for k in range(links.dp.bit_length() - 1)]

    def shards(
        residual_in,
        cotangent,
        triple_weight,
        proj_weight,
        up_weight,
        up_bias,
        down_weight,
        proj_bias,
        down_bias,
        first_gain,
        first_shift,
        second_gain,
        second_shift,
        start_steps,
        cond_counts,
        valid_lengths,
    ):
        kernels = Kernels()
        call = kernels.call
        rows, width = residual_in.shape
        seqs = rows // SEQ
        hidden = up_weight.shape[1]
        row = lambda v: v.reshape(1, -1)
        proj_bias, down_bias, first_gain, first_shift, second_gain, second_shift = map(
            row, (proj_bias, down_bias, first_gain, first_shift, second_gain, second_shift)
        )
        place = lax.axis_index("dp").astype(jnp.int32).reshape(1)
        base = (lax.axis_index("head") * seqs).astype(jnp.int32).reshape(1)
        scalars = (base, start_steps, cond_counts, valid_lengths)
        group = 2 * HEAD_DIM // proj_weight.shape[0]
        units = nslots // group
        (packed,) = call(
            pack_kernel,
            [((proj_weight.shape[0] + 16, width), BF)],
            proj_weight,
            row(up_bias),
            place,
            base,
            scalars=2,
            name="pack",
        )

        own = {"t": triple_weight, "p": packed, "u": up_weight, "d": down_weight}
        slots = {}
        for key, value in own.items():
            far = {0: value}
            bit = nslots // 2
            while bit > 1:
                far.update({k | bit: links.swap(v, bit) for k, v in list(far.items())})
                bit //= 2
            far[1] = links.swap(value, 1)
            slots[key] = far

        def relay(key, k):
            value = slots[key][k]
            (value,) = call(relay_kernel, [(value.shape, BF)], value, name="relay")
            slots[key][k + 1] = links.swap(value, 1)

        def unit_weight(key, u, axis):
            parts = [slots[key][k] for k in range(u * group, (u + 1) * group)]
            if group == 1:
                return parts[0]
            span = own[key].shape[axis] - (16 if key == "p" else 0)
            shape = (group * span, width) if axis == 0 else (width, group * span)
            body = functools.partial(pair_kernel, axis, span)
            return call(body, [(shape, BF)], *parts, name="pair")[0]

        first, first_t, out_low, out_t = call(
            prep_kernel,
            [((rows, width), BF), ((width, rows), BF)] * 2,
            residual_in,
            cotangent,
            first_gain,
            first_shift,
            name="prep",
        )
        triple_w, proj_w, triples, probs, mixeds = {}, {}, {}, {}, {}

        def attend_call(which):
            n = len(which)
            for u in which:
                triple_w[u] = unit_weight("t", u, 1)
            got = call(
                functools.partial(attend_kernel, n, seqs),
                [((rows, 6 * HEAD_DIM), BF)] * n
                + [((2 * seqs, SEQ, SEQ), F32)] * n
                + [((rows, 2 * HEAD_DIM), BF)] * n,
                first,
                *(triple_w[u] for u in which),
                *scalars,
                scalars=4,
                name="attend",
            )
            for i, u in enumerate(which):
                triples[u], probs[u], mixeds[u] = got[i], got[n + i], got[2 * n + i]

        early = list(range(max(1, 2 // group)))
        attend_call(early)
        for u in early:
            proj_w[u] = unit_weight("p", u, 0)
        (acc,) = call(
            functools.partial(project_kernel, len(early)),
            [((rows, width), F32)],
            *(mixeds[u] for u in early),
            *(proj_w[u] for u in early),
            name="project",
        )
        late = [u for u in range(units) if u not in early]
        for k in range(2, nslots, 2):
            relay("t", k)
            for u in sorted({k // group, (k + 1) // group}):
                attend_call([u])
                if u * group <= k:
                    relay("p", k)
        for u in late:
            proj_w[u] = unit_weight("p", u, 0)
        middle, second, second_t = call(
            functools.partial(second_kernel, len(late)),
            [((rows, width), F32), ((rows, width), BF), ((width, rows), BF)],
            *(mixeds[u] for u in late),
            *(proj_w[u] for u in late),
            acc,
            residual_in,
            proj_bias,
            second_gain,
            second_shift,
            name="second",
        )

        def kind(k):
            return BF if k % 2 else F32

        acts, slopes, biases = {}, {}, {}
        down_sum, up_sum, attn_sum = (Chain(links, kernels, place) for _ in range(3))

        def hidden_call(which):
            n = len(which)
            got = call(
                functools.partial(hidden_kernel, n),
                [((rows, hidden), BF)] * n
                + [((rows, hidden), F32)] * n
                + [((width, hidden), kind(k)) for k in which],
                second,
                out_t,
                *(slots["u"][k] for k in which),
                *(slots["p"][k] for k in which),
                name="hidden",
            )
            for i, k in enumerate(which):
                acts[k], slopes[k] = got[i], got[n + i]
                down_sum.give(k, got[2 * n + i])

        def hidden_back_call(which, *acc):
            n = len(which)
            got = call(
                functools.partial(hidden_back_kernel, n, not acc),
                [((width, hidden), kind(k)) for k in which]
                + [((1, hidden), F32)] * n
                + [((rows, width), F32)],
                out_low,
                second_t,
                *(slots["u"][k] for k in which),
                *(slots["d"][k] for k in which),
                *(slopes[k] for k in which),
                *acc,
                scratch=[((rows, hidden), BF)] * n,
                name="hidden_back",
            )
            for i, k in enumerate(which):
                up_sum.give(k, got[i])
                biases[k] = got[n + i]
            return got[2 * n]

        hidden_call([0, 1])
        acc = hidden_back_call([0, 1])
        for k in range(2, nslots, 2):
            relay("u", k)
            hidden_call([k])
            if k == 2:
                down_sum.fold(0)
            hidden_call([k + 1])
            if k == 2:
                up_sum.fold(0)
        for k in range(2, nslots, 2):
            relay("d", k)
            acc = hidden_back_call([k], acc)
            if k == 2:
                down_sum.head()
            acc = hidden_back_call([k + 1], acc)
        grad_middle, middle_low, middle_t, sums_middle = call(
            middle_kernel,
            [((rows, width), F32), ((rows, width), BF), ((width, rows), BF), ((8, width), F32)],
            acc,
            middle,
            second_gain,
            cotangent,
            name="middle",
        )
        up_sum.head()
        while up_sum.bit < nslots:
            down_sum.head()
            up_sum.head()

        attn_width = 8 * HEAD_DIM // group
        gtls = {}

        def attend_back_call(which):
            n = len(which)
            got = call(
                functools.partial(attend_back_kernel, n, group, seqs),
                [((rows, 6 * HEAD_DIM), BF)] * n
                + [((width, attn_width), kind(k)) for u in which for k in range(group * u, group * u + group)],
                middle_low,
                middle_t,
                first_t,
                *(proj_w[u] for u in which),
                *(triples[u] for u in which),
                *(probs[u] for u in which),
                *(mixeds[u] for u in which),
                scratch=[((rows, 2 * HEAD_DIM), BF)] * n,
                name="attend_back",
            )
            for i, u in enumerate(which):
                gtls[u] = got[i]
                for j in range(group):
                    attn_sum.give(u * group + j, got[n + i * group + j])

        attend_back_call(late[::-1])
        down_sum.halve(bits[0])
        attend_back_call(early[::-1])
        attn_sum.head()
        while attn_sum.bit < nslots:
            attn_sum.head()
        grad_input, sums_input = call(
            functools.partial(input_kernel, units),
            [((rows, width), F32, True), ((8, width), F32)],
            *(gtls[u] for u in range(units)),
            *(triple_w[u] for u in range(units)),
            residual_in,
            first_gain,
            grad_middle,
            cotangent,
            name="input",
        )
        (vector,) = call(
            functools.partial(vector_kernel, [3, 3] + [1] * nslots),
            [((16, width), F32)],
            sums_middle,
            sums_input,
            *(biases[k] for k in range(nslots)),
            name="vector",
        )
        vector_bits = [2**k for k in range((links.dp * links.head).bit_length() - 1)]
        vector_got = links.swap(vector, vector_bits[0])

        def vector_step():
            nonlocal vector, vector_got
            bit = vector_bits.pop(0)
            (vector,) = call(
                functools.partial(vector_add_kernel, bit, nslots, 6),
                [((16, width), F32)],
                vector,
                vector_got,
                name="vector_add",
            )
            if vector_bits:
                vector_got = links.swap(vector, vector_bits[0])

        up_sum.halve(bits[0])
        down_sum.halve(bits[1])
        for bit in bits[2:-1]:
            down_sum.halve(bit)
        (block_out,) = call(
            functools.partial(output_kernel, nslots),
            [((rows, width), F32, True)],
            *(acts[k] for k in range(nslots)),
            *(slots["d"][k] for k in range(nslots)),
            middle,
            down_bias,
            name="output",
        )
        vector_step()
        up_sum.halve(bits[1])
        for bit in bits[2:-1]:
            up_sum.halve(bit)
        down_sum.whole(bits[-1])
        attn_sum.halve(bits[0])
        vector_step()
        up_sum.whole(bits[-1])
        down_sum.settle(bits[-2])
        for bit in bits[1:-1]:
            attn_sum.halve(bit)
        vector_step()
        up_sum.settle(bits[-2])
        back = bits[-3::-1]
        for bit in back:
            down_sum.double(bit)
        attn_sum.whole(bits[-1])
        vector_step()
        for bit in back:
            up_sum.double(bit)
        attn_sum.settle(bits[-2])
        while vector_bits:
            vector_step()
        (grad_down,) = down_sum.finish([(hidden, width)], [True])
        (grad_up,) = up_sum.finish([(width, hidden)], [False])
        for bit in back:
            attn_sum.double(bit)
        grad_triple, grad_proj = attn_sum.finish(
            [(width, 3 * attn_width // 4), (attn_width // 4, width)], [False, True]
        )
        return (
            block_out,
            grad_input,
            grad_triple,
            grad_proj,
            grad_up,
            vector[6, :hidden],
            grad_down,
            vector[0],
            vector[3],
            vector[4],
            vector[5],
            vector[1],
            vector[2],
        )

    return shards


def solution(mesh):
    in_specs = (
        P(("dp", "head"), None),
        P(("dp", "head"), None),
        P(None, "head"),
        P("head", None),
        P(None, "head"),
        P("head"),
        P("head", None),
        P(),
        P(),
        P(),
        P(),
        P(),
        P(),
        P("dp"),
        P("dp"),
        P("dp"),
    )
    out_specs = (
        P(("dp", "head"), None),
        P(("dp", "head"), None),
        P(None, "head"),
        P("head", None),
        P(None, "head"),
        P("head"),
        P("head", None),
        P(),
        P(),
        P(),
        P(),
        P(),
        P(),
    )
    return jax.shard_map(
        make(mesh), mesh=mesh, in_specs=in_specs, out_specs=out_specs, check_vma=False
    )
```

time: 235 us -> 141 us (0.60)
  matrix products: 44.8 us -> 0 us
  Pallas kernels: 0 us -> 38.6 us
  local copies, waits for them, and re-layouts: 39 us -> 7.66 us
  other arithmetic: 29.9 us -> 0 us
  starting transfers between devices: 57.3 us -> 38.7 us
  waiting for transfers between devices: 61.4 us -> 54.2 us
    dot_general x17 -> x0, matrix products: 41.4 us -> none  [the longest x1 4.4 us: shards(): jnp.einsum('nd,fd->nf', out_rows, down_use, preferred_element_type=F32)]
    pallas_call x0 -> x51, Pallas kernels: none -> 38.6 us  [call(): pl.pallas_call(ordered, out_shape=[jax.ShapeDtypeStruct(*out[:2]) for out...]
    ppermute x52 -> x41, starting transfers between devices: 57.3 us -> 38.7 us  [swap(): return lax.ppermute(value, AXES, [(i, i ^ bit) for i in range(total)])]
    concatenate x7 -> x0, other arithmetic: 11.1 us -> none  [gather(): slots = jnp.concatenate([slots, self.swap(slots, bit)], 0)]
    another operation x10 -> x0, local copies, waits for them, and re-layouts: 7.98 us -> none  [the longest x4 3.37 us: shards(): split = lambda g: jnp.stack(jnp.split(g, nslots, axis=1))]
    ppermute x52 -> x41, waiting for transfers between devices: 61.4 us -> 54.2 us  [swap(): return lax.ppermute(value, AXES, [(i, i ^ bit) for i in range(total)])]
    unnamed x146 -> x36, local copies, waits for them, and re-layouts: 13.2 us -> 7.05 us
    add x26 -> x0, other arithmetic: 5.73 us -> none  [the longest x9 3.51 us: scatter(): slots = slots[:half] + got.astype(F32)]
  transfers between devices with their start and end apart: 52 -> 41, of which waited for: 21 -> 16; matrix products, arithmetic and copies ran while one was open for 23% -> 0% of each run, Pallas kernels for 0% -> 26%
where the time goes in v2:
time: 141 us; the launch traced here: 140 us
  waiting for transfers between devices  54.2 us (38%)
  starting transfers between devices  38.7 us (27%)
  Pallas kernels  38.6 us (27%)
  local copies, waits for them, and re-layouts  7.66 us (5%)
    ppermute x41, waiting for transfers between devices, swap(): return lax.ppermute(value, AXES, [(i, i ^ bit) for i in range(total)])  54.2 us
    ppermute x41, starting transfers between devices, swap(): return lax.ppermute(value, AXES, [(i, i ^ bit) for i in range(total)])  38.7 us
    pallas_call x51, Pallas kernels, call(): pl.pallas_call(ordered, out_shape=[jax.ShapeDtypeStruct(*out[:2]) for out...  38.6 us
    unnamed x36, local copies, waits for them, and re-layouts  7.05 us
  transfers between devices with their start and end apart: 41, of which 16 were waited for; matrix products, arithmetic and copies ran while one was open for 0% of the time, Pallas kernels for 26%

profile of v2, /device:TPU:0, one launch (start us, length us, event | category | flops | bytes accessed | tf_op | source)
XLA Modules:
  0.0 140.3 jit_solution(2406831567875184777)
XLA Ops:
  1.2 2.6 %collective-permute-start = (bf16[512,384]{1,0:T(8,128)(2,1)}, bf16[512,384]{1,0:T(8,128)(2,1)S(1)}, u32[]{:S(2)}, u32[]{:S(2)}) collective-permute-start(bf16[512,384]{1,0:T(8,128)(2,1)} %refs_4_.10), channel_id=1, source_target_pairs={{0,2},{1,3},{2,0},{3,1},{4,6},{5,7},{6,4},{7,5},{8,10},{9,11},{10,... | collective-permute-start | bytes 1179656 | tf_op jit(solution)/shard_map/ppermute | solution.py:393
  4.4 0.9 copy-done.7
  7.1 1.2 copy-done
  8.3 1.2 copy-done.2
  11.0 3.8 %attend.3 = (bf16[512,384]{1,0:T(8,128)(2,1)S(1)}, bf16[512,384]{1,0:T(8,128)(2,1)S(1)}, f32[8,128,128]{2,1,0:T(8,128)S(1)}, f32[8,128,128]{2,1,0:T(8,128)S(1)},...) custom-call(bf16[512,512]{1,0:T(8,128)(2,1)S(1)} %get-tuple-element.166.refs_0_, ...), custom_call_target="tpu_custom_call" | custom-call | tf_op jit(solution)/shard_map/attend/pallas_call | solution.py:48
  15.4 1.8 %collective-permute-start.4 = (bf16[144,512]{1,0:T(8,128)(2,1)S(1)}, bf16[144,512]{1,0:T(8,128)(2,1)S(1)}, u32[]{:S(2)}, u32[]{:S(2)}) collective-permute-start(bf16[144,512]{1,0:T(8,128)(2,1)S(1)} %get-tuple-element.170.refs_2_.refs_4_), channel_id=1, source_target_pairs={{0,2},{1,3},{2,0},{3,1},{4,6},{5,7},{6,4},{7,5},{8,10},{9,11},{10,... | collective-permute-start | bytes 442376 | tf_op jit(solution)/shard_map/ppermute | solution.py:393
  17.2 2.3 %attend.4 = (bf16[512,384]{1,0:T(8,128)(2,1)S(1)}, f32[8,128,128]{2,1,0:T(8,128)S(1)}, bf16[512,128]{1,0:T(8,128)(2,1)S(1)}, f32[8,128]{1,0:T(8,128)S(1)}) custom-call(bf16[512,512]{1,0:T(8,128)(2,1)S(1)} %get-tuple-element.166.refs_0_, bf16[512,384]{1,0:T(8,128)(2,1)S(1)} %collective-permute-done.refs_0_.refs_1_.refs_6_, s32[1]{0:T(128)} %bitcast.3.refs_3_.refs_2_, ...), custom_call_target="tpu_custom_call" | custom-call | tf_op jit(solution)/shard_map/attend/pallas_call | solution.py:48
  19.5 8.6 %collective-permute-done.4.refs_0_.refs_2_.refs_3_.refs_4_ = bf16[144,512]{1,0:T(8,128)(2,1)S(1)} collective-permute-done((bf16[144,512]{1,0:T(8,128)(2,1)S(1)}, bf16[144,512]{1,0:T(8,128)(2,1)S(1)}, u32[]{:S(2)}, u32[]{:S(2)}) %collective-permute-start.4) | collective-permute-done | bytes 147488 | tf_op jit(solution)/shard_map/ppermute | solution.py:393
  28.2 2.3 %attend.5 = (bf16[512,384]{1,0:T(8,128)(2,1)S(1)}, f32[8,128,128]{2,1,0:T(8,128)S(1)}, bf16[512,128]{1,0:T(8,128)(2,1)S(1)}, f32[8,128]{1,0:T(8,128)S(1)}) custom-call(bf16[512,512]{1,0:T(8,128)(2,1)S(1)} %get-tuple-element.166.refs_0_, bf16[512,384]{1,0:T(8,128)(2,1)S(1)} %collective-permute-done.3.refs_1_.refs_7_, s32[1]{0:T(128)} %bitcast.3.refs_3_.refs_2_, ...), custom_call_target="tpu_custom_call" | custom-call | tf_op jit(solution)/shard_map/attend/pallas_call | solution.py:48
  32.2 2.1 %hidden.3 = (bf16[512,512]{1,0:T(8,128)(2,1)S(1)}, bf16[512,512]{1,0:T(8,128)(2,1)S(1)}, f32[512,512]{1,0:T(8,128)S(1)}, f32[512,512]{1,0:T(8,128)S(1)}, f32[512...) custom-call(bf16[512,512]{1,0:T(8,128)(2,1)S(1)} %get-tuple-element.182.refs_0_, ...), custom_call_target="tpu_custom_call" | custom-call | tf_op jit(solution)/shard_map/hidden/pallas_call | solution.py:48
  34.9 1.8 %hidden_back.3 = (f32[512,512]{1,0:T(8,128)S(1)}, bf16[512,512]{1,0:T(8,128)(2,1)S(1)}, f32[1,512]{1,0:T(1,128)S(1)}, f32[1,512]{1,0:T(1,128)S(1)}, f32[512,512]{1,0:T(8,128)S(1)}, /*index=5*/f32[8,128]{1,0:T(8,128)S(1)}) custom-call(bf16[512,512]{1,0:T(8,128)(2,1)S(1)} %get-tuple-element.187.refs_0_, bf16[512,512]{1,0:T(8,128)(2,1)S(1)} %get-tuple-element.188.refs_1_, ...), custom_call_target="tpu_custom_call" | custom-call | tf_op jit(solution)/shard_map/hidden_back/pallas_call | solution.py:48
  37.4 1.8 %collective-permute-start.11 = (bf16[512,512]{1,0:T(8,128)(2,1)S(1)}, bf16[512,512]{1,0:T(8,128)(2,1)S(1)}, u32[]{:S(2)}, u32[]{:S(2)}) collective-permute-start(bf16[512,512]{1,0:T(8,128)(2,1)S(1)} %copy-done.5), channel_id=1, source_target_pairs={{0,2},{1,3},{2,0},{3,1},{4,6},{5,7},{6,4},{7,5},{8,10},{9,11},{10,... | collective-permute-start | bytes 1572872 | tf_op jit(solution)/shard_map/ppermute | solution.py:393
  39.2 1.2 hidden.4
  40.5 1.3 hidden.5
  42.0 9.3 %collective-permute-done.11.refs_0_.refs_3_.refs_6_ = bf16[512,512]{1,0:T(8,128)(2,1)S(1)} collective-permute-done((bf16[512,512]{1,0:T(8,128)(2,1)S(1)}, bf16[512,512]{1,0:T(8,128)(2,1)S(1)}, u32[]{:S(2)}, u32[]{:S(2)}) %collective-permute-start.11) | collective-permute-done | bytes 524320 | tf_op jit(solution)/shard_map/ppermute | solution.py:393
  51.5 1.0 hidden_back.4
  53.4 1.0 hidden_back.5
  54.6 1.8 %collective-permute-start.15 = (bf16[512,512]{1,0:T(8,128)(2,1)S(1)}, bf16[512,512]{1,0:T(8,128)(2,1)S(1)}, u32[]{:S(2)}, u32[]{:S(2)}) collective-permute-start(bf16[512,512]{1,0:T(8,128)(2,1)S(1)} %get-tuple-element.214), channel_id=1, source_target_pairs={{0,2},{1,3},{2,0},{3,1},{4,6},{5,7},{6,4},{7,5},{8,10},{9,11},{10,... | collective-permute-start | bytes 1572872 | tf_op jit(solution)/shard_map/ppermute | solution.py:393
  56.4 1.1 middle.1
  57.6 3.8 %attend_back.2 = (bf16[512,384]{1,0:T(8,128)(2,1)S(1)}, bf16[512,384]{1,0:T(8,128)(2,1)S(1)}, bf16[512,512]{1,0:T(8,128)(2,1)S(1)}, f32[512,512]{1,0:T(8,128)S(1)}, f32[8,128]{1,0:T(8,128)S(1)}) custom-call(bf16[512,512]{1,0:T(8,128)(2,1)S(1)} %get-tuple-element.220.refs_0_, bf16[512,512]{1,0:T(8,128)(2,1)S(1)} %get-tuple-element.221.refs_1_, ...), custom_call_target="tpu_custom_call" | custom-call | tf_op jit(solution)/shard_map/attend_back/pallas_call | solution.py:48
  62.2 7.1 %collective-permute-done.15.refs_1_ = bf16[512,512]{1,0:T(8,128)(2,1)S(1)} collective-permute-done((bf16[512,512]{1,0:T(8,128)(2,1)S(1)}, bf16[512,512]{1,0:T(8,128)(2,1)S(1)}, u32[]{:S(2)}, u32[]{:S(2)}) %collective-permute-start.15) | collective-permute-done | bytes 524320 | tf_op jit(solution)/shard_map/ppermute | solution.py:393
  69.4 3.8 %attend_back.3 = (bf16[512,384]{1,0:T(8,128)(2,1)S(1)}, bf16[512,384]{1,0:T(8,128)(2,1)S(1)}, bf16[512,512]{1,0:T(8,128)(2,1)S(1)}, f32[512,512]{1,0:T(8,128)S(1)}, f32[8,128]{1,0:T(8,128)S(1)}) custom-call(bf16[512,512]{1,0:T(8,128)(2,1)S(1)} %get-tuple-element.220.refs_0_, bf16[512,512]{1,0:T(8,128)(2,1)S(1)} %get-tuple-element.221.refs_1_, ...), custom_call_target="tpu_custom_call" | custom-call | tf_op jit(solution)/shard_map/attend_back/pallas_call | solution.py:48
  73.5 1.8 %collective-permute-start.21 = (bf16[512,512]{1,0:T(8,128)(2,1)S(1)}, bf16[512,512]{1,0:T(8,128)(2,1)S(1)}, u32[]{:S(2)}, u32[]{:S(2)}) collective-permute-start(bf16[512,512]{1,0:T(8,128)(2,1)S(1)} %get-tuple-element.264), channel_id=1, source_target_pairs={{0,2},{1,3},{2,0},{3,1},{4,6},{5,7},{6,4},{7,5},{8,10},{9,11},{10,... | collective-permute-start | bytes 1572872 | tf_op jit(solution)/shard_map/ppermute | solution.py:393
  75.3 1.5 %collective-permute-start.17 = (bf16[256,512]{1,0:T(8,128)(2,1)S(1)}, bf16[256,512]{1,0:T(8,128)(2,1)S(1)}, u32[]{:S(2)}, u32[]{:S(2)}) collective-permute-start(bf16[256,512]{1,0:T(8,128)(2,1)S(1)} %get-tuple-element.233), channel_id=1, source_target_pairs={{0,4},{1,5},{2,6},{3,7},{4,0},{5,1},{6,2},{7,3},{8,12},{9,13},{10,... | collective-permute-start | bytes 786440 | tf_op jit(solution)/shard_map/ppermute | solution.py:393
  76.7 3.4 %input.1 = (f32[512,512]{1,0:T(8,128)}, f32[8,512]{1,0:T(8,128)S(1)}, f32[8,128]{1,0:T(8,128)S(1)}) custom-call(bf16[512,384]{1,0:T(8,128)(2,1)S(1)} %get-tuple-element.242.refs_0_, bf16[512,384]{1,0:T(8,128)(2,1)S(1)} %get-tuple-element.243.refs_1_, bf16[512,384]{1,0:T(8,128)(2,1)S(1)} %get-tuple-element.244.refs_2_, ...), custom_call_target="tpu_custom_call" | custom-call | tf_op jit(solution)/shard_map/input/pallas_call | solution.py:48
  80.7 1.8 %collective-permute-start.23 = (bf16[256,512]{1,0:T(8,128)(2,1)S(1)}, bf16[256,512]{1,0:T(8,128)(2,1)S(1)}, u32[]{:S(2)}, u32[]{:S(2)}) collective-permute-start(bf16[256,512]{1,0:T(8,128)(2,1)S(1)} %get-tuple-element.268), channel_id=1, source_target_pairs={{0,4},{1,5},{2,6},{3,7},{4,0},{5,1},{6,2},{7,3},{8,12},{9,13},{10,... | collective-permute-start | bytes 786440 | tf_op jit(solution)/shard_map/ppermute | solution.py:393
  82.5 1.9 %collective-permute-done.17.refs_1_ = bf16[256,512]{1,0:T(8,128)(2,1)S(1)} collective-permute-done((bf16[256,512]{1,0:T(8,128)(2,1)S(1)}, bf16[256,512]{1,0:T(8,128)(2,1)S(1)}, u32[]{:S(2)}, u32[]{:S(2)}) %collective-permute-start.17) | collective-permute-done | bytes 262176 | tf_op jit(solution)/shard_map/ppermute | solution.py:393
  84.5 1.6 %collective-permute-start.22 = (bf16[128,512]{1,0:T(8,128)(2,1)S(1)}, bf16[128,512]{1,0:T(8,128)(2,1)S(1)}, u32[]{:S(2)}, u32[]{:S(2)}) collective-permute-start(bf16[128,512]{1,0:T(8,128)(2,1)S(1)} %get-tuple-element.266), channel_id=1, source_target_pairs={{0,8},{1,9},{2,10},{3,11},{4,12},{5,13},{6,14},{7,15},{8,0},{9,1},... | collective-permute-start | bytes 393224 | tf_op jit(solution)/shard_map/ppermute | solution.py:393
  86.8 2.5 %output.1 = (f32[512,512]{1,0:T(8,128)}, f32[8,128]{1,0:T(8,128)S(1)}) custom-call(bf16[512,512]{1,0:T(8,128)(2,1)S(1)} %get-tuple-element.185.refs_0_, bf16[512,512]{1,0:T(8,128)(2,1)S(1)} %get-tuple-element.186.refs_1_, bf16[512,512]{1,0:T(8,128)(2,1)S(1)} %get-tuple-element.194.refs_2_, bf16[512,512]{1,0:T(8,128)(2,1)S(1)} %get-tuple-element.200.refs_3_, ...), custom_call_target="tpu_custom_call" | custom-call | tf_op jit(solution)/shard_map/output/pallas_call | solution.py:48
  89.5 1.7 %collective-permute-done.21.refs_2_ = bf16[512,512]{1,0:T(8,128)(2,1)S(1)} collective-permute-done((bf16[512,512]{1,0:T(8,128)(2,1)S(1)}, bf16[512,512]{1,0:T(8,128)(2,1)S(1)}, u32[]{:S(2)}, u32[]{:S(2)}) %collective-permute-start.21) | collective-permute-done | bytes 524320 | tf_op jit(solution)/shard_map/ppermute | solution.py:393
  91.4 1.8 %collective-permute-start.25 = (bf16[256,512]{1,0:T(8,128)(2,1)S(1)}, bf16[256,512]{1,0:T(8,128)(2,1)S(1)}, u32[]{:S(2)}, u32[]{:S(2)}) collective-permute-start(bf16[256,512]{1,0:T(8,128)(2,1)S(1)} %get-tuple-element.275), channel_id=1, source_target_pairs={{0,4},{1,5},{2,6},{3,7},{4,0},{5,1},{6,2},{7,3},{8,12},{9,13},{10,... | collective-permute-start | bytes 786440 | tf_op jit(solution)/shard_map/ppermute | solution.py:393
  93.2 1.6 %collective-permute-start.27 = (bf16[128,512]{1,0:T(8,128)(2,1)S(1)}, bf16[128,512]{1,0:T(8,128)(2,1)S(1)}, u32[]{:S(2)}, u32[]{:S(2)}) collective-permute-start(bf16[128,512]{1,0:T(8,128)(2,1)S(1)} %get-tuple-element.279), channel_id=1, source_target_pairs={{0,8},{1,9},{2,10},{3,11},{4,12},{5,13},{6,14},{7,15},{8,0},{9,1},... | collective-permute-start | bytes 393224 | tf_op jit(solution)/shard_map/ppermute | solution.py:393
  94.8 1.5 %collective-permute-start.28 = (f32[16,512]{1,0:T(8,128)S(1)}, f32[16,512]{1,0:T(8,128)S(1)}, u32[]{:S(2)}, u32[]{:S(2)}) collective-permute-start(f32[16,512]{1,0:T(8,128)S(1)} %get-tuple-element.280.refs_0_), channel_id=1, source_target_pairs={{0,2},{1,3},{2,0},{3,1},{4,6},{5,7},{6,4},{7,5},{8,10},{9,11},{10,... | collective-permute-start | bytes 98312 | tf_op jit(solution)/shard_map/ppermute | solution.py:393
  96.3 2.6 %collective-permute-start.26 = (bf16[128,512]{1,0:T(8,128)(2,1)S(1)}, bf16[128,512]{1,0:T(8,128)(2,1)S(1)}, u32[]{:S(2)}, u32[]{:S(2)}) collective-permute-start(bf16[128,512]{1,0:T(8,128)(2,1)S(1)} %get-tuple-element.277), channel_id=1, source_target_pairs={{0,16},{1,17},{2,18},{3,19},{4,20},{5,21},{6,22},{7,23},{8,24},{9,... | collective-permute-start | bytes 393224 | tf_op jit(solution)/shard_map/ppermute | solution.py:393
  98.9 3.0 %collective-permute-start.31 = (bf16[128,512]{1,0:T(8,128)(2,1)S(1)}, bf16[128,512]{1,0:T(8,128)(2,1)S(1)}, u32[]{:S(2)}, u32[]{:S(2)}) collective-permute-start(bf16[128,512]{1,0:T(8,128)(2,1)S(1)} %get-tuple-element.289), channel_id=1, source_target_pairs={{0,16},{1,17},{2,18},{3,19},{4,20},{5,21},{6,22},{7,23},{8,24},{9,... | collective-permute-start | bytes 393224 | tf_op jit(solution)/shard_map/ppermute | solution.py:393
  102.6 5.4 %collective-permute-done.26.refs_1_ = bf16[128,512]{1,0:T(8,128)(2,1)S(1)} collective-permute-done((bf16[128,512]{1,0:T(8,128)(2,1)S(1)}, bf16[128,512]{1,0:T(8,128)(2,1)S(1)}, u32[]{:S(2)}, u32[]{:S(2)}) %collective-permute-start.26) | collective-permute-done | bytes 131104 | tf_op jit(solution)/shard_map/ppermute | solution.py:393
  108.1 2.1 %collective-permute-start.29 = (bf16[128,512]{1,0:T(8,128)(2,1)S(1)}, bf16[128,512]{1,0:T(8,128)(2,1)S(1)}, u32[]{:S(2)}, u32[]{:S(2)}) collective-permute-start(bf16[128,512]{1,0:T(8,128)(2,1)S(1)} %get-tuple-element.286), channel_id=1, source_target_pairs={{0,8},{1,9},{2,10},{3,11},{4,12},{5,13},{6,14},{7,15},{8,0},{9,1},... | collective-permute-start | bytes 393224 | tf_op jit(solution)/shard_map/ppermute | solution.py:393
  110.4 2.0 %collective-permute-start.35 = (f32[16,512]{1,0:T(8,128)S(1)}, f32[16,512]{1,0:T(8,128)S(1)}, u32[]{:S(2)}, u32[]{:S(2)}) collective-permute-start(f32[16,512]{1,0:T(8,128)S(1)} %get-tuple-element.298.refs_0_), channel_id=1, source_target_pairs={{0,8},{1,9},{2,10},{3,11},{4,12},{5,13},{6,14},{7,15},{8,0},{9,1},... | collective-permute-start | bytes 98312 | tf_op jit(solution)/shard_map/ppermute | solution.py:393
  112.3 2.1 %collective-permute-done.30.refs_1_ = bf16[128,512]{1,0:T(8,128)(2,1)S(1)} collective-permute-done((bf16[128,512]{1,0:T(8,128)(2,1)S(1)}, bf16[128,512]{1,0:T(8,128)(2,1)S(1)}, u32[]{:S(2)}, u32[]{:S(2)}) %collective-permute-start.30) | collective-permute-done | bytes 131104 | tf_op jit(solution)/shard_map/ppermute | solution.py:393
  115.2 1.9 %collective-permute-done.29.refs_1_ = bf16[128,512]{1,0:T(8,128)(2,1)S(1)} collective-permute-done((bf16[128,512]{1,0:T(8,128)(2,1)S(1)}, bf16[128,512]{1,0:T(8,128)(2,1)S(1)}, u32[]{:S(2)}, u32[]{:S(2)}) %collective-permute-start.29) | collective-permute-done | bytes 131104 | tf_op jit(solution)/shard_map/ppermute | solution.py:393
  117.9 2.4 %collective-permute-done.35.refs_1_ = f32[16,512]{1,0:T(8,128)S(1)} collective-permute-done((f32[16,512]{1,0:T(8,128)S(1)}, f32[16,512]{1,0:T(8,128)S(1)}, u32[]{:S(2)}, u32[]{:S(2)}) %collective-permute-start.35) | collective-permute-done | bytes 32800 | tf_op jit(solution)/shard_map/ppermute | solution.py:393
  120.9 4.1 %collective-permute-done.33.refs_1_ = bf16[128,512]{1,0:T(8,128)(2,1)S(1)} collective-permute-done((bf16[128,512]{1,0:T(8,128)(2,1)S(1)}, bf16[128,512]{1,0:T(8,128)(2,1)S(1)}, u32[]{:S(2)}, u32[]{:S(2)}) %collective-permute-start.33) | collective-permute-done | bytes 131104 | tf_op jit(solution)/shard_map/ppermute | solution.py:393
  125.1 2.0 %collective-permute-start.39 = (f32[16,512]{1,0:T(8,128)S(1)}, f32[16,512]{1,0:T(8,128)S(1)}, u32[]{:S(2)}, u32[]{:S(2)}) collective-permute-start(f32[16,512]{1,0:T(8,128)S(1)} %get-tuple-element.305.refs_0_), channel_id=1, source_target_pairs={{0,16},{1,17},{2,18},{3,19},{4,20},{5,21},{6,22},{7,23},{8,24},{9,... | collective-permute-start | bytes 98312 | tf_op jit(solution)/shard_map/ppermute | solution.py:393
  127.1 3.0 %collective-permute-done.39.refs_1_ = f32[16,512]{1,0:T(8,128)S(1)} collective-permute-done((f32[16,512]{1,0:T(8,128)S(1)}, f32[16,512]{1,0:T(8,128)S(1)}, u32[]{:S(2)}, u32[]{:S(2)}) %collective-permute-start.39) | collective-permute-done | bytes 32800 | tf_op jit(solution)/shard_map/ppermute | solution.py:393
  130.1 1.4 finish.3
  131.5 1.1 finish.4
  133.9 5.2 %collective-permute-done.40.refs_1_ = bf16[256,512]{1,0:T(8,128)(2,1)S(1)} collective-permute-done((bf16[256,512]{1,0:T(8,128)(2,1)S(1)}, bf16[256,512]{1,0:T(8,128)(2,1)S(1)}, u32[]{:S(2)}, u32[]{:S(2)}) %collective-permute-start.40) | collective-permute-done | bytes 262176 | tf_op jit(solution)/shard_map/ppermute | solution.py:393
  139.1 1.2 finish.5
  (124 shorter events, 16.8 us)
Async XLA Ops:
  0.6 5.5 %collective-permute-start.1 = (bf16[512,384]{1,0:T(8,128)(2,1)}, bf16[512,384]{1,0:T(8,128)(2,1)S(1)}, u32[]{:S(2)}, u32[]{:S(2)}) collective-permute-start(bf16[512,384]{1,0:T(8,128)(2,1)} %refs_4_.10), channel_id=1, source_target_pairs={{0,1},{1,0},{2,3},{3,2},{4,5},{5,4},{6,7},{7,6},{8,9},{9,8},{10,11... | collective-permute-start | bytes 1179656 | tf_op jit(solution)/shard_map/ppermute | solution.py:393
  1.2 14.1 %collective-permute-start = (bf16[512,384]{1,0:T(8,128)(2,1)}, bf16[512,384]{1,0:T(8,128)(2,1)S(1)}, u32[]{:S(2)}, u32[]{:S(2)}) collective-permute-start(bf16[512,384]{1,0:T(8,128)(2,1)} %refs_4_.10), channel_id=1, source_target_pairs={{0,2},{1,3},{2,0},{3,1},{4,6},{5,7},{6,4},{7,5},{8,10},{9,11},{10,... | collective-permute-start | bytes 1179656 | tf_op jit(solution)/shard_map/ppermute | solution.py:393
  5.4 9.4 %collective-permute-start.2 = (bf16[144,512]{1,0:T(8,128)(2,1)S(1)}, bf16[144,512]{1,0:T(8,128)(2,1)S(1)}, u32[]{:S(2)}, u32[]{:S(2)}) collective-permute-start(bf16[144,512]{1,0:T(8,128)(2,1)S(1)} %get-tuple-element.170.refs_2_.refs_4_), channel_id=1, source_target_pairs={{0,1},{1,0},{2,3},{3,2},{4,5},{5,4},{6,7},{7,6},{8,9},{9,8},{10,11... | collective-permute-start | bytes 442376 | tf_op jit(solution)/shard_map/ppermute | solution.py:393
  5.6 26.4 %collective-permute-start.6 = (bf16[512,512]{1,0:T(8,128)(2,1)}, bf16[512,512]{1,0:T(8,128)(2,1)S(1)}, u32[]{:S(2)}, u32[]{:S(2)}) collective-permute-start(bf16[512,512]{1,0:T(8,128)(2,1)} %refs_2_.3), channel_id=1, source_target_pairs={{0,1},{1,0},{2,3},{3,2},{4,5},{5,4},{6,7},{7,6},{8,9},{9,8},{10,11... | collective-permute-start | bytes 1572872 | tf_op jit(solution)/shard_map/ppermute | solution.py:393
  5.9 29.0 %collective-permute-start.8 = (bf16[512,512]{1,0:T(8,128)(2,1)}, bf16[512,512]{1,0:T(8,128)(2,1)S(1)}, u32[]{:S(2)}, u32[]{:S(2)}) collective-permute-start(bf16[512,512]{1,0:T(8,128)(2,1)} %refs_4_.11), channel_id=1, source_target_pairs={{0,1},{1,0},{2,3},{3,2},{4,5},{5,4},{6,7},{7,6},{8,9},{9,8},{10,11... | collective-permute-start | bytes 1572872 | tf_op jit(solution)/shard_map/ppermute | solution.py:393
  6.1 30.7 %collective-permute-start.7 = (bf16[512,512]{1,0:T(8,128)(2,1)}, bf16[512,512]{1,0:T(8,128)(2,1)S(1)}, u32[]{:S(2)}, u32[]{:S(2)}) collective-permute-start(bf16[512,512]{1,0:T(8,128)(2,1)} %refs_2_.3), channel_id=1, source_target_pairs={{0,2},{1,3},{2,0},{3,1},{4,6},{5,7},{6,4},{7,5},{8,10},{9,11},{10,... | collective-permute-start | bytes 1572872 | tf_op jit(solution)/shard_map/ppermute | solution.py:393
  7.1 1.2 copy-start
  8.3 1.2 copy-start.2
  15.3 15.2 %copy-start.1 = (f32[512,512]{1,0:T(8,128)S(1)}, f32[512,512]{1,0:T(8,128)}, u32[]{:S(2)}) copy-start(f32[512,512]{1,0:T(8,128)} %refs_8_.1) | copy-start | bytes 3145732
  15.3 12.9 %collective-permute-start.3 = (bf16[512,384]{1,0:T(8,128)(2,1)S(1)}, bf16[512,384]{1,0:T(8,128)(2,1)S(1)}, u32[]{:S(2)}, u32[]{:S(2)}) collective-permute-start(bf16[512,384]{1,0:T(8,128)(2,1)S(1)} %get-tuple-element.175), channel_id=1, source_target_pairs={{0,1},{1,0},{2,3},{3,2},{4,5},{5,4},{6,7},{7,6},{8,9},{9,8},{10,11... | collective-permute-start | bytes 1179656 | tf_op jit(solution)/shard_map/ppermute | solution.py:393
  15.4 12.6 %collective-permute-start.4 = (bf16[144,512]{1,0:T(8,128)(2,1)S(1)}, bf16[144,512]{1,0:T(8,128)(2,1)S(1)}, u32[]{:S(2)}, u32[]{:S(2)}) collective-permute-start(bf16[144,512]{1,0:T(8,128)(2,1)S(1)} %get-tuple-element.170.refs_2_.refs_4_), channel_id=1, source_target_pairs={{0,2},{1,3},{2,0},{3,1},{4,6},{5,7},{6,4},{7,5},{8,10},{9,11},{10,... | collective-permute-start | bytes 442376 | tf_op jit(solution)/shard_map/ppermute | solution.py:393
  28.1 2.4 %collective-permute-start.5 = (bf16[144,512]{1,0:T(8,128)(2,1)S(1)}, bf16[144,512]{1,0:T(8,128)(2,1)S(1)}, u32[]{:S(2)}, u32[]{:S(2)}) collective-permute-start(bf16[144,512]{1,0:T(8,128)(2,1)S(1)} %get-tuple-element.179), channel_id=1, source_target_pairs={{0,1},{1,0},{2,3},{3,2},{4,5},{5,4},{6,7},{7,6},{8,9},{9,8},{10,11... | collective-permute-start | bytes 442376 | tf_op jit(solution)/shard_map/ppermute | solution.py:393
  28.2 2.4 %copy-start.14 = (f32[512]{0:T(512)S(1)}, f32[512]{0:T(512)}, u32[]{:S(2)}) copy-start(f32[512]{0:T(512)} %param.28) | copy-start | bytes 6148
  31.2 1.0 copy-start.4
  32.2 2.7 %copy-start.5 = (bf16[512,512]{1,0:T(8,128)(2,1)S(1)}, bf16[512,512]{1,0:T(8,128)(2,1)}, u32[]{:S(2)}) copy-start(bf16[512,512]{1,0:T(8,128)(2,1)} %refs_4_.11) | copy-start | bytes 1572868
  34.4 6.0 %collective-permute-start.10 = (bf16[512,512]{1,0:T(8,128)(2,1)S(1)}, bf16[512,512]{1,0:T(8,128)(2,1)S(1)}, u32[]{:S(2)}, u32[]{:S(2)}) collective-permute-start(bf16[512,512]{1,0:T(8,128)(2,1)S(1)} %get-tuple-element.197), channel_id=1, source_target_pairs={{0,1},{1,0},{2,3},{3,2},{4,5},{5,4},{6,7},{7,6},{8,9},{9,8},{10,11... | collective-permute-start | bytes 1572872 | tf_op jit(solution)/shard_map/ppermute | solution.py:393
  36.8 3.6 %collective-permute-start.9 = (bf16[512,512]{1,0:T(8,128)(2,1)S(1)}, bf16[512,512]{1,0:T(8,128)(2,1)S(1)}, u32[]{:S(2)}, u32[]{:S(2)}) collective-permute-start(bf16[512,512]{1,0:T(8,128)(2,1)S(1)} %get-tuple-element.195), channel_id=1, source_target_pairs={{0,1},{1,0},{2,3},{3,2},{4,5},{5,4},{6,7},{7,6},{8,9},{9,8},{10,11... | collective-permute-start | bytes 1572872 | tf_op jit(solution)/shard_map/ppermute | solution.py:393
  36.9 5.0 %collective-permute-start.12 = (bf16[512,512]{1,0:T(8,128)(2,1)S(1)}, bf16[512,512]{1,0:T(8,128)(2,1)S(1)}, u32[]{:S(2)}, u32[]{:S(2)}) collective-permute-start(bf16[512,512]{1,0:T(8,128)(2,1)S(1)} %get-tuple-element.202), channel_id=1, source_target_pairs={{0,1},{1,0},{2,3},{3,2},{4,5},{5,4},{6,7},{7,6},{8,9},{9,8},{10,11... | collective-permute-start | bytes 1572872 | tf_op jit(solution)/shard_map/ppermute | solution.py:393
  37.4 13.9 %collective-permute-start.11 = (bf16[512,512]{1,0:T(8,128)(2,1)S(1)}, bf16[512,512]{1,0:T(8,128)(2,1)S(1)}, u32[]{:S(2)}, u32[]{:S(2)}) collective-permute-start(bf16[512,512]{1,0:T(8,128)(2,1)S(1)} %copy-done.5), channel_id=1, source_target_pairs={{0,2},{1,3},{2,0},{3,1},{4,6},{5,7},{6,4},{7,5},{8,10},{9,11},{10,... | collective-permute-start | bytes 1572872 | tf_op jit(solution)/shard_map/ppermute | solution.py:393
  41.8 10.7 %collective-permute-start.14 = (bf16[512,512]{1,0:T(8,128)(2,1)S(1)}, bf16[512,512]{1,0:T(8,128)(2,1)S(1)}, u32[]{:S(2)}, u32[]{:S(2)}) collective-permute-start(bf16[512,512]{1,0:T(8,128)(2,1)S(1)} %get-tuple-element.209), channel_id=1, source_target_pairs={{0,1},{1,0},{2,3},{3,2},{4,5},{5,4},{6,7},{7,6},{8,9},{9,8},{10,11... | collective-permute-start | bytes 1572872 | tf_op jit(solution)/shard_map/ppermute | solution.py:393
  51.4 2.0 %collective-permute-start.13 = (bf16[512,512]{1,0:T(8,128)(2,1)S(1)}, bf16[512,512]{1,0:T(8,128)(2,1)S(1)}, u32[]{:S(2)}, u32[]{:S(2)}) collective-permute-start(bf16[512,512]{1,0:T(8,128)(2,1)S(1)} %get-tuple-element.205), channel_id=1, source_target_pairs={{0,1},{1,0},{2,3},{3,2},{4,5},{5,4},{6,7},{7,6},{8,9},{9,8},{10,11... | collective-permute-start | bytes 1572872 | tf_op jit(solution)/shard_map/ppermute | solution.py:393
  53.4 3.0 %copy-start.3 = (f32[512,512]{1,0:T(8,128)S(1)}, f32[512,512]{1,0:T(8,128)}, u32[]{:S(2)}) copy-start(f32[512,512]{1,0:T(8,128)} %refs_11_.1) | copy-start | bytes 3145732
  54.4 3.1 %collective-permute-start.16 = (bf16[512,512]{1,0:T(8,128)(2,1)S(1)}, bf16[512,512]{1,0:T(8,128)(2,1)S(1)}, u32[]{:S(2)}, u32[]{:S(2)}) collective-permute-start(bf16[512,512]{1,0:T(8,128)(2,1)S(1)} %get-tuple-element.228), channel_id=1, source_target_pairs={{0,1},{1,0},{2,3},{3,2},{4,5},{5,4},{6,7},{7,6},{8,9},{9,8},{10,11... | collective-permute-start | bytes 1572872 | tf_op jit(solution)/shard_map/ppermute | solution.py:393
  54.6 14.8 %collective-permute-start.15 = (bf16[512,512]{1,0:T(8,128)(2,1)S(1)}, bf16[512,512]{1,0:T(8,128)(2,1)S(1)}, u32[]{:S(2)}, u32[]{:S(2)}) collective-permute-start(bf16[512,512]{1,0:T(8,128)(2,1)S(1)} %get-tuple-element.214), channel_id=1, source_target_pairs={{0,2},{1,3},{2,0},{3,1},{4,6},{5,7},{6,4},{7,5},{8,10},{9,11},{10,... | collective-permute-start | bytes 1572872 | tf_op jit(solution)/shard_map/ppermute | solution.py:393
  61.4 12.0 %collective-permute-start.19 = (bf16[512,512]{1,0:T(8,128)(2,1)S(1)}, bf16[512,512]{1,0:T(8,128)(2,1)S(1)}, u32[]{:S(2)}, u32[]{:S(2)}) collective-permute-start(bf16[512,512]{1,0:T(8,128)(2,1)S(1)} %get-tuple-element.247), channel_id=1, source_target_pairs={{0,1},{1,0},{2,3},{3,2},{4,5},{5,4},{6,7},{7,6},{8,9},{9,8},{10,11... | collective-permute-start | bytes 1572872 | tf_op jit(solution)/shard_map/ppermute | solution.py:393
  61.5 19.1 %collective-permute-start.18 = (bf16[512,512]{1,0:T(8,128)(2,1)S(1)}, bf16[512,512]{1,0:T(8,128)(2,1)S(1)}, u32[]{:S(2)}, u32[]{:S(2)}) collective-permute-start(bf16[512,512]{1,0:T(8,128)(2,1)S(1)} %get-tuple-element.235), channel_id=1, source_target_pairs={{0,2},{1,3},{2,0},{3,1},{4,6},{5,7},{6,4},{7,5},{8,10},{9,11},{10,... | collective-permute-start | bytes 1572872 | tf_op jit(solution)/shard_map/ppermute | solution.py:393
  73.2 16.3 %collective-permute-start.20 = (bf16[512,512]{1,0:T(8,128)(2,1)S(1)}, bf16[512,512]{1,0:T(8,128)(2,1)S(1)}, u32[]{:S(2)}, u32[]{:S(2)}) collective-permute-start(bf16[512,512]{1,0:T(8,128)(2,1)S(1)} %get-tuple-element.262), channel_id=1, source_target_pairs={{0,1},{1,0},{2,3},{3,2},{4,5},{5,4},{6,7},{7,6},{8,9},{9,8},{10,11... | collective-permute-start | bytes 1572872 | tf_op jit(solution)/shard_map/ppermute | solution.py:393
  73.5 17.8 %collective-permute-start.21 = (bf16[512,512]{1,0:T(8,128)(2,1)S(1)}, bf16[512,512]{1,0:T(8,128)(2,1)S(1)}, u32[]{:S(2)}, u32[]{:S(2)}) collective-permute-start(bf16[512,512]{1,0:T(8,128)(2,1)S(1)} %get-tuple-element.264), channel_id=1, source_target_pairs={{0,2},{1,3},{2,0},{3,1},{4,6},{5,7},{6,4},{7,5},{8,10},{9,11},{10,... | collective-permute-start | bytes 1572872 | tf_op jit(solution)/shard_map/ppermute | solution.py:393
  75.3 9.1 %collective-permute-start.17 = (bf16[256,512]{1,0:T(8,128)(2,1)S(1)}, bf16[256,512]{1,0:T(8,128)(2,1)S(1)}, u32[]{:S(2)}, u32[]{:S(2)}) collective-permute-start(bf16[256,512]{1,0:T(8,128)(2,1)S(1)} %get-tuple-element.233), channel_id=1, source_target_pairs={{0,4},{1,5},{2,6},{3,7},{4,0},{5,1},{6,2},{7,3},{8,12},{9,13},{10,... | collective-permute-start | bytes 786440 | tf_op jit(solution)/shard_map/ppermute | solution.py:393
  80.7 8.6 %collective-permute-start.23 = (bf16[256,512]{1,0:T(8,128)(2,1)S(1)}, bf16[256,512]{1,0:T(8,128)(2,1)S(1)}, u32[]{:S(2)}, u32[]{:S(2)}) collective-permute-start(bf16[256,512]{1,0:T(8,128)(2,1)S(1)} %get-tuple-element.268), channel_id=1, source_target_pairs={{0,4},{1,5},{2,6},{3,7},{4,0},{5,1},{6,2},{7,3},{8,12},{9,13},{10,... | collective-permute-start | bytes 786440 | tf_op jit(solution)/shard_map/ppermute | solution.py:393
  84.5 5.0 %collective-permute-start.22 = (bf16[128,512]{1,0:T(8,128)(2,1)S(1)}, bf16[128,512]{1,0:T(8,128)(2,1)S(1)}, u32[]{:S(2)}, u32[]{:S(2)}) collective-permute-start(bf16[128,512]{1,0:T(8,128)(2,1)S(1)} %get-tuple-element.266), channel_id=1, source_target_pairs={{0,8},{1,9},{2,10},{3,11},{4,12},{5,13},{6,14},{7,15},{8,0},{9,1},... | collective-permute-start | bytes 393224 | tf_op jit(solution)/shard_map/ppermute | solution.py:393
  86.1 3.1 %collective-permute-start.24 = (f32[16,512]{1,0:T(8,128)S(1)}, f32[16,512]{1,0:T(8,128)S(1)}, u32[]{:S(2)}, u32[]{:S(2)}) collective-permute-start(f32[16,512]{1,0:T(8,128)S(1)} %get-tuple-element.269.refs_0_), channel_id=1, source_target_pairs={{0,1},{1,0},{2,3},{3,2},{4,5},{5,4},{6,7},{7,6},{8,9},{9,8},{10,11... | collective-permute-start | bytes 98312 | tf_op jit(solution)/shard_map/ppermute | solution.py:393
  91.4 16.6 %collective-permute-start.25 = (bf16[256,512]{1,0:T(8,128)(2,1)S(1)}, bf16[256,512]{1,0:T(8,128)(2,1)S(1)}, u32[]{:S(2)}, u32[]{:S(2)}) collective-permute-start(bf16[256,512]{1,0:T(8,128)(2,1)S(1)} %get-tuple-element.275), channel_id=1, source_target_pairs={{0,4},{1,5},{2,6},{3,7},{4,0},{5,1},{6,2},{7,3},{8,12},{9,13},{10,... | collective-permute-start | bytes 786440 | tf_op jit(solution)/shard_map/ppermute | solution.py:393
  93.2 5.7 %collective-permute-start.27 = (bf16[128,512]{1,0:T(8,128)(2,1)S(1)}, bf16[128,512]{1,0:T(8,128)(2,1)S(1)}, u32[]{:S(2)}, u32[]{:S(2)}) collective-permute-start(bf16[128,512]{1,0:T(8,128)(2,1)S(1)} %get-tuple-element.279), channel_id=1, source_target_pairs={{0,8},{1,9},{2,10},{3,11},{4,12},{5,13},{6,14},{7,15},{8,0},{9,1},... | collective-permute-start | bytes 393224 | tf_op jit(solution)/shard_map/ppermute | solution.py:393
  94.8 4.1 %collective-permute-start.28 = (f32[16,512]{1,0:T(8,128)S(1)}, f32[16,512]{1,0:T(8,128)S(1)}, u32[]{:S(2)}, u32[]{:S(2)}) collective-permute-start(f32[16,512]{1,0:T(8,128)S(1)} %get-tuple-element.280.refs_0_), channel_id=1, source_target_pairs={{0,2},{1,3},{2,0},{3,1},{4,6},{5,7},{6,4},{7,5},{8,10},{9,11},{10,... | collective-permute-start | bytes 98312 | tf_op jit(solution)/shard_map/ppermute | solution.py:393
  96.3 11.6 %collective-permute-start.26 = (bf16[128,512]{1,0:T(8,128)(2,1)S(1)}, bf16[128,512]{1,0:T(8,128)(2,1)S(1)}, u32[]{:S(2)}, u32[]{:S(2)}) collective-permute-start(bf16[128,512]{1,0:T(8,128)(2,1)S(1)} %get-tuple-element.277), channel_id=1, source_target_pairs={{0,16},{1,17},{2,18},{3,19},{4,20},{5,21},{6,22},{7,23},{8,24},{9,... | collective-permute-start | bytes 393224 | tf_op jit(solution)/shard_map/ppermute | solution.py:393
  98.9 11.3 %collective-permute-start.31 = (bf16[128,512]{1,0:T(8,128)(2,1)S(1)}, bf16[128,512]{1,0:T(8,128)(2,1)S(1)}, u32[]{:S(2)}, u32[]{:S(2)}) collective-permute-start(bf16[128,512]{1,0:T(8,128)(2,1)S(1)} %get-tuple-element.289), channel_id=1, source_target_pairs={{0,16},{1,17},{2,18},{3,19},{4,20},{5,21},{6,22},{7,23},{8,24},{9,... | collective-permute-start | bytes 393224 | tf_op jit(solution)/shard_map/ppermute | solution.py:393
  102.0 8.2 %collective-permute-start.32 = (f32[16,512]{1,0:T(8,128)S(1)}, f32[16,512]{1,0:T(8,128)S(1)}, u32[]{:S(2)}, u32[]{:S(2)}) collective-permute-start(f32[16,512]{1,0:T(8,128)S(1)} %get-tuple-element.290.refs_0_), channel_id=1, source_target_pairs={{0,4},{1,5},{2,6},{3,7},{4,0},{5,1},{6,2},{7,3},{8,12},{9,13},{10,... | collective-permute-start | bytes 98312 | tf_op jit(solution)/shard_map/ppermute | solution.py:393
  108.0 6.5 %collective-permute-start.30 = (bf16[128,512]{1,0:T(8,128)(2,1)S(1)}, bf16[128,512]{1,0:T(8,128)(2,1)S(1)}, u32[]{:S(2)}, u32[]{:S(2)}) collective-permute-start(bf16[128,512]{1,0:T(8,128)(2,1)S(1)} %get-tuple-element.287.refs_0_), channel_id=1, source_target_pairs={{0,8},{1,9},{2,10},{3,11},{4,12},{5,13},{6,14},{7,15},{8,0},{9,1},... | collective-permute-start | bytes 393224 | tf_op jit(solution)/shard_map/ppermute | solution.py:393
  108.1 9.0 %collective-permute-start.29 = (bf16[128,512]{1,0:T(8,128)(2,1)S(1)}, bf16[128,512]{1,0:T(8,128)(2,1)S(1)}, u32[]{:S(2)}, u32[]{:S(2)}) collective-permute-start(bf16[128,512]{1,0:T(8,128)(2,1)S(1)} %get-tuple-element.286), channel_id=1, source_target_pairs={{0,8},{1,9},{2,10},{3,11},{4,12},{5,13},{6,14},{7,15},{8,0},{9,1},... | collective-permute-start | bytes 393224 | tf_op jit(solution)/shard_map/ppermute | solution.py:393
  110.3 10.0 %collective-permute-start.34 = (bf16[128,512]{1,0:T(8,128)(2,1)S(1)}, bf16[128,512]{1,0:T(8,128)(2,1)S(1)}, u32[]{:S(2)}, u32[]{:S(2)}) collective-permute-start(bf16[128,512]{1,0:T(8,128)(2,1)S(1)} %get-tuple-element.297.refs_0_), channel_id=1, source_target_pairs={{0,8},{1,9},{2,10},{3,11},{4,12},{5,13},{6,14},{7,15},{8,0},{9,1},... | collective-permute-start | bytes 393224 | tf_op jit(solution)/shard_map/ppermute | solution.py:393
  110.4 9.9 %collective-permute-start.35 = (f32[16,512]{1,0:T(8,128)S(1)}, f32[16,512]{1,0:T(8,128)S(1)}, u32[]{:S(2)}, u32[]{:S(2)}) collective-permute-start(f32[16,512]{1,0:T(8,128)S(1)} %get-tuple-element.298.refs_0_), channel_id=1, source_target_pairs={{0,8},{1,9},{2,10},{3,11},{4,12},{5,13},{6,14},{7,15},{8,0},{9,1},... | collective-permute-start | bytes 98312 | tf_op jit(solution)/shard_map/ppermute | solution.py:393
  114.5 15.6 %collective-permute-start.38 = (bf16[256,512]{1,0:T(8,128)(2,1)S(1)}, bf16[256,512]{1,0:T(8,128)(2,1)S(1)}, u32[]{:S(2)}, u32[]{:S(2)}) collective-permute-start(bf16[256,512]{1,0:T(8,128)(2,1)S(1)} %get-tuple-element.304.refs_0_), channel_id=1, source_target_pairs={{0,4},{1,5},{2,6},{3,7},{4,0},{5,1},{6,2},{7,3},{8,12},{9,13},{10,... | collective-permute-start | bytes 786440 | tf_op jit(solution)/shard_map/ppermute | solution.py:393
  117.1 7.9 %collective-permute-start.33 = (bf16[128,512]{1,0:T(8,128)(2,1)S(1)}, bf16[128,512]{1,0:T(8,128)(2,1)S(1)}, u32[]{:S(2)}, u32[]{:S(2)}) collective-permute-start(bf16[128,512]{1,0:T(8,128)(2,1)S(1)} %get-tuple-element.296), channel_id=1, source_target_pairs={{0,16},{1,17},{2,18},{3,19},{4,20},{5,21},{6,22},{7,23},{8,24},{9,... | collective-permute-start | bytes 393224 | tf_op jit(solution)/shard_map/ppermute | solution.py:393
  120.3 11.2 %collective-permute-start.37 = (bf16[256,512]{1,0:T(8,128)(2,1)S(1)}, bf16[256,512]{1,0:T(8,128)(2,1)S(1)}, u32[]{:S(2)}, u32[]{:S(2)}) collective-permute-start(bf16[256,512]{1,0:T(8,128)(2,1)S(1)} %get-tuple-element.303.refs_0_), channel_id=1, source_target_pairs={{0,4},{1,5},{2,6},{3,7},{4,0},{5,1},{6,2},{7,3},{8,12},{9,13},{10,... | collective-permute-start | bytes 786440 | tf_op jit(solution)/shard_map/ppermute | solution.py:393
  125.0 7.6 %collective-permute-start.36 = (bf16[128,512]{1,0:T(8,128)(2,1)S(1)}, bf16[128,512]{1,0:T(8,128)(2,1)S(1)}, u32[]{:S(2)}, u32[]{:S(2)}) collective-permute-start(bf16[128,512]{1,0:T(8,128)(2,1)S(1)} %get-tuple-element.302.refs_0_), channel_id=1, source_target_pairs={{0,8},{1,9},{2,10},{3,11},{4,12},{5,13},{6,14},{7,15},{8,0},{9,1},... | collective-permute-start | bytes 393224 | tf_op jit(solution)/shard_map/ppermute | solution.py:393
  125.1 5.0 %collective-permute-start.39 = (f32[16,512]{1,0:T(8,128)S(1)}, f32[16,512]{1,0:T(8,128)S(1)}, u32[]{:S(2)}, u32[]{:S(2)}) collective-permute-start(f32[16,512]{1,0:T(8,128)S(1)} %get-tuple-element.305.refs_0_), channel_id=1, source_target_pairs={{0,16},{1,17},{2,18},{3,19},{4,20},{5,21},{6,22},{7,23},{8,24},{9,... | collective-permute-start | bytes 98312 | tf_op jit(solution)/shard_map/ppermute | solution.py:393
  132.7 6.4 %collective-permute-start.40 = (bf16[256,512]{1,0:T(8,128)(2,1)S(1)}, bf16[256,512]{1,0:T(8,128)(2,1)S(1)}, u32[]{:S(2)}, u32[]{:S(2)}) collective-permute-start(bf16[256,512]{1,0:T(8,128)(2,1)S(1)} %get-tuple-element.310.refs_0_), channel_id=1, source_target_pairs={{0,4},{1,5},{2,6},{3,7},{4,0},{5,1},{6,2},{7,3},{8,12},{9,13},{10,... | collective-permute-start | bytes 786440 | tf_op jit(solution)/shard_map/ppermute | solution.py:393
  (11 other events, 8.1 us)

commit v3 on v2

v3 whole, which is shorter than its diff:
```python
import functools
import types

import jax
import jax.numpy as jnp
from jax import lax
from jax.experimental import pallas as pl
from jax.experimental.pallas import tpu as pltpu
from jax.sharding import PartitionSpec as P

HEAD_DIM = 64
SEQ = 128
EPSILON = 1e-05
NEG_FILL = -1e30
BF = jnp.bfloat16
F32 = jnp.float32
AXES = ("dp", "head")
CHUNK = 128
VMEM_LIMIT = 8 * 2**20


def nn(a, b):
    return lax.dot_general(a, b, (((1,), (0,)), ((), ())), preferred_element_type=F32)


def nt(a, b):
    return lax.dot_general(a, b, (((1,), (1,)), ((), ())), preferred_element_type=F32)


def tn(a, b):
    return lax.dot_general(a, b, (((0,), (0,)), ((), ())), preferred_element_type=F32)


class Kernels:
    def __init__(self):
        self.token = jnp.zeros((8, 128), F32)

    def call(self, body, outs, *args, scalars=0, scratch=(), also=(), name=None):
        vmem = pl.BlockSpec(memory_space=pltpu.VMEM)
        smem = pl.BlockSpec(memory_space=pltpu.SMEM)
        plain, count = len(args) - scalars, len(args)

        mine = count + len(also)
        last = mine + 1 + len(outs)

        def ordered(*refs):
            refs[last][...] = refs[mine][...]
            body(*refs[:count], *refs[mine + 1 : last], *refs[last + 1 :])

        got = pl.pallas_call(
            ordered,
            out_shape=[jax.ShapeDtypeStruct(*out[:2]) for out in outs]
            + [jax.ShapeDtypeStruct((8, 128), F32)],
            in_specs=[vmem] * plain + [smem] * scalars + [vmem] * (len(also) + 1),
            out_specs=[vmem] * (len(outs) + 1),
            compiler_params=pltpu.CompilerParams(vmem_limit_bytes=VMEM_LIMIT),
            scratch_shapes=[pltpu.VMEM(*s) for s in scratch],
            cost_estimate=pl.CostEstimate(flops=0, bytes_accessed=0, transcendentals=0),
            name=name,
        )(*args, *also, self.token)
        self.token = got[-1]
        return got[:-1]

    def wait(self, *arrays):
        self.call(touch_kernel, [], *arrays, name="touch")


def centred(rows):
    centre = rows - jnp.mean(rows, axis=-1, keepdims=True)
    spread = jnp.mean(centre * centre, axis=-1, keepdims=True)
    rstd = lax.rsqrt(spread + EPSILON)
    return centre * rstd, rstd


def norm_back(grad, rows, gain):
    xhat, rstd = centred(rows)
    q = grad * gain
    inner = jnp.mean(q * xhat, axis=-1, keepdims=True)
    row = rstd * (q - jnp.mean(q, axis=-1, keepdims=True) - xhat * inner)
    return row, jnp.sum(grad * xhat, axis=0, keepdims=True), jnp.sum(grad, axis=0, keepdims=True)


def prep_kernel(res, gain, shift, first, first_t):
    for r in range(0, res.shape[0], CHUNK):
        xhat, _ = centred(res[r : r + CHUNK, :])
        low = (xhat * gain[...] + shift[...]).astype(BF)
        first[r : r + CHUNK, :] = low
        first_t[:, r : r + CHUNK] = low.T


def out_kernel(cot, out_low, out_t):
    for r in range(0, cot.shape[0], CHUNK):
        low = cot[r : r + CHUNK, :].astype(BF)
        out_low[r : r + CHUNK, :] = low
        out_t[:, r : r + CHUNK] = low.T


def lanes_low(shape):
    return lax.broadcasted_iota(jnp.int32, shape, 1) < HEAD_DIM


def half_turn(block):
    return jnp.concatenate([block[:, HEAD_DIM:], block[:, :HEAD_DIM]], 1)


def mask_of(start, count, length):
    m = lax.broadcasted_iota(jnp.int32, (SEQ, SEQ), 0)
    n = lax.broadcasted_iota(jnp.int32, (SEQ, SEQ), 1)
    group_m = jnp.maximum((m * 43) >> 8, start)
    group_n = jnp.maximum((n * 43) >> 8, start)
    seen = (m < length) & ((group_m <= group_n) | (m < count))
    return jnp.where(seen, 0.0, NEG_FILL)


def blocks_of(triple, s):
    at = slice(s * SEQ, (s + 1) * SEQ)
    b0, b1, b2 = (triple[at, c * 128 : (c + 1) * 128] for c in range(3))
    low, zero = lanes_low(b0.shape), jnp.zeros(b0.shape, BF)
    keys = jnp.concatenate([jnp.where(low, zero, b0), jnp.where(low, b2, zero)], 0)
    values = jnp.concatenate([jnp.where(low, b1, zero), jnp.where(low, zero, b2)], 0)
    queries = half_turn(jnp.where(low, b0, b1)) * jnp.asarray(HEAD_DIM**-0.5, BF)
    return keys, values, queries


def attend(first, weight, triple, probs, mixed, scalars, seqs):
    triple[...] = nn(first[...], weight[...]).astype(BF)
    base, starts, counts, lengths = scalars
    parts = [blocks_of(triple, s) for s in range(seqs)]
    for s, (keys, _, queries) in enumerate(parts):
        probs[s] = nt(keys, queries)
    for s in range(seqs):
        bias = mask_of(*(ref[base + s] for ref in (starts, counts, lengths)))
        for h in range(2):
            at = slice(h * SEQ, (h + 1) * SEQ)
            score = probs[s, at, :] + bias
            weights = jnp.exp(score - jnp.max(score, axis=0, keepdims=True))
            probs[s, at, :] = weights * (1.0 / jnp.sum(weights, axis=0, keepdims=True))
    for s, (_, values, _) in enumerate(parts):
        mixed[s * SEQ : (s + 1) * SEQ, :] = tn(probs[s].astype(BF), values).astype(BF)


def attend_back(middle_low, proj, triple, probs, seqs, gtl, grad_mixed, grad_probs):
    grad_mixed[...] = nn(middle_low[...], proj[: middle_low.shape[1], :]).astype(BF)
    parts = [blocks_of(triple, s) for s in range(seqs)]
    spots = [slice(s * SEQ, (s + 1) * SEQ) for s in range(seqs)]
    for s, (_, values, _) in enumerate(parts):
        grad_probs[s] = nt(values, grad_mixed[spots[s], :])
    lows = []
    for s in range(seqs):
        scores = []
        for h in range(2):
            at = slice(h * SEQ, (h + 1) * SEQ)
            prob, grad = probs[s, at, :], grad_probs[s, at, :]
            inner = jnp.sum(grad * prob, axis=0, keepdims=True)
            scores.append((prob * (grad - inner)).astype(BF))
        lows.append(jnp.concatenate(scores, 0))
    low = lanes_low((SEQ, 2 * HEAD_DIM))
    for s, (keys, _, queries) in enumerate(parts):
        grad_queries = half_turn(tn(lows[s], keys) * HEAD_DIM**-0.5)
        grad_keys = nn(lows[s], queries)
        grad_values = nn(probs[s].astype(BF), grad_mixed[spots[s], :])
        gtl[spots[s], 0:128] = jnp.where(low, grad_queries, grad_keys[:SEQ]).astype(BF)
        gtl[spots[s], 128:256] = jnp.where(low, grad_values[:SEQ], grad_queries).astype(BF)
        gtl[spots[s], 256:384] = jnp.where(low, grad_keys[SEQ:], grad_values[SEQ:]).astype(BF)


def gelu_parts(x):
    c0, c1 = 0.7978845608028654, 0.044715
    square = x * x
    t = jnp.tanh(x * (c0 + (c0 * c1) * square))
    h = 0.5 * (1.0 + t)
    slope = h + (0.5 * x) * (1.0 - t * t) * (c0 + (3.0 * c0 * c1) * square)
    return x * h, slope


def pack_kernel(proj, bias, place, base, out, *more):
    deep, span = proj.shape[1], out.shape[1]
    out[:deep, :] = proj[...].T
    rows = bias.shape[1] // span
    out[deep:, :] = jnp.concatenate(
        [bias[:, k * span : (k + 1) * span] for k in range(rows)]
        + [jnp.zeros((16 - rows, span), out.dtype)],
        0,
    )


def bundle_kernel(proj, bias, down, place, base, out, bundle):
    pack_kernel(proj, bias, place, base, out)
    deep, span = out.shape
    bundle[:deep, :] = out[...]
    half, per = down.shape[0] // 2, down.shape[1] // span
    rows = down[pl.ds(pl.multiple_of((place[0] % 2) * half, half), half), :]
    for k in range(per):
        bundle[deep + k * half : deep + (k + 1) * half, :] = rows[:, k * span : (k + 1) * span]


def unbundle_kernel(bundle, out, rows):
    deep, span = out.shape
    out[...] = bundle[:deep, :]
    half = rows.shape[0]
    for k in range(rows.shape[1] // span):
        rows[:, k * span : (k + 1) * span] = bundle[deep + k * half : deep + (k + 1) * half, :]


def pair_kernel(*refs):
    out, col = refs[-1], 0
    for part in refs[:-1]:
        out[:, col : col + part.shape[1]] = part[...]
        col += part.shape[1]


def touch_kernel(*refs):
    pass


def relay_kernel(value, out):
    out[...] = value[...]


def attend_kernel(units, seqs, *refs):
    refs = list(refs)
    take = lambda n: [refs.pop(0) for _ in range(n)]
    (first,) = take(1)
    weights = take(units)
    scalars = take(4)
    scalars = [scalars[0][0]] + scalars[1:]
    triples, probs, mixeds = take(units), take(units), take(units)
    for u in range(units):
        attend(first, weights[u], triples[u], probs[u], mixeds[u], scalars, seqs)


def project_kernel(units, *refs):
    mixeds, projs, acc = refs[:units], refs[units : 2 * units], refs[2 * units]
    acc[...] = sum(
        nt(mixeds[u][...], projs[u][: acc.shape[1], :]) for u in range(units)
    )


def second_kernel(units, *refs):
    refs = list(refs)
    take = lambda n: [refs.pop(0) for _ in range(n)]
    mixeds, projs = take(units), take(units)
    acc, residual, bias, gain, shift, middle, second, second_t = refs
    for r in range(0, acc.shape[0], CHUNK):
        at = slice(r, r + CHUNK)
        out = acc[at, :] + sum(
            nt(mixeds[u][at, :], projs[u][: acc.shape[1], :]) for u in range(units)
        )
        out = residual[at, :] + out + bias[...]
        middle[at, :] = out
        xhat, _ = centred(out)
        low = (xhat * gain[...] + shift[...]).astype(BF)
        second[at, :] = low
        second_t[:, at] = low.T


def hidden_kernel(slots, *refs):
    refs = list(refs)
    take = lambda n: [refs.pop(0) for _ in range(n)]
    second, out_t = take(2)
    ups, biases = take(slots), take(slots)
    acts, slopes, grads = take(slots), take(slots), take(slots)
    for j in range(slots):
        span, deep = biases[j].shape[1], second.shape[1]
        bias = jnp.concatenate(
            [biases[j][deep + k : deep + k + 1, :] for k in range(ups[j].shape[1] // span)], 1
        ).astype(F32)
        for r in range(0, second.shape[0], 2 * CHUNK):
            at = slice(r, r + 2 * CHUNK)
            act, slope = gelu_parts(nn(second[at, :], ups[j][...]) + bias)
            acts[j][at, :] = act.astype(BF)
            slopes[j][at, :] = slope
        grads[j][...] = nn(out_t[...], acts[j][...]).astype(grads[j].dtype)


def hidden_back_kernel(pieces, first_call, *refs):
    refs, slots = list(refs), len(pieces)
    take = lambda n: [refs.pop(0) for _ in range(n)]
    out_low, second_t = take(2)
    ups, downs, slopes = take(slots), take(slots), take(slots)
    acc_in = None if first_call else take(1)[0]
    grads, biases = [take(n) for n in pieces], take(slots)
    (acc,) = take(1)
    pre = take(slots)
    for j in range(slots):
        total = 0.0
        for r in range(0, out_low.shape[0], 2 * CHUNK):
            at = slice(r, r + 2 * CHUNK)
            low = (nt(out_low[at, :], downs[j][...]) * slopes[j][at, :]).astype(BF)
            pre[j][at, :] = low
            total = total + jnp.sum(low.astype(F32), axis=0, keepdims=True)
        biases[j][...] = total
        grad, first = nn(second_t[...], pre[j][...]), 0
        for out in grads[j]:
            out[...] = grad[first : first + out.shape[0], :].astype(out.dtype)
            first += out.shape[0]
    for r in range(0, out_low.shape[0], 2 * CHUNK):
        at = slice(r, r + 2 * CHUNK)
        out = sum(nt(pre[j][at, :], ups[j][...]) for j in range(slots))
        acc[at, :] = out if first_call else acc_in[at, :] + out


def middle_kernel(grad_second, middle, gain, cot, grad_middle, middle_low, middle_t, sums):
    totals = [0.0, 0.0, 0.0]
    for r in range(0, cot.shape[0], CHUNK):
        at = slice(r, r + CHUNK)
        row, dgain, dshift = norm_back(grad_second[at, :], middle[at, :], gain[...])
        grad = cot[at, :] + row
        grad_middle[at, :] = grad
        low = grad.astype(BF)
        middle_low[at, :] = low
        middle_t[:, at] = low.T
        parts = (jnp.sum(grad, axis=0, keepdims=True), dgain, dshift)
        totals = [t + p for t, p in zip(totals, parts)]
    for i, t in enumerate(totals):
        sums[i : i + 1, :] = t


def attend_back_kernel(units, group, pieces, seqs, *refs):
    refs = list(refs)
    take = lambda n: [refs.pop(0) for _ in range(n)]
    middle_low, middle_t, first_t = take(3)
    projs, triples, probs, mixeds = take(units), take(units), take(units), take(units)
    gtls, grads = take(units), [take(n) for n in pieces]
    grad_mixed, grad_probs = take(units), take(units)
    span, small = 6 * HEAD_DIM // group, 2 * HEAD_DIM // group
    for u in range(units):
        attend_back(
            middle_low,
            projs[u],
            triples[u],
            probs[u],
            seqs,
            gtls[u],
            grad_mixed[u],
            grad_probs[u],
        )
        grad = nn(first_t[...], gtls[u][...])
        proj_grad = nn(middle_t[...], mixeds[u][...])
        for k in range(group):
            first = 0
            for out in grads[u * group + k]:
                at = slice(first, first + out.shape[0])
                first += out.shape[0]
                out[:, :span] = grad[at, k * span : (k + 1) * span].astype(out.dtype)
                out[:, span:] = proj_grad[at, k * small : (k + 1) * small].astype(out.dtype)


def input_kernel(units, *refs):
    refs = list(refs)
    take = lambda n: [refs.pop(0) for _ in range(n)]
    gtls, weights = take(units), take(units)
    residual, gain, grad_middle, cot = take(4)
    grad_input, sums = take(2)
    totals = [0.0, 0.0, 0.0]
    for r in range(0, cot.shape[0], CHUNK):
        at = slice(r, r + CHUNK)
        grad = sum(nt(gtls[u][at, :], weights[u][...]) for u in range(units))
        row, dgain, dshift = norm_back(grad, residual[at, :], gain[...])
        grad_input[at, :] = grad_middle[at, :] + row
        parts = (jnp.sum(cot[at, :], axis=0, keepdims=True), dgain, dshift)
        totals = [t + p for t, p in zip(totals, parts)]
    for i, t in enumerate(totals):
        sums[i : i + 1, :] = t


def output_kernel(slots, *refs):
    acts, downs = refs[:slots], refs[slots : 2 * slots]
    middle, bias, out = refs[2 * slots :]
    for r in range(0, middle.shape[0], 2 * CHUNK):
        at = slice(r, r + 2 * CHUNK)
        total = sum(nn(acts[j][at, :], downs[j][...]) for j in range(slots))
        out[at, :] = middle[at, :] + total + bias[...]


def total(terms):
    out = terms[0]
    for term in terms[1:]:
        out = out + term
    return out


def read(refs, spots, at):
    terms = []
    for where, first in spots:
        if len(where) > 1:
            terms.append(jnp.concatenate([refs[i][...] for i in where], 0).astype(F32))
        else:
            terms.append(refs[where[0]][pl.ds(first + at[0], at[1]), :].astype(F32))
    return total(terms)


def rider_rows(rider, cols):
    return 2 * rider[0] * -(-(rider[1] // 128) // max(1, cols // 128))


def pack_rider(rider, out, first):
    per, deep = max(1, out.shape[1] // 128), 2 * rider.shape[0]
    high = rider.astype(BF)
    rest = (rider - high.astype(F32)).astype(BF)
    for j in range(rider.shape[1] // 128):
        at, row, col = slice(j * 128, (j + 1) * 128), first + deep * (j // per), 128 * (j % per)
        block = jnp.concatenate([high[:, at], rest[:, at]], 0)
        out[row : row + deep, col : col + 128] = block


def unpack_rider(value, first, shape):
    rows, per, parts = shape[0], max(1, value.shape[1] // 128), []
    for j in range(shape[1] // 128):
        row, col = first + 2 * rows * (j // per), 128 * (j % per)
        block = value[row : row + 2 * rows, col : col + 128].astype(F32)
        parts.append(block[:rows, :] + block[rows:, :])
    return jnp.concatenate(parts, 1)


def rider_total(refs, ride):
    kept, came, first = ride
    rider = refs[kept][...]
    for i in came:
        rider = rider + unpack_rider(refs[i], first, rider.shape)
    return rider


def send_kernel(spots, rows, *refs):
    count = 1 + max(i for spot in spots for where, _ in spot for i in where)
    outs = refs[count:]
    if len(outs) > 1:
        value = read(refs, spots[0], (0, rows)).astype(BF)
        for k, out in enumerate(outs):
            out[...] = value[k * out.shape[0] : (k + 1) * out.shape[0], :]
        return
    (out,) = outs
    used = len(spots) * rows
    for k, spot in enumerate(spots):
        out[k * rows : (k + 1) * rows, :] = read(refs, spot, (0, rows)).astype(out.dtype)
    if used < out.shape[0]:
        out[used:, :] = jnp.zeros((out.shape[0] - used, out.shape[1]), out.dtype)


def halve_kernel(spots, rows, bit, ride, *refs):
    refs = list(refs)
    if ride:
        rider_keep = refs.pop()
    send = refs.pop()
    stays = [refs.pop() for _ in spots][::-1]
    place = refs.pop()
    half = rows // 2
    mine = (place[0] // bit) % 2
    for k, spot in enumerate(spots):
        stays[k][...] = read(refs, spot, (pl.multiple_of(mine * half, half), half))
        leave = read(refs, spot, (pl.multiple_of((1 - mine) * half, half), half))
        send[k * half : (k + 1) * half, :] = leave.astype(BF)
    room = len(spots) * half
    if room < send.shape[0]:
        send[room:, :] = jnp.zeros((send.shape[0] - room, send.shape[1]), BF)
    if ride:
        rider = rider_total(refs, ride)
        rider_keep[...] = rider
        pack_rider(rider, send, len(spots) * half)


def whole_kernel(spots, rows, ride, *refs):
    refs = list(refs)
    if ride:
        rider_keep = refs.pop()
    send, keep = refs.pop(), refs.pop()
    value = read(refs, spots[0], (0, rows))
    keep[...] = value
    send[:rows, :] = value.astype(BF)
    send[rows:, :] = jnp.zeros((send.shape[0] - rows, send.shape[1]), BF)
    if ride:
        rider = rider_total(refs, ride)
        rider_keep[...] = rider
        pack_rider(rider, send, rows)


def settle_kernel(spots, rows, ride, *refs):
    refs = list(refs)
    if ride:
        rider_out = refs.pop()
    out = refs.pop()
    out[...] = read(refs, spots[0], (0, rows)).astype(out.dtype)
    if ride:
        rider_out[...] = rider_total(refs, ride)


def join_kernel(bit, own, other, place, out):
    half = own.shape[0]
    mine = (place[0] // bit) % 2
    out[pl.ds(pl.multiple_of(mine * half, half), half), :] = own[...].astype(out.dtype)
    out[pl.ds(pl.multiple_of((1 - mine) * half, half), half), :] = other[...].astype(out.dtype)


def finish_kernel(bit, blocks, turned, own, other, place, *refs):
    outs, low = refs[:-1], refs[-1]
    join_kernel(bit, own, other, place, low)
    rows, col = low.shape[0] // len(blocks), 0
    for out, turn in zip(outs, turned):
        span = out.shape[0] if turn else out.shape[1]
        for to, at in enumerate(blocks):
            part = low[at * rows : (at + 1) * rows, col : col + span]
            if turn:
                out[:, to * rows : (to + 1) * rows] = part.T
            else:
                out[to * rows : (to + 1) * rows, :] = part
        col += span


def vector_kernel(parts, *refs):
    out = refs[-1]
    out[...] = jnp.zeros_like(out)
    row = 0
    for ref, n in zip(refs, parts):
        out[row : row + n, : ref.shape[1]] = ref[:n, :]
        row += n


def vector_core_kernel(heads, fixed, mine, got, out):
    out[...] = jnp.zeros_like(out)
    out[:fixed, :] = mine[:fixed, :] + got[:fixed, :]
    for k in range(0, heads, 2):
        at, other, to = fixed + k, fixed + k + 1, fixed + k // 2
        out[to : to + 1, :] = mine[at : at + 1, :] + got[other : other + 1, :]


def vector_add_kernel(bit, fixed, mine, got, out):
    out[...] = mine[...] + got[...]
    for k in range(out.shape[0] - fixed):
        if k ^ bit < out.shape[0] - fixed:
            at, other = fixed + k, fixed + (k ^ bit)
            out[at : at + 1, :] = mine[at : at + 1, :] + got[other : other + 1, :]


def vector_last_kernel(bit, fixed, mine, got, *outs):
    for k in range(fixed + 1):
        other, span = (k if k < fixed else fixed + bit), outs[k].shape[1]
        outs[k][...] = mine[k : k + 1, :span] + got[other : other + 1, :span]


class Links:
    def __init__(self, mesh):
        self.dp, self.head = mesh.shape["dp"], mesh.shape["head"]

    def swap(self, value, bit):
        total = self.dp * self.head
        return lax.ppermute(value, AXES, [(i, i ^ bit) for i in range(total)])


class Chain:
    def __init__(self, links, kernels, place, room, tag):
        self.tag = tag
        self.room = room
        self.links, self.kernels, self.place = links, kernels, place
        self.slots, self.bit, self.halved = {}, 2, []
        self.rider, self.rider_came = None, []
        self.rider_first = 0

    def give(self, slot, *values):
        self.rows, self.cols = sum(v.shape[0] for v in values), values[0].shape[1]
        if slot % 2:
            got = [self.links.swap(v, 1) for v in values]
            self.slots.setdefault(slot - 1, []).insert(0, (got, 0))
        else:
            self.slots.setdefault(slot, []).insert(0, (list(values), 0))

    def give_later(self, slot, value):
        (value,) = self.kernels.call(relay_kernel, [(value.shape, BF)], value, name="relay")
        self.give(slot, value)

    def spots(self, sums):
        arrays, spots = [], []
        for terms in sums:
            spots.append([])
            for values, first in terms:
                where = []
                for value in values:
                    known = [i for i, a in enumerate(arrays) if a is value]
                    if not known:
                        arrays.append(value)
                        known = [len(arrays) - 1]
                    where.append(known[0])
                spots[-1].append((where, first))
        return arrays, spots

    def head(self, pieces=1, spare=False):
        leave = [k for k in self.slots if k & self.bit]
        arrays, spots = self.spots([self.slots[k] for k in leave])
        room = rider_rows(self.room, self.cols) if self.halved or spare else 0
        deep = len(leave) * self.rows + room
        sends = self.kernels.call(
            functools.partial(send_kernel, spots, self.rows),
            [((deep // pieces, self.cols), BF)] * pieces,
            *arrays,
            name="send_" + self.tag,
        )
        got = [self.links.swap(send, self.bit) for send in sends]
        for i, k in enumerate(leave):
            del self.slots[k]
            self.slots.setdefault(k ^ self.bit, []).append((got, i * self.rows))
        self.bit *= 2

    def fold(self, slot, count=2):
        arrays, spots = self.spots([self.slots[slot][:count]])
        (value,) = self.kernels.call(
            functools.partial(send_kernel, spots, self.rows),
            [((self.rows, self.cols), F32)],
            *arrays,
            name="fold_" + self.tag,
        )
        self.slots[slot][:count] = [([value], 0)]

    def ride(self, arrays):
        if self.rider is None:
            return None
        arrays.append(self.rider)
        came = [i for i, a in enumerate(arrays) if any(a is b for b in self.rider_came)]
        return len(arrays) - 1, came, self.rider_first

    def rode(self, kept, came, first):
        if self.rider is not None:
            self.rider, self.rider_came, self.rider_first = kept, came, first

    def halve(self, bit):
        keys = list(self.slots)
        arrays, spots = self.spots([self.slots[k] for k in keys])
        half = self.rows // 2
        ride = self.ride(arrays)
        rider = [(self.rider.shape, F32)] if ride else []
        more = rider_rows(self.room, self.cols) if self.halved or len(keys) == 1 else 0
        got = self.kernels.call(
            functools.partial(halve_kernel, spots, self.rows, bit, ride),
            [((half, self.cols), F32)] * len(keys)
            + [((len(keys) * half + more, self.cols), BF)]
            + rider,
            *arrays,
            self.place,
            scalars=1,
            name="halve_" + self.tag,
        )
        came = self.links.swap(got[len(keys)], bit * self.links.head)
        self.slots = {k: [([got[i]], 0), ([came], i * half)] for i, k in enumerate(keys)}
        self.rode(got[-1], [came], len(keys) * half)
        self.rows = half
        self.halved.append(bit)

    def whole(self, bit):
        arrays, spots = self.spots([self.slots[0]])
        ride = self.ride(arrays)
        rider = [(self.rider.shape, F32)] if ride else []
        more = rider_rows(self.room, self.cols)
        got = self.kernels.call(
            functools.partial(whole_kernel, spots, self.rows, ride),
            [((self.rows, self.cols), F32), ((self.rows + more, self.cols), BF)] + rider,
            *arrays,
            name="whole_" + self.tag,
        )
        came = self.links.swap(got[1], bit * self.links.head)
        self.slots = {0: [([got[0]], 0), ([came], 0)]}
        self.rode(got[-1], [came], self.rows)

    def settle(self, order):
        arrays, spots = self.spots([self.slots[0]])
        ride = self.ride(arrays)
        got = self.kernels.call(
            functools.partial(settle_kernel, spots, self.rows, ride),
            [((self.rows, self.cols), BF)] + ([(self.rider.shape, F32)] if ride else []),
            *arrays,
            name="settle_" + self.tag,
        )
        self.own, self.order, self.left = got[0], list(order), list(order)
        self.back()
        return got[-1]

    def back(self):
        self.last = self.left.pop(0)
        self.got = self.links.swap(self.own, self.last * self.links.head)

    def double(self):
        self.rows *= 2
        (self.own,) = self.kernels.call(
            functools.partial(join_kernel, self.last),
            [((self.rows, self.cols), BF)],
            self.own,
            self.got,
            self.place,
            scalars=1,
            name="join_" + self.tag,
        )
        self.back()

    def finish(self, outs, turned):
        blocks = []
        for to in range(2 ** len(self.order)):
            digits = {b: to >> (len(self.halved) - 1 - i) & 1 for i, b in enumerate(self.halved)}
            blocks.append(sum(digits[b] << i for i, b in enumerate(self.order)))
        if blocks == sorted(blocks):
            blocks = [0]
        return self.kernels.call(
            functools.partial(finish_kernel, self.last, blocks, turned),
            [(o, F32, True) for o in outs],
            self.own,
            self.got,
            self.place,
            scalars=1,
            scratch=[((2 * self.rows, self.cols), F32)],
            name="finish_" + self.tag,
        )


def make(mesh):
    links = Links(mesh)
    nslots = links.head
    bits = [2**k for k in range(links.dp.bit_length() - 1)]

    def shards(
        residual_in,
        cotangent,
        triple_weight,
        proj_weight,
        up_weight,
        up_bias,
        down_weight,
        proj_bias,
        down_bias,
        first_gain,
        first_shift,
        second_gain,
        second_shift,
        start_steps,
        cond_counts,
        valid_lengths,
    ):
        kernels = Kernels()
        call = kernels.call
        rows, width = residual_in.shape
        seqs = rows // SEQ
        hidden, proj_rows = up_weight.shape[1], proj_weight.shape[0]
        row = lambda v: v.reshape(1, -1)
        proj_bias, down_bias, first_gain, first_shift, second_gain, second_shift = map(
            row, (proj_bias, down_bias, first_gain, first_shift, second_gain, second_shift)
        )
        place = lax.axis_index("dp").astype(jnp.int32).reshape(1)
        base = (lax.axis_index("head") * seqs).astype(jnp.int32).reshape(1)
        scalars = (base, start_steps, cond_counts, valid_lengths)
        group = 2 * HEAD_DIM // proj_rows
        units = nslots // group

        slots = {}

        def far(key, value):
            known = {0: value}
            bit = nslots // 2
            while bit > 1:
                known.update({k | bit: links.swap(v, bit) for k, v in list(known.items())})
                bit //= 2
            slots[key] = known

        def near(key):
            slots[key][1] = links.swap(slots[key][0], 1)

        def relay(key, k):
            value = slots[key][k]
            (value,) = call(relay_kernel, [(value.shape, BF)], value, name="relay")
            slots[key][k + 1] = links.swap(value, 1)

        far("t", triple_weight)
        near("t")
        far("u", up_weight)
        near("u")
        slots["d"] = {0: down_weight, 1: links.swap(down_weight, 1)}
        shared = nslots == 4 and len(bits) > 1
        pack_shape = (width + 16, proj_rows)
        half = (down_weight.shape[0] // 2, width)
        evens, odds = range(2, nslots, 2), range(3, nslots, 2)
        early = list(range(max(1, 2 // group)))
        late = [u for u in range(units) if u not in early]
        triple_w, proj_w, triples, probs, mixeds = {}, {}, {}, {}, {}
        acts, slopes, biases, down_grads, up_grads = {}, {}, {}, {}, {}
        gtls, triple_grads = {}, {}
        room = (8 * -(-(6 + nslots // 2) // 8), width)
        down_sum, up_sum, triple_sum = (Chain(links, kernels, place, room, t) for t in "dut")
        middle_bits, there = bits[1:-1], bits[:-1]
        s = types.SimpleNamespace()
        thirds = [width // 48 * 16 + 16] * 2
        thirds = thirds + [width - sum(thirds)]

        def kind(k):
            return BF if k % 2 else F32

        def bundle():
            if shared:
                deep = pack_shape[0] + half[0] * width // proj_rows
                packed, sent = call(
                    bundle_kernel,
                    [(pack_shape, BF), ((deep, proj_rows), BF)],
                    proj_weight,
                    row(up_bias),
                    down_weight,
                    place,
                    base,
                    scalars=2,
                    name="bundle",
                )
                s.bundle = links.swap(sent, 2)
                slots["p"] = {0: packed, 1: links.swap(packed, 1)}
                return
            (packed,) = call(
                pack_kernel,
                [(pack_shape, BF)],
                proj_weight,
                row(up_bias),
                place,
                base,
                scalars=2,
                name="pack",
            )
            far("p", packed)
            near("p")
            far("d", down_weight)
            near("d")

        def prep():
            s.first, s.first_t = call(
                prep_kernel,
                [((rows, width), BF), ((width, rows), BF)],
                residual_in,
                first_gain,
                first_shift,
                also=[slots["u"][1], slots["d"][1]],
                name="prep",
            )

        def attend_call(which):
            n = len(which)
            for u in which:
                parts = [slots["t"][k] for k in range(u * group, (u + 1) * group)]
                triple_w[u] = parts[0]
                if group > 1:
                    (triple_w[u],) = call(
                        pair_kernel, [((width, 6 * HEAD_DIM), BF)], *parts, name="pair"
                    )
            got = call(
                functools.partial(attend_kernel, n, seqs),
                [((rows, 6 * HEAD_DIM), BF)] * n
                + [((seqs, 2 * SEQ, SEQ), F32)] * n
                + [((rows, 2 * HEAD_DIM), BF)] * n,
                s.first,
                *(triple_w[u] for u in which),
                *scalars,
                scalars=4,
                name="attend",
            )
            for i, u in enumerate(which):
                triples[u], probs[u], mixeds[u] = got[i], got[n + i], got[2 * n + i]

        def project_rows(which):
            for u in which:
                parts = [slots["p"][k] for k in range(u * group, (u + 1) * group)]
                proj_w[u] = parts[0]
                if group > 1:
                    (proj_w[u],) = call(
                        pair_kernel, [((width + 16, 2 * HEAD_DIM), BF)], *parts, name="pair"
                    )

        def cot_low():
            s.out_low, s.out_t = call(
                out_kernel, [((rows, width), BF), ((width, rows), BF)], cotangent, name="out"
            )

        def project():
            project_rows(early)
            (s.acc,) = call(
                functools.partial(project_kernel, len(early)),
                [((rows, width), F32)],
                *(mixeds[u] for u in early),
                *(proj_w[u] for u in early),
                name="project",
            )

        def relay_triple():
            for k in evens:
                relay("t", k)

        def unbundle():
            if shared:
                slots["p"][2], s.half_low = call(
                    unbundle_kernel, [(pack_shape, BF), (half, BF)], s.bundle, name="unbundle"
                )
                slots["p"][3] = links.swap(slots["p"][2], 1)
                s.down_other = links.swap(s.half_low, nslots)
                return
            for k in evens:
                relay("p", k)

        def second():
            project_rows(late)
            s.middle, s.second, s.second_t = call(
                functools.partial(second_kernel, len(late)),
                [((rows, width), F32), ((rows, width), BF), ((width, rows), BF)],
                *(mixeds[u] for u in late),
                *(proj_w[u] for u in late),
                s.acc,
                residual_in,
                proj_bias,
                second_gain,
                second_shift,
                name="second",
            )

        def hidden_call(which):
            n = len(which)
            got = call(
                functools.partial(hidden_kernel, n),
                [((rows, hidden), BF)] * n
                + [((rows, hidden), F32)] * n
                + [((width, hidden), kind(k)) for k in which],
                s.second,
                s.out_t,
                *(slots["u"][k] for k in which),
                *(slots["p"][k] for k in which),
                name="hidden",
            )
            for i, k in enumerate(which):
                acts[k], slopes[k], down_grads[k] = got[i], got[n + i], got[2 * n + i]
                if k != 1:
                    down_sum.give(k, down_grads[k])

        def hidden_back_call(which):
            n, acc = len(which), [s.grad_second] if hasattr(s, "grad_second") else []
            pieces = [thirds if k % 2 and k > 1 else [width] for k in which]
            got = call(
                functools.partial(hidden_back_kernel, [len(p) for p in pieces], not acc),
                [((r, hidden), kind(k)) for k, p in zip(which, pieces) for r in p]
                + [((1, hidden), F32)] * n
                + [((rows, width), F32)],
                s.out_low,
                s.second_t,
                *(slots["u"][k] for k in which),
                *(slots["d"][k] for k in which),
                *(slopes[k] for k in which),
                *acc,
                scratch=[((rows, hidden), BF)] * n,
                name="hidden_back",
            )
            got = list(got)
            for k, p in zip(which, pieces):
                up_grads[k] = [got.pop(0) for _ in p]
                if k != 1:
                    up_sum.give(k, *up_grads[k])
            for k in which:
                biases[k] = got.pop(0)
            s.grad_second = got.pop(0)

        def join_down():
            if shared:
                (slots["d"][2],) = call(
                    functools.partial(join_kernel, 1),
                    [(down_weight.shape, BF)],
                    s.half_low,
                    s.down_other,
                    place,
                    scalars=1,
                    name="join",
                )
                slots["d"][3] = links.swap(slots["d"][2], 1)
                return
            for k in evens:
                relay("d", k)

        def relay_up():
            for k in evens:
                relay("u", k)

        def middle():
            s.grad_middle, s.middle_low, s.middle_t, s.sums_middle = call(
                middle_kernel,
                [((rows, width), F32), ((rows, width), BF), ((width, rows), BF), ((8, width), F32)],
                s.grad_second,
                s.middle,
                second_gain,
                cotangent,
                name="middle",
            )

        def attend_back_call(which):
            n = len(which)
            which_slots = [k for u in which for k in range(group * u, group * (u + 1))]
            pieces = [thirds if k % 2 and k > 1 else [width] for k in which_slots]
            span = 8 * HEAD_DIM // group
            got = call(
                functools.partial(attend_back_kernel, n, group, [len(p) for p in pieces], seqs),
                [((rows, 6 * HEAD_DIM), BF)] * n
                + [((r, span), kind(k)) for k, p in zip(which_slots, pieces) for r in p],
                s.middle_low,
                s.middle_t,
                s.first_t,
                *(proj_w[u] for u in which),
                *(triples[u] for u in which),
                *(probs[u] for u in which),
                *(mixeds[u] for u in which),
                scratch=[((rows, 2 * HEAD_DIM), BF)] * n + [((seqs, 2 * SEQ, SEQ), F32)] * n,
                name="attend_back",
            )
            for i, u in enumerate(which):
                gtls[u] = got[i]
            got = list(got[n:])
            for k, p in zip(which_slots, pieces):
                triple_sum.give(k, *(got.pop(0) for _ in p))

        def heads(chain, spare=False):
            while chain.bit < nslots:
                chain.head(spare=spare)

        def input_grad():
            s.grad_input, s.sums_input = call(
                functools.partial(input_kernel, units),
                [((rows, width), F32, True), ((8, width), F32)],
                *(gtls[u] for u in range(units)),
                *(triple_w[u] for u in range(units)),
                residual_in,
                first_gain,
                s.grad_middle,
                cotangent,
                name="input",
            )

        def vector():
            (s.vector,) = call(
                functools.partial(vector_kernel, [3, 3] + [1] * nslots),
                [((16, width), F32)],
                s.sums_middle,
                s.sums_input,
                *(biases[k] for k in range(nslots)),
                name="vector",
            )
            s.vector_got = links.swap(s.vector, 1)

        def vector_core():
            (triple_sum.rider,) = call(
                functools.partial(vector_core_kernel, nslots, 6),
                [(room, F32)],
                s.vector,
                s.vector_got,
                name="vector_core",
            )

        def halves(chain):
            for bit in middle_bits:
                chain.halve(bit)

        def block():
            (s.block_out,) = call(
                functools.partial(output_kernel, nslots),
                [((rows, width), F32, True)],
                *(acts[k] for k in range(nslots)),
                *(slots["d"][k] for k in range(nslots)),
                s.middle,
                down_bias,
                name="output",
            )

        def settle(chain, order=None):
            chain.settle(order or there[::-1])
            for _ in there[2:]:
                chain.double()

        def settle_triple():
            s.vector = triple_sum.settle(there[::-1])
            for _ in there[2:]:
                triple_sum.double()
            s.vector_bit = 2
            s.vector_got = links.swap(s.vector, 2)

        def finish_triple():
            outs = [(width, 6 * HEAD_DIM // group), (proj_rows, width)], [False, True]
            s.grad_triple, s.grad_proj = triple_sum.finish(*outs)

        def totals():
            while 2 * s.vector_bit < nslots:
                (s.vector,) = call(
                    functools.partial(vector_add_kernel, s.vector_bit // 2, 6),
                    [(room, F32)],
                    s.vector,
                    s.vector_got,
                    name="vector_add",
                )
                s.vector_bit *= 2
                s.vector_got = links.swap(s.vector, s.vector_bit)
            s.totals = call(
                functools.partial(vector_last_kernel, s.vector_bit // 2, 6),
                [((1, width), F32)] * 6 + [((1, hidden), F32)],
                s.vector,
                s.vector_got,
                name="vector_last",
            )

        def finish_down():
            (s.grad_down,) = down_sum.finish([(hidden, width)], [True])

        def finish_up():
            (s.grad_up,) = up_sum.finish([(width, hidden)], [False])

        bundle()
        prep()
        attend_call(early)
        cot_low()
        project()
        relay_triple()
        for u in late:
            attend_call([u])
        unbundle()
        second()
        hidden_call([0, 1])
        hidden_back_call([0, 1])
        join_down()
        relay_up()
        down_sum.give_later(1, down_grads[1])
        up_sum.give_later(1, *up_grads[1])
        for k in evens:
            hidden_call([k])
        for k in odds:
            hidden_call([k])
        down_sum.fold(0)
        up_sum.fold(0)
        for k in evens:
            hidden_back_call([k])
        heads(down_sum, True)
        for k in odds:
            hidden_back_call([k])
        middle()
        for k in evens:
            up_sum.fold(k)
        up_sum.halve(bits[0])
        attend_back_call(late[::-1])
        attend_back_call(early[::-1])
        heads(triple_sum)
        input_grad()
        heads(up_sum)
        down_sum.halve(bits[0])
        vector()
        vector_core()
        halves(down_sum)
        triple_sum.halve(bits[0])
        halves(up_sum)
        down_sum.whole(bits[-1])
        halves(triple_sum)
        triple_sum.whole(bits[-1])
        up_sum.whole(bits[-1])
        block()
        settle(down_sum, there)
        settle_triple()
        settle(up_sum, there)
        down_sum.double()
        triple_sum.double()
        up_sum.double()
        totals()
        finish_down()
        finish_triple()
        finish_up()
        totals = [v.reshape(-1) for v in s.totals]
        return (
            s.block_out,
            s.grad_input,
            s.grad_triple,
            s.grad_proj,
            s.grad_up,
            totals[6],
            s.grad_down,
            totals[0],
            totals[3],
            totals[4],
            totals[5],
            totals[1],
            totals[2],
        )

    return shards


def solution(mesh):
    in_specs = (
        P(("dp", "head"), None),
        P(("dp", "head"), None),
        P(None, "head"),
        P("head", None),
        P(None, "head"),
        P("head"),
        P("head", None),
        P(),
        P(),
        P(),
        P(),
        P(),
        P(),
        P("dp"),
        P("dp"),
        P("dp"),
    )
    out_specs = (
        P(("dp", "head"), None),
        P(("dp", "head"), None),
        P(None, "head"),
        P("head", None),
        P(None, "head"),
        P("head"),
        P("head", None),
        P(),
        P(),
        P(),
        P(),
        P(),
        P(),
    )
    return jax.shard_map(
        make(mesh), mesh=mesh, in_specs=in_specs, out_specs=out_specs, check_vma=False
    )
```

time: 141 us -> 115 us (0.82)
  waiting for transfers between devices: 54.2 us -> 40.1 us
  starting transfers between devices: 38.7 us -> 32.6 us
  Pallas kernels: 38.6 us -> 34.3 us
    ppermute x41 -> x42, waiting for transfers between devices: 54.2 us -> 40.1 us  [swap(): return lax.ppermute(value, AXES, [(i, i ^ bit) for i in range(total)])]
    ppermute x41 -> x42, starting transfers between devices: 38.7 us -> 32.6 us  [swap(): return lax.ppermute(value, AXES, [(i, i ^ bit) for i in range(total)])]
    pallas_call x51 -> x52, Pallas kernels: 38.6 us -> 34.3 us  [call(): pl.pallas_call(ordered, out_shape=[jax.ShapeDtypeStruct(*out[:2]) for out...]
  transfers between devices with their start and end apart: 41 -> 42, of which waited for: 16 -> 20; matrix products, arithmetic and copies ran while one was open for 0% -> 0% of each run, Pallas kernels for 26% -> 28%
where the time goes in v3:
time: 115 us; the launch traced here: 114 us
  waiting for transfers between devices  40.1 us (35%)
  Pallas kernels  34.3 us (30%)
  starting transfers between devices  32.6 us (28%)
  local copies, waits for them, and re-layouts  6.35 us (6%)
    ppermute x42, waiting for transfers between devices, swap(): return lax.ppermute(value, AXES, [(i, i ^ bit) for i in range(total)])  40.1 us
    pallas_call x52, Pallas kernels, call(): pl.pallas_call(ordered, out_shape=[jax.ShapeDtypeStruct(*out[:2]) for out...  34.3 us
    ppermute x42, starting transfers between devices, swap(): return lax.ppermute(value, AXES, [(i, i ^ bit) for i in range(total)])  32.6 us
    unnamed x36, local copies, waits for them, and re-layouts  6.34 us
  transfers between devices with their start and end apart: 42, of which 20 were waited for; matrix products, arithmetic and copies ran while one was open for 0% of the time, Pallas kernels for 28%

profile of v3, /device:TPU:0, one launch (start us, length us, event | category | flops | bytes accessed | tf_op | source)
XLA Modules:
  0.0 114.5 jit_solution(2733308919176757897)
XLA Ops:
  1.7 2.6 %collective-permute-start.2 = (bf16[512,384]{1,0:T(8,128)(2,1)}, bf16[512,384]{1,0:T(8,128)(2,1)S(1)}, u32[]{:S(2)}, u32[]{:S(2)}) collective-permute-start(bf16[512,384]{1,0:T(8,128)(2,1)} %refs_4_.10), channel_id=1, source_target_pairs={{0,2},{1,3},{2,0},{3,1},{4,6},{5,7},{6,4},{7,5},{8,10},{9,11},{10,... | collective-permute-start | bytes 1179656 | tf_op jit(solution)/shard_map/ppermute | solution.py:546
  5.0 1.0 copy-done.3
  6.0 0.9 copy-done.7
  8.2 1.2 %copy-done = f32[512,512]{1,0:T(8,128)S(1)} copy-done((f32[512,512]{1,0:T(8,128)S(1)}, f32[512,512]{1,0:T(8,128)}, u32[]{:S(2)}) %copy-start) | copy-done | bytes 1048600
  10.4 2.5 %attend.3 = (bf16[512,384]{1,0:T(8,128)(2,1)S(1)}, bf16[512,384]{1,0:T(8,128)(2,1)S(1)}, f32[4,256,128]{2,1,0:T(8,128)S(1)}, f32[4,256,128]{2,1,0:T(8,128)S(1)},...) custom-call(bf16[512,512]{1,0:T(8,128)(2,1)S(1)} %get-tuple-element.184.refs_0_, ...), custom_call_target="tpu_custom_call" | custom-call | tf_op jit(solution)/shard_map/attend/pallas_call | solution.py:50
  13.6 0.9 collective-permute-done.2.refs_0_.refs_1_.refs_6_
  14.6 2.0 %collective-permute-start.8 = (bf16[512,512]{1,0:T(8,128)(2,1)S(1)}, bf16[512,512]{1,0:T(8,128)(2,1)S(1)}, u32[]{:S(2)}, u32[]{:S(2)}) collective-permute-start(bf16[512,512]{1,0:T(8,128)(2,1)S(1)} %copy-done.5), channel_id=1, source_target_pairs={{0,2},{1,3},{2,0},{3,1},{4,6},{5,7},{6,4},{7,5},{8,10},{9,11},{10,... | collective-permute-start | bytes 1572872 | tf_op jit(solution)/shard_map/ppermute | solution.py:546
  16.6 1.6 %attend.4 = (bf16[512,384]{1,0:T(8,128)(2,1)S(1)}, f32[4,256,128]{2,1,0:T(8,128)S(1)}, bf16[512,128]{1,0:T(8,128)(2,1)S(1)}, f32[8,128]{1,0:T(8,128)S(1)}) custom-call(bf16[512,512]{1,0:T(8,128)(2,1)S(1)} %get-tuple-element.184.refs_0_, bf16[512,384]{1,0:T(8,128)(2,1)S(1)} %collective-permute-done.2.refs_0_.refs_1_.refs_6_, ...), custom_call_target="tpu_custom_call" | custom-call | tf_op jit(solution)/shard_map/attend/pallas_call | solution.py:50
  18.3 1.6 %attend.5 = (bf16[512,384]{1,0:T(8,128)(2,1)S(1)}, f32[4,256,128]{2,1,0:T(8,128)S(1)}, bf16[512,128]{1,0:T(8,128)(2,1)S(1)}, f32[8,128]{1,0:T(8,128)S(1)}) custom-call(bf16[512,512]{1,0:T(8,128)(2,1)S(1)} %get-tuple-element.184.refs_0_, bf16[512,384]{1,0:T(8,128)(2,1)S(1)} %collective-permute-done.5.refs_1_.refs_7_, s32[1]{0:T(128)} %bitcast.3.refs_4_.refs_3_.refs_2_, ...), custom_call_target="tpu_custom_call" | custom-call | tf_op jit(solution)/shard_map/attend/pallas_call | solution.py:50
  19.9 3.1 %collective-permute-done.6.refs_0_ = bf16[1552,128]{1,0:T(8,128)(2,1)S(1)} collective-permute-done((bf16[1552,128]{1,0:T(8,128)(2,1)S(1)}, bf16[1552,128]{1,0:T(8,128)(2,1)S(1)}, u32[]{:S(2)}, u32[]{:S(2)}) %collective-permute-start.6) | collective-permute-done | bytes 397344 | tf_op jit(solution)/shard_map/ppermute | solution.py:546
  23.0 2.0 %collective-permute-start.9 = (bf16[256,512]{1,0:T(8,128)(2,1)S(1)}, bf16[256,512]{1,0:T(8,128)(2,1)S(1)}, u32[]{:S(2)}, u32[]{:S(2)}) collective-permute-start(bf16[256,512]{1,0:T(8,128)(2,1)S(1)} %get-tuple-element.214.refs_0_), channel_id=1, source_target_pairs={{0,4},{1,5},{2,6},{3,7},{4,0},{5,1},{6,2},{7,3},{8,12},{9,13},{10,... | collective-permute-start | bytes 786440 | tf_op jit(solution)/shard_map/ppermute | solution.py:546
  25.0 1.4 %collective-permute-done.7.refs_3_ = bf16[528,128]{1,0:T(8,128)(2,1)S(1)} collective-permute-done((bf16[528,128]{1,0:T(8,128)(2,1)S(1)}, bf16[528,128]{1,0:T(8,128)(2,1)S(1)}, u32[]{:S(2)}, u32[]{:S(2)}) %collective-permute-start.7) | collective-permute-done | bytes 135200 | tf_op jit(solution)/shard_map/ppermute | solution.py:546
  27.9 2.2 %hidden.3 = (bf16[512,512]{1,0:T(8,128)(2,1)S(1)}, bf16[512,512]{1,0:T(8,128)(2,1)S(1)}, f32[512,512]{1,0:T(8,128)S(1)}, f32[512,512]{1,0:T(8,128)S(1)}, f32[512...) custom-call(bf16[512,512]{1,0:T(8,128)(2,1)S(1)} %get-tuple-element.202.refs_0_, ...), custom_call_target="tpu_custom_call" | custom-call | tf_op jit(solution)/shard_map/hidden/pallas_call | solution.py:50
  30.1 1.8 %hidden_back.3 = (f32[512,512]{1,0:T(8,128)S(1)}, bf16[512,512]{1,0:T(8,128)(2,1)S(1)}, f32[1,512]{1,0:T(1,128)S(1)}, f32[1,512]{1,0:T(1,128)S(1)}, f32[512,512]{1,0:T(8,128)S(1)}, /*index=5*/f32[8,128]{1,0:T(8,128)S(1)}) custom-call(bf16[512,512]{1,0:T(8,128)(2,1)S(1)} %get-tuple-element.207.refs_0_, bf16[512,512]{1,0:T(8,128)(2,1)S(1)} %get-tuple-element.208.refs_1_, ...), custom_call_target="tpu_custom_call" | custom-call | tf_op jit(solution)/shard_map/hidden_back/pallas_call | solution.py:50
  32.0 2.0 %collective-permute-done.8.refs_0_.refs_2_ = bf16[512,512]{1,0:T(8,128)(2,1)S(1)} collective-permute-done((bf16[512,512]{1,0:T(8,128)(2,1)S(1)}, bf16[512,512]{1,0:T(8,128)(2,1)S(1)}, u32[]{:S(2)}, u32[]{:S(2)}) %collective-permute-start.8) | collective-permute-done | bytes 524320 | tf_op jit(solution)/shard_map/ppermute | solution.py:546
  34.8 1.2 %hidden.4 = (bf16[512,512]{1,0:T(8,128)(2,1)S(1)}, f32[512,512]{1,0:T(8,128)S(1)}, f32[512,512]{1,0:T(8,128)S(1)}, f32[8,128]{1,0:T(8,128)S(1)}) custom-call(bf16[512,512]{1,0:T(8,128)(2,1)S(1)} %get-tuple-element.202.refs_0_, bf16[512,512]{1,0:T(8,128)(2,1)S(1)} %get-tuple-element.203.refs_1_, bf16[512,512]{1,0:T(8,128)(2,1)S(1)} %collective-permute-done.8.refs_0_.refs_2_, ...), custom_call_target="tpu_custom_call" | custom-call | tf_op jit(solution)/shard_map/hidden/pallas_call | solution.py:50
  36.0 1.2 %hidden.5 = (bf16[512,512]{1,0:T(8,128)(2,1)S(1)}, f32[512,512]{1,0:T(8,128)S(1)}, bf16[512,512]{1,0:T(8,128)(2,1)S(1)}, f32[8,128]{1,0:T(8,128)S(1)}) custom-call(bf16[512,512]{1,0:T(8,128)(2,1)S(1)} %get-tuple-element.202.refs_0_, bf16[512,512]{1,0:T(8,128)(2,1)S(1)} %get-tuple-element.203.refs_1_, bf16[512,512]{1,0:T(8,128)(2,1)S(1)} %collective-permute-done.10.refs_2_, ...), custom_call_target="tpu_custom_call" | custom-call | tf_op jit(solution)/shard_map/hidden/pallas_call | solution.py:50
  38.2 1.0 hidden_back.4
  40.0 1.0 hidden_back.5
  41.9 1.8 %collective-permute-start.25 = (bf16[528,512]{1,0:T(8,128)(2,1)S(1)}, bf16[528,512]{1,0:T(8,128)(2,1)S(1)}, u32[]{:S(2)}, u32[]{:S(2)}) collective-permute-start(bf16[528,512]{1,0:T(8,128)(2,1)S(1)} %get-tuple-element.290), channel_id=1, source_target_pairs={{0,2},{1,3},{2,0},{3,1},{4,6},{5,7},{6,4},{7,5},{8,10},{9,11},{10,... | collective-permute-start | bytes 1622024 | tf_op jit(solution)/shard_map/ppermute | solution.py:546
  43.7 1.0 middle.1
  45.0 1.6 %collective-permute-start.18 = (bf16[512,512]{1,0:T(8,128)(2,1)S(1)}, bf16[512,512]{1,0:T(8,128)(2,1)S(1)}, u32[]{:S(2)}, u32[]{:S(2)}) collective-permute-start(bf16[512,512]{1,0:T(8,128)(2,1)S(1)} %get-tuple-element.252), channel_id=1, source_target_pairs={{0,4},{1,5},{2,6},{3,7},{4,0},{5,1},{6,2},{7,3},{8,12},{9,13},{10,... | collective-permute-start | bytes 1572872 | tf_op jit(solution)/shard_map/ppermute | solution.py:546
  46.6 2.6 %attend_back.2 = (bf16[512,384]{1,0:T(8,128)(2,1)S(1)}, bf16[512,384]{1,0:T(8,128)(2,1)S(1)}, bf16[176,512]{1,0:T(8,128)(2,1)S(1)}, bf16[176,512]{1,0:T(8,128)(2...) custom-call(bf16[512,512]{1,0:T(8,128)(2,1)S(1)} %get-tuple-element.254.refs_0_, ...), custom_call_target="tpu_custom_call" | custom-call | tf_op jit(solution)/shard_map/attend_back/pallas_call | solution.py:50
  49.9 2.6 %attend_back.3 = (bf16[512,384]{1,0:T(8,128)(2,1)S(1)}, bf16[512,384]{1,0:T(8,128)(2,1)S(1)}, bf16[512,512]{1,0:T(8,128)(2,1)S(1)}, f32[512,512]{1,0:T(8,128)S(1)}, f32[8,128]{1,0:T(8,128)S(1)}) custom-call(bf16[512,512]{1,0:T(8,128)(2,1)S(1)} %get-tuple-element.254.refs_0_, bf16[512,512]{1,0:T(8,128)(2,1)S(1)} %get-tuple-element.255.refs_1_, ...), custom_call_target="tpu_custom_call" | custom-call | tf_op jit(solution)/shard_map/attend_back/pallas_call | solution.py:50
  53.7 3.3 %input.1 = (f32[512,512]{1,0:T(8,128)}, f32[8,512]{1,0:T(8,128)S(1)}, f32[8,128]{1,0:T(8,128)S(1)}) custom-call(bf16[512,384]{1,0:T(8,128)(2,1)S(1)} %get-tuple-element.267.refs_0_, bf16[512,384]{1,0:T(8,128)(2,1)S(1)} %get-tuple-element.268.refs_1_, bf16[512,384]{1,0:T(8,128)(2,1)S(1)} %get-tuple-element.269.refs_2_, ...), custom_call_target="tpu_custom_call" | custom-call | tf_op jit(solution)/shard_map/input/pallas_call | solution.py:50
  57.0 1.7 %collective-permute-done.18.refs_1_ = bf16[512,512]{1,0:T(8,128)(2,1)S(1)} collective-permute-done((bf16[512,512]{1,0:T(8,128)(2,1)S(1)}, bf16[512,512]{1,0:T(8,128)(2,1)S(1)}, u32[]{:S(2)}, u32[]{:S(2)}) %collective-permute-start.18) | collective-permute-done | bytes 524320 | tf_op jit(solution)/shard_map/ppermute | solution.py:546
  59.0 1.6 %collective-permute-start.27 = (bf16[272,512]{1,0:T(8,128)(2,1)S(1)}, bf16[272,512]{1,0:T(8,128)(2,1)S(1)}, u32[]{:S(2)}, u32[]{:S(2)}) collective-permute-start(bf16[272,512]{1,0:T(8,128)(2,1)S(1)} %get-tuple-element.297), channel_id=1, source_target_pairs={{0,4},{1,5},{2,6},{3,7},{4,0},{5,1},{6,2},{7,3},{8,12},{9,13},{10,... | collective-permute-start | bytes 835592 | tf_op jit(solution)/shard_map/ppermute | solution.py:546
  61.8 4.8 %collective-permute-done.27.refs_1_ = bf16[272,512]{1,0:T(8,128)(2,1)S(1)} collective-permute-done((bf16[272,512]{1,0:T(8,128)(2,1)S(1)}, bf16[272,512]{1,0:T(8,128)(2,1)S(1)}, u32[]{:S(2)}, u32[]{:S(2)}) %collective-permute-start.27) | collective-permute-done | bytes 278560 | tf_op jit(solution)/shard_map/ppermute | solution.py:546
  66.6 1.4 %collective-permute-done.24.refs_2_ = bf16[512,512]{1,0:T(8,128)(2,1)S(1)} collective-permute-done((bf16[512,512]{1,0:T(8,128)(2,1)S(1)}, bf16[512,512]{1,0:T(8,128)(2,1)S(1)}, u32[]{:S(2)}, u32[]{:S(2)}) %collective-permute-start.24) | collective-permute-done | bytes 524320 | tf_op jit(solution)/shard_map/ppermute | solution.py:546
  68.2 2.1 %collective-permute-start.29 = (bf16[272,512]{1,0:T(8,128)(2,1)S(1)}, bf16[272,512]{1,0:T(8,128)(2,1)S(1)}, u32[]{:S(2)}, u32[]{:S(2)}) collective-permute-start(bf16[272,512]{1,0:T(8,128)(2,1)S(1)} %get-tuple-element.304), channel_id=1, source_target_pairs={{0,4},{1,5},{2,6},{3,7},{4,0},{5,1},{6,2},{7,3},{8,12},{9,13},{10,... | collective-permute-start | bytes 835592 | tf_op jit(solution)/shard_map/ppermute | solution.py:546
  70.3 1.6 %collective-permute-start.30 = (bf16[144,512]{1,0:T(8,128)(2,1)S(1)}, bf16[144,512]{1,0:T(8,128)(2,1)S(1)}, u32[]{:S(2)}, u32[]{:S(2)}) collective-permute-start(bf16[144,512]{1,0:T(8,128)(2,1)S(1)} %get-tuple-element.307), channel_id=1, source_target_pairs={{0,8},{1,9},{2,10},{3,11},{4,12},{5,13},{6,14},{7,15},{8,0},{9,1},... | collective-permute-start | bytes 442376 | tf_op jit(solution)/shard_map/ppermute | solution.py:546
  71.8 1.7 %collective-permute-done.22.refs_2_ = bf16[272,512]{1,0:T(8,128)(2,1)S(1)} collective-permute-done((bf16[272,512]{1,0:T(8,128)(2,1)S(1)}, bf16[272,512]{1,0:T(8,128)(2,1)S(1)}, u32[]{:S(2)}, u32[]{:S(2)}) %collective-permute-start.22) | collective-permute-done | bytes 278560 | tf_op jit(solution)/shard_map/ppermute | solution.py:546
  73.6 1.8 %collective-permute-done.30.refs_1_ = bf16[144,512]{1,0:T(8,128)(2,1)S(1)} collective-permute-done((bf16[144,512]{1,0:T(8,128)(2,1)S(1)}, bf16[144,512]{1,0:T(8,128)(2,1)S(1)}, u32[]{:S(2)}, u32[]{:S(2)}) %collective-permute-start.30) | collective-permute-done | bytes 147488 | tf_op jit(solution)/shard_map/ppermute | solution.py:546
  76.0 1.8 %collective-permute-start.31 = (bf16[144,512]{1,0:T(8,128)(2,1)S(1)}, bf16[144,512]{1,0:T(8,128)(2,1)S(1)}, u32[]{:S(2)}, u32[]{:S(2)}) collective-permute-start(bf16[144,512]{1,0:T(8,128)(2,1)S(1)} %get-tuple-element.311), channel_id=1, source_target_pairs={{0,8},{1,9},{2,10},{3,11},{4,12},{5,13},{6,14},{7,15},{8,0},{9,1},... | collective-permute-start | bytes 442376 | tf_op jit(solution)/shard_map/ppermute | solution.py:546
  78.1 2.8 %collective-permute-start.33 = (bf16[144,512]{1,0:T(8,128)(2,1)S(1)}, bf16[144,512]{1,0:T(8,128)(2,1)S(1)}, u32[]{:S(2)}, u32[]{:S(2)}) collective-permute-start(bf16[144,512]{1,0:T(8,128)(2,1)S(1)} %get-tuple-element.322), channel_id=1, source_target_pairs={{0,16},{1,17},{2,18},{3,19},{4,20},{5,21},{6,22},{7,23},{8,24},{9,... | collective-permute-start | bytes 442376 | tf_op jit(solution)/shard_map/ppermute | solution.py:546
  80.9 4.0 %collective-permute-done.31.refs_1_ = bf16[144,512]{1,0:T(8,128)(2,1)S(1)} collective-permute-done((bf16[144,512]{1,0:T(8,128)(2,1)S(1)}, bf16[144,512]{1,0:T(8,128)(2,1)S(1)}, u32[]{:S(2)}, u32[]{:S(2)}) %collective-permute-start.31) | collective-permute-done | bytes 147488 | tf_op jit(solution)/shard_map/ppermute | solution.py:546
  84.9 1.3 %collective-permute-start.32 = (bf16[144,512]{1,0:T(8,128)(2,1)S(1)}, bf16[144,512]{1,0:T(8,128)(2,1)S(1)}, u32[]{:S(2)}, u32[]{:S(2)}) collective-permute-start(bf16[144,512]{1,0:T(8,128)(2,1)S(1)} %get-tuple-element.319), channel_id=1, source_target_pairs={{0,16},{1,17},{2,18},{3,19},{4,20},{5,21},{6,22},{7,23},{8,24},{9,... | collective-permute-start | bytes 442376 | tf_op jit(solution)/shard_map/ppermute | solution.py:546
  86.2 1.8 %collective-permute-done.28.refs_1_ = bf16[144,512]{1,0:T(8,128)(2,1)S(1)} collective-permute-done((bf16[144,512]{1,0:T(8,128)(2,1)S(1)}, bf16[144,512]{1,0:T(8,128)(2,1)S(1)}, u32[]{:S(2)}, u32[]{:S(2)}) %collective-permute-start.28) | collective-permute-done | bytes 147488 | tf_op jit(solution)/shard_map/ppermute | solution.py:546
  89.6 2.2 %output.1 = (f32[512,512]{1,0:T(8,128)}, f32[8,128]{1,0:T(8,128)S(1)}) custom-call(bf16[512,512]{1,0:T(8,128)(2,1)S(1)} %get-tuple-element.205.refs_0_, bf16[512,512]{1,0:T(8,128)(2,1)S(1)} %get-tuple-element.206.refs_1_, bf16[512,512]{1,0:T(8,128)(2,1)S(1)} %get-tuple-element.220.refs_2_, bf16[512,512]{1,0:T(8,128)(2,1)S(1)} %get-tuple-element.223.refs_3_, ...), custom_call_target="tpu_custom_call" | custom-call | tf_op jit(solution)/shard_map/output/pallas_call | solution.py:50
  91.8 3.3 %collective-permute-done.33.refs_1_ = bf16[144,512]{1,0:T(8,128)(2,1)S(1)} collective-permute-done((bf16[144,512]{1,0:T(8,128)(2,1)S(1)}, bf16[144,512]{1,0:T(8,128)(2,1)S(1)}, u32[]{:S(2)}, u32[]{:S(2)}) %collective-permute-start.33) | collective-permute-done | bytes 147488 | tf_op jit(solution)/shard_map/ppermute | solution.py:546
  95.1 0.9 collective-permute-start.35
  96.0 1.8 %collective-permute-done.32.refs_1_ = bf16[144,512]{1,0:T(8,128)(2,1)S(1)} collective-permute-done((bf16[144,512]{1,0:T(8,128)(2,1)S(1)}, bf16[144,512]{1,0:T(8,128)(2,1)S(1)}, u32[]{:S(2)}, u32[]{:S(2)}) %collective-permute-start.32) | collective-permute-done | bytes 147488 | tf_op jit(solution)/shard_map/ppermute | solution.py:546
  97.9 1.5 %collective-permute-done.36.refs_1_ = bf16[144,512]{1,0:T(8,128)(2,1)S(1)} collective-permute-done((bf16[144,512]{1,0:T(8,128)(2,1)S(1)}, bf16[144,512]{1,0:T(8,128)(2,1)S(1)}, u32[]{:S(2)}, u32[]{:S(2)}) %collective-permute-start.36) | collective-permute-done | bytes 147488 | tf_op jit(solution)/shard_map/ppermute | solution.py:546
  100.8 3.6 %collective-permute-done.34.refs_1_ = bf16[128,512]{1,0:T(8,128)(2,1)S(1)} collective-permute-done((bf16[128,512]{1,0:T(8,128)(2,1)S(1)}, bf16[128,512]{1,0:T(8,128)(2,1)S(1)}, u32[]{:S(2)}, u32[]{:S(2)}) %collective-permute-start.34) | collective-permute-done | bytes 131104 | tf_op jit(solution)/shard_map/ppermute | solution.py:546
  107.1 3.1 %collective-permute-done.39.refs_1_ = f32[8,512]{1,0:T(8,128)S(1)} collective-permute-done((f32[8,512]{1,0:T(8,128)S(1)}, f32[8,512]{1,0:T(8,128)S(1)}, u32[]{:S(2)}, u32[]{:S(2)}) %collective-permute-start.39) | collective-permute-done | bytes 16416 | tf_op jit(solution)/shard_map/ppermute | solution.py:546
  110.8 1.4 %finish_d.1 = (f32[512,512]{1,0:T(8,128)}, f32[8,128]{1,0:T(8,128)S(1)}) custom-call(bf16[256,512]{1,0:T(8,128)(2,1)S(1)} %get-tuple-element.333.refs_0_, bf16[256,512]{1,0:T(8,128)(2,1)S(1)} %collective-permute-done.38.refs_1_, s32[1]{0:T(128)} %bitcast.2.refs_3_.refs_2_.refs_4_, f32[8,128]{1,0:T(8,128)S(1)} %get-tuple-element.338.refs_3_), custom_call_target="tpu_custom_call" | custom-call | tf_op jit(solution)/shard_map/finish_d/pallas_call | solution.py:50
  112.2 1.2 %finish_t.1 = (f32[512,384]{1,0:T(8,128)}, f32[128,512]{1,0:T(8,128)}, f32[8,128]{1,0:T(8,128)S(1)}) custom-call(bf16[256,512]{1,0:T(8,128)(2,1)S(1)} %get-tuple-element.332.refs_0_, bf16[256,512]{1,0:T(8,128)(2,1)S(1)} %collective-permute-done.37.refs_1_, s32[1]{0:T(128)} %bitcast.2.refs_3_.refs_2_.refs_4_, f32[8,128]{1,0:T(8,128)S(1)} %get-tuple-element.339.refs_3_), custom_call_target="tpu_custom_call" | custom-call | tf_op jit(solution)/shard_map/finish_t/pallas_call | solution.py:50
  113.4 1.1 finish_u.1
  (126 shorter events, 21.0 us)
Async XLA Ops:
  0.6 6.6 %collective-permute-start = (bf16[512,512]{1,0:T(8,128)(2,1)}, bf16[512,512]{1,0:T(8,128)(2,1)S(1)}, u32[]{:S(2)}, u32[]{:S(2)}) collective-permute-start(bf16[512,512]{1,0:T(8,128)(2,1)} %refs_2_.5), channel_id=1, source_target_pairs={{0,1},{1,0},{2,3},{3,2},{4,5},{5,4},{6,7},{7,6},{8,9},{9,8},{10,11... | collective-permute-start | bytes 1572872 | tf_op jit(solution)/shard_map/ppermute | solution.py:546
  1.2 6.4 %collective-permute-start.1 = (bf16[512,512]{1,0:T(8,128)(2,1)}, bf16[512,512]{1,0:T(8,128)(2,1)S(1)}, u32[]{:S(2)}, u32[]{:S(2)}) collective-permute-start(bf16[512,512]{1,0:T(8,128)(2,1)} %refs_4_.11), channel_id=1, source_target_pairs={{0,1},{1,0},{2,3},{3,2},{4,5},{5,4},{6,7},{7,6},{8,9},{9,8},{10,11... | collective-permute-start | bytes 1572872 | tf_op jit(solution)/shard_map/ppermute | solution.py:546
  1.2 8.8 %collective-permute-start.3 = (bf16[512,384]{1,0:T(8,128)(2,1)}, bf16[512,384]{1,0:T(8,128)(2,1)S(1)}, u32[]{:S(2)}, u32[]{:S(2)}) collective-permute-start(bf16[512,384]{1,0:T(8,128)(2,1)} %refs_4_.10), channel_id=1, source_target_pairs={{0,1},{1,0},{2,3},{3,2},{4,5},{5,4},{6,7},{7,6},{8,9},{9,8},{10,11... | collective-permute-start | bytes 1179656 | tf_op jit(solution)/shard_map/ppermute | solution.py:546
  1.7 12.8 %collective-permute-start.2 = (bf16[512,384]{1,0:T(8,128)(2,1)}, bf16[512,384]{1,0:T(8,128)(2,1)S(1)}, u32[]{:S(2)}, u32[]{:S(2)}) collective-permute-start(bf16[512,384]{1,0:T(8,128)(2,1)} %refs_4_.10), channel_id=1, source_target_pairs={{0,2},{1,3},{2,0},{3,1},{4,6},{5,7},{6,4},{7,5},{8,10},{9,11},{10,... | collective-permute-start | bytes 1179656 | tf_op jit(solution)/shard_map/ppermute | solution.py:546
  7.0 6.1 %collective-permute-start.4 = (bf16[528,128]{1,0:T(8,128)(2,1)S(1)}, bf16[528,128]{1,0:T(8,128)(2,1)S(1)}, u32[]{:S(2)}, u32[]{:S(2)}) collective-permute-start(bf16[528,128]{1,0:T(8,128)(2,1)S(1)} %get-tuple-element.188.refs_2_.refs_4_), channel_id=1, source_target_pairs={{0,1},{1,0},{2,3},{3,2},{4,5},{5,4},{6,7},{7,6},{8,9},{9,8},{10,11... | collective-permute-start | bytes 405512 | tf_op jit(solution)/shard_map/ppermute | solution.py:546
  7.2 15.7 %collective-permute-start.6 = (bf16[1552,128]{1,0:T(8,128)(2,1)S(1)}, bf16[1552,128]{1,0:T(8,128)(2,1)S(1)}, u32[]{:S(2)}, u32[]{:S(2)}) collective-permute-start(bf16[1552,128]{1,0:T(8,128)(2,1)S(1)} %get-tuple-element.197), channel_id=1, source_target_pairs={{0,2},{1,3},{2,0},{3,1},{4,6},{5,7},{6,4},{7,5},{8,10},{9,11},{10,... | collective-permute-start | bytes 1191944 | tf_op jit(solution)/shard_map/ppermute | solution.py:546
  8.2 1.2 %copy-start = (f32[512,512]{1,0:T(8,128)S(1)}, f32[512,512]{1,0:T(8,128)}, u32[]{:S(2)}) copy-start(f32[512,512]{1,0:T(8,128)} %refs_8_.1) | copy-start | bytes 3145732
  10.0 2.9 %copy-start.2 = (f32[512,512]{1,0:T(8,128)S(1)}, f32[512,512]{1,0:T(8,128)}, u32[]{:S(2)}) copy-start(f32[512,512]{1,0:T(8,128)} %refs_11_.1) | copy-start | bytes 3145732
  13.1 1.4 %copy-start.5 = (bf16[512,512]{1,0:T(8,128)(2,1)S(1)}, bf16[512,512]{1,0:T(8,128)(2,1)}, u32[]{:S(2)}) copy-start(bf16[512,512]{1,0:T(8,128)(2,1)} %refs_2_.5) | copy-start | bytes 1572868
  14.5 3.8 %collective-permute-start.5 = (bf16[512,384]{1,0:T(8,128)(2,1)S(1)}, bf16[512,384]{1,0:T(8,128)(2,1)S(1)}, u32[]{:S(2)}, u32[]{:S(2)}) collective-permute-start(bf16[512,384]{1,0:T(8,128)(2,1)S(1)} %get-tuple-element.194), channel_id=1, source_target_pairs={{0,1},{1,0},{2,3},{3,2},{4,5},{5,4},{6,7},{7,6},{8,9},{9,8},{10,11... | collective-permute-start | bytes 1179656 | tf_op jit(solution)/shard_map/ppermute | solution.py:546
  14.6 19.4 %collective-permute-start.8 = (bf16[512,512]{1,0:T(8,128)(2,1)S(1)}, bf16[512,512]{1,0:T(8,128)(2,1)S(1)}, u32[]{:S(2)}, u32[]{:S(2)}) collective-permute-start(bf16[512,512]{1,0:T(8,128)(2,1)S(1)} %copy-done.5), channel_id=1, source_target_pairs={{0,2},{1,3},{2,0},{3,1},{4,6},{5,7},{6,4},{7,5},{8,10},{9,11},{10,... | collective-permute-start | bytes 1572872 | tf_op jit(solution)/shard_map/ppermute | solution.py:546
  16.6 9.8 %copy-start.1 = (f32[512,512]{1,0:T(8,128)S(1)}, f32[512,512]{1,0:T(8,128)}, u32[]{:S(2)}) copy-start(f32[512,512]{1,0:T(8,128)} %refs_8_.1) | copy-start | bytes 3145732
  23.0 3.4 %copy-start.16 = (f32[512]{0:T(512)S(1)}, f32[512]{0:T(512)}, u32[]{:S(2)}) copy-start(f32[512]{0:T(512)} %param.28) | copy-start | bytes 6148
  23.0 8.9 %collective-permute-start.9 = (bf16[256,512]{1,0:T(8,128)(2,1)S(1)}, bf16[256,512]{1,0:T(8,128)(2,1)S(1)}, u32[]{:S(2)}, u32[]{:S(2)}) collective-permute-start(bf16[256,512]{1,0:T(8,128)(2,1)S(1)} %get-tuple-element.214.refs_0_), channel_id=1, source_target_pairs={{0,4},{1,5},{2,6},{3,7},{4,0},{5,1},{6,2},{7,3},{8,12},{9,13},{10,... | collective-permute-start | bytes 786440 | tf_op jit(solution)/shard_map/ppermute | solution.py:546
  25.0 1.4 %collective-permute-start.7 = (bf16[528,128]{1,0:T(8,128)(2,1)S(1)}, bf16[528,128]{1,0:T(8,128)(2,1)S(1)}, u32[]{:S(2)}, u32[]{:S(2)}) collective-permute-start(bf16[528,128]{1,0:T(8,128)(2,1)S(1)} %get-tuple-element.199.refs_2_.refs_3_.refs_4_), channel_id=1, source_target_pairs={{0,1},{1,0},{2,3},{3,2},{4,5},{5,4},{6,7},{7,6},{8,9},{9,8},{10,11... | collective-permute-start | bytes 405512 | tf_op jit(solution)/shard_map/ppermute | solution.py:546
  27.9 2.2 %copy-start.4 = (bf16[512,512]{1,0:T(8,128)(2,1)S(1)}, bf16[512,512]{1,0:T(8,128)(2,1)}, u32[]{:S(2)}) copy-start(bf16[512,512]{1,0:T(8,128)(2,1)} %refs_4_.11) | copy-start | bytes 1572868
  34.0 2.0 %collective-permute-start.10 = (bf16[512,512]{1,0:T(8,128)(2,1)S(1)}, bf16[512,512]{1,0:T(8,128)(2,1)S(1)}, u32[]{:S(2)}, u32[]{:S(2)}) collective-permute-start(bf16[512,512]{1,0:T(8,128)(2,1)S(1)} %get-tuple-element.221), channel_id=1, source_target_pairs={{0,1},{1,0},{2,3},{3,2},{4,5},{5,4},{6,7},{7,6},{8,9},{9,8},{10,11... | collective-permute-start | bytes 1572872 | tf_op jit(solution)/shard_map/ppermute | solution.py:546
  34.1 3.7 %collective-permute-start.13 = (bf16[512,512]{1,0:T(8,128)(2,1)S(1)}, bf16[512,512]{1,0:T(8,128)(2,1)S(1)}, u32[]{:S(2)}, u32[]{:S(2)}) collective-permute-start(bf16[512,512]{1,0:T(8,128)(2,1)S(1)} %get-tuple-element.228), channel_id=1, source_target_pairs={{0,1},{1,0},{2,3},{3,2},{4,5},{5,4},{6,7},{7,6},{8,9},{9,8},{10,11... | collective-permute-start | bytes 1572872 | tf_op jit(solution)/shard_map/ppermute | solution.py:546
  34.7 3.2 %collective-permute-start.12 = (bf16[512,512]{1,0:T(8,128)(2,1)S(1)}, bf16[512,512]{1,0:T(8,128)(2,1)S(1)}, u32[]{:S(2)}, u32[]{:S(2)}) collective-permute-start(bf16[512,512]{1,0:T(8,128)(2,1)S(1)} %get-tuple-element.226), channel_id=1, source_target_pairs={{0,1},{1,0},{2,3},{3,2},{4,5},{5,4},{6,7},{7,6},{8,9},{9,8},{10,11... | collective-permute-start | bytes 1572872 | tf_op jit(solution)/shard_map/ppermute | solution.py:546
  37.1 2.1 %collective-permute-start.14 = (bf16[512,512]{1,0:T(8,128)(2,1)S(1)}, bf16[512,512]{1,0:T(8,128)(2,1)S(1)}, u32[]{:S(2)}, u32[]{:S(2)}) collective-permute-start(bf16[512,512]{1,0:T(8,128)(2,1)S(1)} %get-tuple-element.238), channel_id=1, source_target_pairs={{0,1},{1,0},{2,3},{3,2},{4,5},{5,4},{6,7},{7,6},{8,9},{9,8},{10,11... | collective-permute-start | bytes 1572872 | tf_op jit(solution)/shard_map/ppermute | solution.py:546
  37.7 2.3 %collective-permute-start.11 = (bf16[512,512]{1,0:T(8,128)(2,1)S(1)}, bf16[512,512]{1,0:T(8,128)(2,1)S(1)}, u32[]{:S(2)}, u32[]{:S(2)}) collective-permute-start(bf16[512,512]{1,0:T(8,128)(2,1)S(1)} %get-tuple-element.224.refs_3_.refs_6_), channel_id=1, source_target_pairs={{0,1},{1,0},{2,3},{3,2},{4,5},{5,4},{6,7},{7,6},{8,9},{9,8},{10,11... | collective-permute-start | bytes 1572872 | tf_op jit(solution)/shard_map/ppermute | solution.py:546
  41.0 3.8 %collective-permute-start.15 = (bf16[176,512]{1,0:T(8,128)(2,1)S(1)}, bf16[176,512]{1,0:T(8,128)(2,1)S(1)}, u32[]{:S(2)}, u32[]{:S(2)}) collective-permute-start(bf16[176,512]{1,0:T(8,128)(2,1)S(1)} %get-tuple-element.242), channel_id=1, source_target_pairs={{0,1},{1,0},{2,3},{3,2},{4,5},{5,4},{6,7},{7,6},{8,9},{9,8},{10,11... | collective-permute-start | bytes 540680 | tf_op jit(solution)/shard_map/ppermute | solution.py:546
  41.4 3.3 %collective-permute-start.16 = (bf16[176,512]{1,0:T(8,128)(2,1)S(1)}, bf16[176,512]{1,0:T(8,128)(2,1)S(1)}, u32[]{:S(2)}, u32[]{:S(2)}) collective-permute-start(bf16[176,512]{1,0:T(8,128)(2,1)S(1)} %get-tuple-element.243), channel_id=1, source_target_pairs={{0,1},{1,0},{2,3},{3,2},{4,5},{5,4},{6,7},{7,6},{8,9},{9,8},{10,11... | collective-permute-start | bytes 540680 | tf_op jit(solution)/shard_map/ppermute | solution.py:546
  41.6 3.2 %collective-permute-start.17 = (bf16[160,512]{1,0:T(8,128)(2,1)S(1)}, bf16[160,512]{1,0:T(8,128)(2,1)S(1)}, u32[]{:S(2)}, u32[]{:S(2)}) collective-permute-start(bf16[160,512]{1,0:T(8,128)(2,1)S(1)} %get-tuple-element.244), channel_id=1, source_target_pairs={{0,1},{1,0},{2,3},{3,2},{4,5},{5,4},{6,7},{7,6},{8,9},{9,8},{10,11... | collective-permute-start | bytes 491528 | tf_op jit(solution)/shard_map/ppermute | solution.py:546
  41.9 16.9 %collective-permute-start.25 = (bf16[528,512]{1,0:T(8,128)(2,1)S(1)}, bf16[528,512]{1,0:T(8,128)(2,1)S(1)}, u32[]{:S(2)}, u32[]{:S(2)}) collective-permute-start(bf16[528,512]{1,0:T(8,128)(2,1)S(1)} %get-tuple-element.290), channel_id=1, source_target_pairs={{0,2},{1,3},{2,0},{3,1},{4,6},{5,7},{6,4},{7,5},{8,10},{9,11},{10,... | collective-permute-start | bytes 1622024 | tf_op jit(solution)/shard_map/ppermute | solution.py:546
  45.0 13.8 %collective-permute-start.18 = (bf16[512,512]{1,0:T(8,128)(2,1)S(1)}, bf16[512,512]{1,0:T(8,128)(2,1)S(1)}, u32[]{:S(2)}, u32[]{:S(2)}) collective-permute-start(bf16[512,512]{1,0:T(8,128)(2,1)S(1)} %get-tuple-element.252), channel_id=1, source_target_pairs={{0,4},{1,5},{2,6},{3,7},{4,0},{5,1},{6,2},{7,3},{8,12},{9,13},{10,... | collective-permute-start | bytes 1572872 | tf_op jit(solution)/shard_map/ppermute | solution.py:546
  49.2 3.8 %collective-permute-start.19 = (bf16[176,512]{1,0:T(8,128)(2,1)S(1)}, bf16[176,512]{1,0:T(8,128)(2,1)S(1)}, u32[]{:S(2)}, u32[]{:S(2)}) collective-permute-start(bf16[176,512]{1,0:T(8,128)(2,1)S(1)} %get-tuple-element.273), channel_id=1, source_target_pairs={{0,1},{1,0},{2,3},{3,2},{4,5},{5,4},{6,7},{7,6},{8,9},{9,8},{10,11... | collective-permute-start | bytes 540680 | tf_op jit(solution)/shard_map/ppermute | solution.py:546
  49.3 3.7 %collective-permute-start.20 = (bf16[176,512]{1,0:T(8,128)(2,1)S(1)}, bf16[176,512]{1,0:T(8,128)(2,1)S(1)}, u32[]{:S(2)}, u32[]{:S(2)}) collective-permute-start(bf16[176,512]{1,0:T(8,128)(2,1)S(1)} %get-tuple-element.274), channel_id=1, source_target_pairs={{0,1},{1,0},{2,3},{3,2},{4,5},{5,4},{6,7},{7,6},{8,9},{9,8},{10,11... | collective-permute-start | bytes 540680 | tf_op jit(solution)/shard_map/ppermute | solution.py:546
  49.8 2.7 %collective-permute-start.21 = (bf16[160,512]{1,0:T(8,128)(2,1)S(1)}, bf16[160,512]{1,0:T(8,128)(2,1)S(1)}, u32[]{:S(2)}, u32[]{:S(2)}) collective-permute-start(bf16[160,512]{1,0:T(8,128)(2,1)S(1)} %get-tuple-element.275), channel_id=1, source_target_pairs={{0,1},{1,0},{2,3},{3,2},{4,5},{5,4},{6,7},{7,6},{8,9},{9,8},{10,11... | collective-permute-start | bytes 491528 | tf_op jit(solution)/shard_map/ppermute | solution.py:546
  52.6 14.1 %collective-permute-start.23 = (bf16[512,512]{1,0:T(8,128)(2,1)S(1)}, bf16[512,512]{1,0:T(8,128)(2,1)S(1)}, u32[]{:S(2)}, u32[]{:S(2)}) collective-permute-start(bf16[512,512]{1,0:T(8,128)(2,1)S(1)} %get-tuple-element.281), channel_id=1, source_target_pairs={{0,1},{1,0},{2,3},{3,2},{4,5},{5,4},{6,7},{7,6},{8,9},{9,8},{10,11... | collective-permute-start | bytes 1572872 | tf_op jit(solution)/shard_map/ppermute | solution.py:546
  53.2 14.8 %collective-permute-start.24 = (bf16[512,512]{1,0:T(8,128)(2,1)S(1)}, bf16[512,512]{1,0:T(8,128)(2,1)S(1)}, u32[]{:S(2)}, u32[]{:S(2)}) collective-permute-start(bf16[512,512]{1,0:T(8,128)(2,1)S(1)} %get-tuple-element.282), channel_id=1, source_target_pairs={{0,2},{1,3},{2,0},{3,1},{4,6},{5,7},{6,4},{7,5},{8,10},{9,11},{10,... | collective-permute-start | bytes 1572872 | tf_op jit(solution)/shard_map/ppermute | solution.py:546
  59.0 7.6 %collective-permute-start.27 = (bf16[272,512]{1,0:T(8,128)(2,1)S(1)}, bf16[272,512]{1,0:T(8,128)(2,1)S(1)}, u32[]{:S(2)}, u32[]{:S(2)}) collective-permute-start(bf16[272,512]{1,0:T(8,128)(2,1)S(1)} %get-tuple-element.297), channel_id=1, source_target_pairs={{0,4},{1,5},{2,6},{3,7},{4,0},{5,1},{6,2},{7,3},{8,12},{9,13},{10,... | collective-permute-start | bytes 835592 | tf_op jit(solution)/shard_map/ppermute | solution.py:546
  60.5 1.3 %collective-permute-start.26 = (f32[16,512]{1,0:T(8,128)S(1)}, f32[16,512]{1,0:T(8,128)S(1)}, u32[]{:S(2)}, u32[]{:S(2)}) collective-permute-start(f32[16,512]{1,0:T(8,128)S(1)} %get-tuple-element.293.refs_0_), channel_id=1, source_target_pairs={{0,1},{1,0},{2,3},{3,2},{4,5},{5,4},{6,7},{7,6},{8,9},{9,8},{10,11... | collective-permute-start | bytes 98312 | tf_op jit(solution)/shard_map/ppermute | solution.py:546
  60.6 12.9 %collective-permute-start.22 = (bf16[272,512]{1,0:T(8,128)(2,1)S(1)}, bf16[272,512]{1,0:T(8,128)(2,1)S(1)}, u32[]{:S(2)}, u32[]{:S(2)}) collective-permute-start(bf16[272,512]{1,0:T(8,128)(2,1)S(1)} %get-tuple-element.279), channel_id=1, source_target_pairs={{0,2},{1,3},{2,0},{3,1},{4,6},{5,7},{6,4},{7,5},{8,10},{9,11},{10,... | collective-permute-start | bytes 835592 | tf_op jit(solution)/shard_map/ppermute | solution.py:546
  68.2 7.8 %collective-permute-start.29 = (bf16[272,512]{1,0:T(8,128)(2,1)S(1)}, bf16[272,512]{1,0:T(8,128)(2,1)S(1)}, u32[]{:S(2)}, u32[]{:S(2)}) collective-permute-start(bf16[272,512]{1,0:T(8,128)(2,1)S(1)} %get-tuple-element.304), channel_id=1, source_target_pairs={{0,4},{1,5},{2,6},{3,7},{4,0},{5,1},{6,2},{7,3},{8,12},{9,13},{10,... | collective-permute-start | bytes 835592 | tf_op jit(solution)/shard_map/ppermute | solution.py:546
  70.3 5.1 %collective-permute-start.30 = (bf16[144,512]{1,0:T(8,128)(2,1)S(1)}, bf16[144,512]{1,0:T(8,128)(2,1)S(1)}, u32[]{:S(2)}, u32[]{:S(2)}) collective-permute-start(bf16[144,512]{1,0:T(8,128)(2,1)S(1)} %get-tuple-element.307), channel_id=1, source_target_pairs={{0,8},{1,9},{2,10},{3,11},{4,12},{5,13},{6,14},{7,15},{8,0},{9,1},... | collective-permute-start | bytes 442376 | tf_op jit(solution)/shard_map/ppermute | solution.py:546
  76.0 8.9 %collective-permute-start.31 = (bf16[144,512]{1,0:T(8,128)(2,1)S(1)}, bf16[144,512]{1,0:T(8,128)(2,1)S(1)}, u32[]{:S(2)}, u32[]{:S(2)}) collective-permute-start(bf16[144,512]{1,0:T(8,128)(2,1)S(1)} %get-tuple-element.311), channel_id=1, source_target_pairs={{0,8},{1,9},{2,10},{3,11},{4,12},{5,13},{6,14},{7,15},{8,0},{9,1},... | collective-permute-start | bytes 442376 | tf_op jit(solution)/shard_map/ppermute | solution.py:546
  77.8 10.2 %collective-permute-start.28 = (bf16[144,512]{1,0:T(8,128)(2,1)S(1)}, bf16[144,512]{1,0:T(8,128)(2,1)S(1)}, u32[]{:S(2)}, u32[]{:S(2)}) collective-permute-start(bf16[144,512]{1,0:T(8,128)(2,1)S(1)} %get-tuple-element.302), channel_id=1, source_target_pairs={{0,8},{1,9},{2,10},{3,11},{4,12},{5,13},{6,14},{7,15},{8,0},{9,1},... | collective-permute-start | bytes 442376 | tf_op jit(solution)/shard_map/ppermute | solution.py:546
  78.1 17.0 %collective-permute-start.33 = (bf16[144,512]{1,0:T(8,128)(2,1)S(1)}, bf16[144,512]{1,0:T(8,128)(2,1)S(1)}, u32[]{:S(2)}, u32[]{:S(2)}) collective-permute-start(bf16[144,512]{1,0:T(8,128)(2,1)S(1)} %get-tuple-element.322), channel_id=1, source_target_pairs={{0,16},{1,17},{2,18},{3,19},{4,20},{5,21},{6,22},{7,23},{8,24},{9,... | collective-permute-start | bytes 442376 | tf_op jit(solution)/shard_map/ppermute | solution.py:546
  84.9 12.9 %collective-permute-start.32 = (bf16[144,512]{1,0:T(8,128)(2,1)S(1)}, bf16[144,512]{1,0:T(8,128)(2,1)S(1)}, u32[]{:S(2)}, u32[]{:S(2)}) collective-permute-start(bf16[144,512]{1,0:T(8,128)(2,1)S(1)} %get-tuple-element.319), channel_id=1, source_target_pairs={{0,16},{1,17},{2,18},{3,19},{4,20},{5,21},{6,22},{7,23},{8,24},{9,... | collective-permute-start | bytes 442376 | tf_op jit(solution)/shard_map/ppermute | solution.py:546
  88.1 11.3 %collective-permute-start.36 = (bf16[144,512]{1,0:T(8,128)(2,1)S(1)}, bf16[144,512]{1,0:T(8,128)(2,1)S(1)}, u32[]{:S(2)}, u32[]{:S(2)}) collective-permute-start(bf16[144,512]{1,0:T(8,128)(2,1)S(1)} %get-tuple-element.328), channel_id=1, source_target_pairs={{0,16},{1,17},{2,18},{3,19},{4,20},{5,21},{6,22},{7,23},{8,24},{9,... | collective-permute-start | bytes 442376 | tf_op jit(solution)/shard_map/ppermute | solution.py:546
  95.1 5.0 %collective-permute-start.35 = (bf16[128,512]{1,0:T(8,128)(2,1)S(1)}, bf16[128,512]{1,0:T(8,128)(2,1)S(1)}, u32[]{:S(2)}, u32[]{:S(2)}) collective-permute-start(bf16[128,512]{1,0:T(8,128)(2,1)S(1)} %get-tuple-element.326.refs_0_), channel_id=1, source_target_pairs={{0,4},{1,5},{2,6},{3,7},{4,0},{5,1},{6,2},{7,3},{8,12},{9,13},{10,... | collective-permute-start | bytes 393224 | tf_op jit(solution)/shard_map/ppermute | solution.py:546
  97.8 6.5 %collective-permute-start.34 = (bf16[128,512]{1,0:T(8,128)(2,1)S(1)}, bf16[128,512]{1,0:T(8,128)(2,1)S(1)}, u32[]{:S(2)}, u32[]{:S(2)}) collective-permute-start(bf16[128,512]{1,0:T(8,128)(2,1)S(1)} %get-tuple-element.325.refs_0_), channel_id=1, source_target_pairs={{0,8},{1,9},{2,10},{3,11},{4,12},{5,13},{6,14},{7,15},{8,0},{9,1},... | collective-permute-start | bytes 393224 | tf_op jit(solution)/shard_map/ppermute | solution.py:546
  99.4 6.3 %collective-permute-start.40 = (bf16[128,512]{1,0:T(8,128)(2,1)S(1)}, bf16[128,512]{1,0:T(8,128)(2,1)S(1)}, u32[]{:S(2)}, u32[]{:S(2)}) collective-permute-start(bf16[128,512]{1,0:T(8,128)(2,1)S(1)} %get-tuple-element.335.refs_0_), channel_id=1, source_target_pairs={{0,4},{1,5},{2,6},{3,7},{4,0},{5,1},{6,2},{7,3},{8,12},{9,13},{10,... | collective-permute-start | bytes 393224 | tf_op jit(solution)/shard_map/ppermute | solution.py:546
  100.2 10.6 %collective-permute-start.38 = (bf16[256,512]{1,0:T(8,128)(2,1)S(1)}, bf16[256,512]{1,0:T(8,128)(2,1)S(1)}, u32[]{:S(2)}, u32[]{:S(2)}) collective-permute-start(bf16[256,512]{1,0:T(8,128)(2,1)S(1)} %get-tuple-element.333.refs_0_), channel_id=1, source_target_pairs={{0,8},{1,9},{2,10},{3,11},{4,12},{5,13},{6,14},{7,15},{8,0},{9,1},... | collective-permute-start | bytes 786440 | tf_op jit(solution)/shard_map/ppermute | solution.py:546
  104.4 7.8 %collective-permute-start.37 = (bf16[256,512]{1,0:T(8,128)(2,1)S(1)}, bf16[256,512]{1,0:T(8,128)(2,1)S(1)}, u32[]{:S(2)}, u32[]{:S(2)}) collective-permute-start(bf16[256,512]{1,0:T(8,128)(2,1)S(1)} %get-tuple-element.332.refs_0_), channel_id=1, source_target_pairs={{0,4},{1,5},{2,6},{3,7},{4,0},{5,1},{6,2},{7,3},{8,12},{9,13},{10,... | collective-permute-start | bytes 786440 | tf_op jit(solution)/shard_map/ppermute | solution.py:546
  105.7 7.6 %collective-permute-start.41 = (bf16[256,512]{1,0:T(8,128)(2,1)S(1)}, bf16[256,512]{1,0:T(8,128)(2,1)S(1)}, u32[]{:S(2)}, u32[]{:S(2)}) collective-permute-start(bf16[256,512]{1,0:T(8,128)(2,1)S(1)} %get-tuple-element.342.refs_0_), channel_id=1, source_target_pairs={{0,8},{1,9},{2,10},{3,11},{4,12},{5,13},{6,14},{7,15},{8,0},{9,1},... | collective-permute-start | bytes 786440 | tf_op jit(solution)/shard_map/ppermute | solution.py:546
  106.4 3.7 %collective-permute-start.39 = (f32[8,512]{1,0:T(8,128)S(1)}, f32[8,512]{1,0:T(8,128)S(1)}, u32[]{:S(2)}, u32[]{:S(2)}) collective-permute-start(f32[8,512]{1,0:T(8,128)S(1)} %get-tuple-element.334.refs_0_), channel_id=1, source_target_pairs={{0,2},{1,3},{2,0},{3,1},{4,6},{5,7},{6,4},{7,5},{8,10},{9,11},{10,... | collective-permute-start | bytes 49160 | tf_op jit(solution)/shard_map/ppermute | solution.py:546
  (12 other events, 10.0 us)

commit v4 on v3

--- a/solution.py
+++ b/solution.py
@@ -60,9 +60,6 @@
         )(*args, *also, self.token)
         self.token = got[-1]
         return got[:-1]
-
-    def wait(self, *arrays):
-        self.call(touch_kernel, [], *arrays, name="touch")
 
 
 def centred(rows):
@@ -209,10 +206,6 @@
         col += part.shape[1]
 
 
-def touch_kernel(*refs):
-    pass
-
-
 def relay_kernel(value, out):
     out[...] = value[...]
 
@@ -261,10 +254,8 @@
     ups, biases = take(slots), take(slots)
     acts, slopes, grads = take(slots), take(slots), take(slots)
     for j in range(slots):
-        span, deep = biases[j].shape[1], second.shape[1]
-        bias = jnp.concatenate(
-            [biases[j][deep + k : deep + k + 1, :] for k in range(ups[j].shape[1] // span)], 1
-        ).astype(F32)
+        span, tile = biases[j].shape[1], biases[j][second.shape[1] :, :].astype(F32)
+        bias = jnp.concatenate([tile[k : k + 1, :] for k in range(ups[j].shape[1] // span)], 1)
         for r in range(0, second.shape[0], 2 * CHUNK):
             at = slice(r, r + 2 * CHUNK)
             act, slope = gelu_parts(nn(second[at, :], ups[j][...]) + bias)
@@ -676,6 +667,8 @@
         self.got = self.links.swap(self.own, self.last * self.links.head)
 
     def double(self):
+        if not self.left:
+            return
         self.rows *= 2
         (self.own,) = self.kernels.call(
             functools.partial(join_kernel, self.last),
@@ -1111,21 +1104,21 @@
         unbundle()
         second()
         hidden_call([0, 1])
+        join_down()
         hidden_back_call([0, 1])
-        join_down()
+        down_sum.give_later(1, down_grads[1])
         relay_up()
-        down_sum.give_later(1, down_grads[1])
         up_sum.give_later(1, *up_grads[1])
+        down_sum.fold(0)
+        for k in odds:
+            hidden_call([k])
+        for k in odds:
+            hidden_back_call([k])
         for k in evens:
             hidden_call([k])
-        for k in odds:
-            hidden_call([k])
-        down_sum.fold(0)
         up_sum.fold(0)
+        heads(down_sum, True)
         for k in evens:
-            hidden_back_call([k])
-        heads(down_sum, True)
-        for k in odds:
             hidden_back_call([k])
         middle()
         for k in evens:
@@ -1138,16 +1131,16 @@
         heads(up_sum)
         down_sum.halve(bits[0])
         vector()
+        halves(down_sum)
         vector_core()
-        halves(down_sum)
         triple_sum.halve(bits[0])
         halves(up_sum)
+        halves(triple_sum)
         down_sum.whole(bits[-1])
-        halves(triple_sum)
         triple_sum.whole(bits[-1])
-        up_sum.whole(bits[-1])
         block()
         settle(down_sum, there)
+        up_sum.whole(bits[-1])
         settle_triple()
         settle(up_sum, there)
         down_sum.double()

time: 115 us -> 113 us (0.983)
  waiting for transfers between devices: 40.1 us -> 32.9 us
  starting transfers between devices: 32.6 us -> 37.5 us
    ppermute x42, waiting for transfers between devices: 40.1 us -> 32.9 us  [swap(): return lax.ppermute(value, AXES, [(i, i ^ bit) for i in range(total)])]
    ppermute x42, starting transfers between devices: 32.6 us -> 37.5 us  [swap(): return lax.ppermute(value, AXES, [(i, i ^ bit) for i in range(total)])]
  transfers between devices with their start and end apart: 42 -> 42, of which waited for: 20 -> 18; matrix products, arithmetic and copies ran while one was open for 0% -> 0% of each run, Pallas kernels for 28% -> 29%
where the time goes in v4:
time: 113 us; the launch traced here: 112 us
  starting transfers between devices  37.5 us (33%)
  Pallas kernels  34.3 us (30%)
  waiting for transfers between devices  32.9 us (29%)
  local copies, waits for them, and re-layouts  6.51 us (6%)
  between operations  1.14 us (1%)
    ppermute x42, starting transfers between devices, swap(): return lax.ppermute(value, AXES, [(i, i ^ bit) for i in range(total)])  37.5 us
    pallas_call x52, Pallas kernels, call(): pl.pallas_call(ordered, out_shape=[jax.ShapeDtypeStruct(*out[:2]) for out...  34.3 us
    ppermute x42, waiting for transfers between devices, swap(): return lax.ppermute(value, AXES, [(i, i ^ bit) for i in range(total)])  32.9 us
    unnamed x36, local copies, waits for them, and re-layouts  6.51 us
  transfers between devices with their start and end apart: 42, of which 18 were waited for; matrix products, arithmetic and copies ran while one was open for 0% of the time, Pallas kernels for 29%

profile of v4, /device:TPU:0, one launch (start us, length us, event | category | flops | bytes accessed | tf_op | source)
XLA Modules:
  0.0 112.4 jit_solution(11147285174077917998)
XLA Ops:
  1.7 2.6 %collective-permute-start.2 = (bf16[512,384]{1,0:T(8,128)(2,1)}, bf16[512,384]{1,0:T(8,128)(2,1)S(1)}, u32[]{:S(2)}, u32[]{:S(2)}) collective-permute-start(bf16[512,384]{1,0:T(8,128)(2,1)} %refs_4_.10), channel_id=1, source_target_pairs={{0,2},{1,3},{2,0},{3,1},{4,6},{5,7},{6,4},{7,5},{8,10},{9,11},{10,... | collective-permute-start | bytes 1179656 | tf_op jit(solution)/shard_map/ppermute | solution.py:537
  5.0 1.0 copy-done.3
  6.0 0.9 copy-done.7
  8.2 1.2 %copy-done = f32[512,512]{1,0:T(8,128)S(1)} copy-done((f32[512,512]{1,0:T(8,128)S(1)}, f32[512,512]{1,0:T(8,128)}, u32[]{:S(2)}) %copy-start) | copy-done | bytes 1048600
  10.4 2.5 %attend.3 = (bf16[512,384]{1,0:T(8,128)(2,1)S(1)}, bf16[512,384]{1,0:T(8,128)(2,1)S(1)}, f32[4,256,128]{2,1,0:T(8,128)S(1)}, f32[4,256,128]{2,1,0:T(8,128)S(1)},...) custom-call(bf16[512,512]{1,0:T(8,128)(2,1)S(1)} %get-tuple-element.184.refs_0_, ...), custom_call_target="tpu_custom_call" | custom-call | tf_op jit(solution)/shard_map/attend/pallas_call | solution.py:50
  13.6 0.9 collective-permute-done.2.refs_0_.refs_1_.refs_6_
  14.6 2.0 %collective-permute-start.8 = (bf16[512,512]{1,0:T(8,128)(2,1)S(1)}, bf16[512,512]{1,0:T(8,128)(2,1)S(1)}, u32[]{:S(2)}, u32[]{:S(2)}) collective-permute-start(bf16[512,512]{1,0:T(8,128)(2,1)S(1)} %copy-done.5), channel_id=1, source_target_pairs={{0,2},{1,3},{2,0},{3,1},{4,6},{5,7},{6,4},{7,5},{8,10},{9,11},{10,... | collective-permute-start | bytes 1572872 | tf_op jit(solution)/shard_map/ppermute | solution.py:537
  16.6 1.6 %attend.4 = (bf16[512,384]{1,0:T(8,128)(2,1)S(1)}, f32[4,256,128]{2,1,0:T(8,128)S(1)}, bf16[512,128]{1,0:T(8,128)(2,1)S(1)}, f32[8,128]{1,0:T(8,128)S(1)}) custom-call(bf16[512,512]{1,0:T(8,128)(2,1)S(1)} %get-tuple-element.184.refs_0_, bf16[512,384]{1,0:T(8,128)(2,1)S(1)} %collective-permute-done.2.refs_0_.refs_1_.refs_6_, ...), custom_call_target="tpu_custom_call" | custom-call | tf_op jit(solution)/shard_map/attend/pallas_call | solution.py:50
  18.3 1.6 %attend.5 = (bf16[512,384]{1,0:T(8,128)(2,1)S(1)}, f32[4,256,128]{2,1,0:T(8,128)S(1)}, bf16[512,128]{1,0:T(8,128)(2,1)S(1)}, f32[8,128]{1,0:T(8,128)S(1)}) custom-call(bf16[512,512]{1,0:T(8,128)(2,1)S(1)} %get-tuple-element.184.refs_0_, bf16[512,384]{1,0:T(8,128)(2,1)S(1)} %collective-permute-done.5.refs_1_.refs_7_, s32[1]{0:T(128)} %bitcast.3.refs_4_.refs_3_.refs_2_, ...), custom_call_target="tpu_custom_call" | custom-call | tf_op jit(solution)/shard_map/attend/pallas_call | solution.py:50
  19.9 3.1 %collective-permute-done.6.refs_0_ = bf16[1552,128]{1,0:T(8,128)(2,1)S(1)} collective-permute-done((bf16[1552,128]{1,0:T(8,128)(2,1)S(1)}, bf16[1552,128]{1,0:T(8,128)(2,1)S(1)}, u32[]{:S(2)}, u32[]{:S(2)}) %collective-permute-start.6) | collective-permute-done | bytes 397344 | tf_op jit(solution)/shard_map/ppermute | solution.py:537
  23.0 2.0 %collective-permute-start.9 = (bf16[256,512]{1,0:T(8,128)(2,1)S(1)}, bf16[256,512]{1,0:T(8,128)(2,1)S(1)}, u32[]{:S(2)}, u32[]{:S(2)}) collective-permute-start(bf16[256,512]{1,0:T(8,128)(2,1)S(1)} %get-tuple-element.212.refs_0_), channel_id=1, source_target_pairs={{0,4},{1,5},{2,6},{3,7},{4,0},{5,1},{6,2},{7,3},{8,12},{9,13},{10,... | collective-permute-start | bytes 786440 | tf_op jit(solution)/shard_map/ppermute | solution.py:537
  25.0 1.4 %collective-permute-done.7.refs_3_ = bf16[528,128]{1,0:T(8,128)(2,1)S(1)} collective-permute-done((bf16[528,128]{1,0:T(8,128)(2,1)S(1)}, bf16[528,128]{1,0:T(8,128)(2,1)S(1)}, u32[]{:S(2)}, u32[]{:S(2)}) %collective-permute-start.7) | collective-permute-done | bytes 135200 | tf_op jit(solution)/shard_map/ppermute | solution.py:537
  27.1 0.8 second.1
  27.9 2.2 %hidden.3 = (bf16[512,512]{1,0:T(8,128)(2,1)S(1)}, bf16[512,512]{1,0:T(8,128)(2,1)S(1)}, f32[512,512]{1,0:T(8,128)S(1)}, f32[512,512]{1,0:T(8,128)S(1)}, f32[512...) custom-call(bf16[512,512]{1,0:T(8,128)(2,1)S(1)} %get-tuple-element.202.refs_0_, ...), custom_call_target="tpu_custom_call" | custom-call | tf_op jit(solution)/shard_map/hidden/pallas_call | solution.py:50
  31.1 1.8 %hidden_back.3 = (f32[512,512]{1,0:T(8,128)S(1)}, bf16[512,512]{1,0:T(8,128)(2,1)S(1)}, f32[1,512]{1,0:T(1,128)S(1)}, f32[1,512]{1,0:T(1,128)S(1)}, f32[512,512]{1,0:T(8,128)S(1)}, /*index=5*/f32[8,128]{1,0:T(8,128)S(1)}) custom-call(bf16[512,512]{1,0:T(8,128)(2,1)S(1)} %get-tuple-element.207.refs_0_, bf16[512,512]{1,0:T(8,128)(2,1)S(1)} %get-tuple-element.208.refs_1_, ...), custom_call_target="tpu_custom_call" | custom-call | tf_op jit(solution)/shard_map/hidden_back/pallas_call | solution.py:50
  35.1 0.9 collective-permute-done.10.refs_2_
  36.0 1.2 %hidden.4 = (bf16[512,512]{1,0:T(8,128)(2,1)S(1)}, f32[512,512]{1,0:T(8,128)S(1)}, bf16[512,512]{1,0:T(8,128)(2,1)S(1)}, f32[8,128]{1,0:T(8,128)S(1)}) custom-call(bf16[512,512]{1,0:T(8,128)(2,1)S(1)} %get-tuple-element.202.refs_0_, bf16[512,512]{1,0:T(8,128)(2,1)S(1)} %get-tuple-element.203.refs_1_, bf16[512,512]{1,0:T(8,128)(2,1)S(1)} %collective-permute-done.10.refs_2_, ...), custom_call_target="tpu_custom_call" | custom-call | tf_op jit(solution)/shard_map/hidden/pallas_call | solution.py:50
  37.3 1.0 hidden_back.4
  39.3 1.2 %hidden.5 = (bf16[512,512]{1,0:T(8,128)(2,1)S(1)}, f32[512,512]{1,0:T(8,128)S(1)}, f32[512,512]{1,0:T(8,128)S(1)}, f32[8,128]{1,0:T(8,128)S(1)}) custom-call(bf16[512,512]{1,0:T(8,128)(2,1)S(1)} %get-tuple-element.202.refs_0_, bf16[512,512]{1,0:T(8,128)(2,1)S(1)} %get-tuple-element.203.refs_1_, bf16[512,512]{1,0:T(8,128)(2,1)S(1)} %collective-permute-done.8.refs_0_.refs_2_, ...), custom_call_target="tpu_custom_call" | custom-call | tf_op jit(solution)/shard_map/hidden/pallas_call | solution.py:50
  40.8 1.8 %collective-permute-start.23 = (bf16[528,512]{1,0:T(8,128)(2,1)S(1)}, bf16[528,512]{1,0:T(8,128)(2,1)S(1)}, u32[]{:S(2)}, u32[]{:S(2)}) collective-permute-start(bf16[528,512]{1,0:T(8,128)(2,1)S(1)} %get-tuple-element.285), channel_id=1, source_target_pairs={{0,2},{1,3},{2,0},{3,1},{4,6},{5,7},{6,4},{7,5},{8,10},{9,11},{10,... | collective-permute-start | bytes 1622024 | tf_op jit(solution)/shard_map/ppermute | solution.py:537
  42.6 1.0 hidden_back.5
  43.6 1.1 middle.1
  45.0 1.6 %collective-permute-start.24 = (bf16[512,512]{1,0:T(8,128)(2,1)S(1)}, bf16[512,512]{1,0:T(8,128)(2,1)S(1)}, u32[]{:S(2)}, u32[]{:S(2)}) collective-permute-start(bf16[512,512]{1,0:T(8,128)(2,1)S(1)} %get-tuple-element.287), channel_id=1, source_target_pairs={{0,4},{1,5},{2,6},{3,7},{4,0},{5,1},{6,2},{7,3},{8,12},{9,13},{10,... | collective-permute-start | bytes 1572872 | tf_op jit(solution)/shard_map/ppermute | solution.py:537
  46.6 2.6 %attend_back.2 = (bf16[512,384]{1,0:T(8,128)(2,1)S(1)}, bf16[512,384]{1,0:T(8,128)(2,1)S(1)}, bf16[176,512]{1,0:T(8,128)(2,1)S(1)}, bf16[176,512]{1,0:T(8,128)(2...) custom-call(bf16[512,512]{1,0:T(8,128)(2,1)S(1)} %get-tuple-element.243.refs_0_, ...), custom_call_target="tpu_custom_call" | custom-call | tf_op jit(solution)/shard_map/attend_back/pallas_call | solution.py:50
  49.9 2.6 %attend_back.3 = (bf16[512,384]{1,0:T(8,128)(2,1)S(1)}, bf16[512,384]{1,0:T(8,128)(2,1)S(1)}, bf16[512,512]{1,0:T(8,128)(2,1)S(1)}, f32[512,512]{1,0:T(8,128)S(1)}, f32[8,128]{1,0:T(8,128)S(1)}) custom-call(bf16[512,512]{1,0:T(8,128)(2,1)S(1)} %get-tuple-element.243.refs_0_, bf16[512,512]{1,0:T(8,128)(2,1)S(1)} %get-tuple-element.244.refs_1_, ...), custom_call_target="tpu_custom_call" | custom-call | tf_op jit(solution)/shard_map/attend_back/pallas_call | solution.py:50
  53.7 3.3 %input.1 = (f32[512,512]{1,0:T(8,128)}, f32[8,512]{1,0:T(8,128)S(1)}, f32[8,128]{1,0:T(8,128)S(1)}) custom-call(bf16[512,384]{1,0:T(8,128)(2,1)S(1)} %get-tuple-element.273.refs_0_, bf16[512,384]{1,0:T(8,128)(2,1)S(1)} %get-tuple-element.274.refs_1_, bf16[512,384]{1,0:T(8,128)(2,1)S(1)} %get-tuple-element.275.refs_2_, ...), custom_call_target="tpu_custom_call" | custom-call | tf_op jit(solution)/shard_map/input/pallas_call | solution.py:50
  57.0 1.8 %collective-permute-done.24.refs_1_ = bf16[512,512]{1,0:T(8,128)(2,1)S(1)} collective-permute-done((bf16[512,512]{1,0:T(8,128)(2,1)S(1)}, bf16[512,512]{1,0:T(8,128)(2,1)S(1)}, u32[]{:S(2)}, u32[]{:S(2)}) %collective-permute-start.24) | collective-permute-done | bytes 524320 | tf_op jit(solution)/shard_map/ppermute | solution.py:537
  59.0 1.6 %collective-permute-start.26 = (bf16[272,512]{1,0:T(8,128)(2,1)S(1)}, bf16[272,512]{1,0:T(8,128)(2,1)S(1)}, u32[]{:S(2)}, u32[]{:S(2)}) collective-permute-start(bf16[272,512]{1,0:T(8,128)(2,1)S(1)} %get-tuple-element.293), channel_id=1, source_target_pairs={{0,4},{1,5},{2,6},{3,7},{4,0},{5,1},{6,2},{7,3},{8,12},{9,13},{10,... | collective-permute-start | bytes 835592 | tf_op jit(solution)/shard_map/ppermute | solution.py:537
  61.2 5.5 %collective-permute-done.26.refs_1_ = bf16[272,512]{1,0:T(8,128)(2,1)S(1)} collective-permute-done((bf16[272,512]{1,0:T(8,128)(2,1)S(1)}, bf16[272,512]{1,0:T(8,128)(2,1)S(1)}, u32[]{:S(2)}, u32[]{:S(2)}) %collective-permute-start.26) | collective-permute-done | bytes 278560 | tf_op jit(solution)/shard_map/ppermute | solution.py:537
  66.8 1.2 %collective-permute-done.22.refs_2_ = bf16[512,512]{1,0:T(8,128)(2,1)S(1)} collective-permute-done((bf16[512,512]{1,0:T(8,128)(2,1)S(1)}, bf16[512,512]{1,0:T(8,128)(2,1)S(1)}, u32[]{:S(2)}, u32[]{:S(2)}) %collective-permute-start.22) | collective-permute-done | bytes 524320 | tf_op jit(solution)/shard_map/ppermute | solution.py:537
  68.9 1.6 %collective-permute-start.30 = (bf16[144,512]{1,0:T(8,128)(2,1)S(1)}, bf16[144,512]{1,0:T(8,128)(2,1)S(1)}, u32[]{:S(2)}, u32[]{:S(2)}) collective-permute-start(bf16[144,512]{1,0:T(8,128)(2,1)S(1)} %get-tuple-element.309), channel_id=1, source_target_pairs={{0,8},{1,9},{2,10},{3,11},{4,12},{5,13},{6,14},{7,15},{8,0},{9,1},... | collective-permute-start | bytes 442376 | tf_op jit(solution)/shard_map/ppermute | solution.py:537
  70.5 2.6 %collective-permute-done.28.refs_2_ = bf16[272,512]{1,0:T(8,128)(2,1)S(1)} collective-permute-done((bf16[272,512]{1,0:T(8,128)(2,1)S(1)}, bf16[272,512]{1,0:T(8,128)(2,1)S(1)}, u32[]{:S(2)}, u32[]{:S(2)}) %collective-permute-start.28) | collective-permute-done | bytes 278560 | tf_op jit(solution)/shard_map/ppermute | solution.py:537
  73.2 2.0 %collective-permute-done.27.refs_1_ = bf16[272,512]{1,0:T(8,128)(2,1)S(1)} collective-permute-done((bf16[272,512]{1,0:T(8,128)(2,1)S(1)}, bf16[272,512]{1,0:T(8,128)(2,1)S(1)}, u32[]{:S(2)}, u32[]{:S(2)}) %collective-permute-start.27) | collective-permute-done | bytes 278560 | tf_op jit(solution)/shard_map/ppermute | solution.py:537
  75.2 1.6 %collective-permute-start.29 = (bf16[144,512]{1,0:T(8,128)(2,1)S(1)}, bf16[144,512]{1,0:T(8,128)(2,1)S(1)}, u32[]{:S(2)}, u32[]{:S(2)}) collective-permute-start(bf16[144,512]{1,0:T(8,128)(2,1)S(1)} %get-tuple-element.306), channel_id=1, source_target_pairs={{0,8},{1,9},{2,10},{3,11},{4,12},{5,13},{6,14},{7,15},{8,0},{9,1},... | collective-permute-start | bytes 442376 | tf_op jit(solution)/shard_map/ppermute | solution.py:537
  76.9 2.7 %collective-permute-start.33 = (bf16[144,512]{1,0:T(8,128)(2,1)S(1)}, bf16[144,512]{1,0:T(8,128)(2,1)S(1)}, u32[]{:S(2)}, u32[]{:S(2)}) collective-permute-start(bf16[144,512]{1,0:T(8,128)(2,1)S(1)} %get-tuple-element.321), channel_id=1, source_target_pairs={{0,16},{1,17},{2,18},{3,19},{4,20},{5,21},{6,22},{7,23},{8,24},{9,... | collective-permute-start | bytes 442376 | tf_op jit(solution)/shard_map/ppermute | solution.py:537
  80.0 5.3 %collective-permute-done.29.refs_1_ = bf16[144,512]{1,0:T(8,128)(2,1)S(1)} collective-permute-done((bf16[144,512]{1,0:T(8,128)(2,1)S(1)}, bf16[144,512]{1,0:T(8,128)(2,1)S(1)}, u32[]{:S(2)}, u32[]{:S(2)}) %collective-permute-start.29) | collective-permute-done | bytes 147488 | tf_op jit(solution)/shard_map/ppermute | solution.py:537
  86.2 2.2 %output.1 = (f32[512,512]{1,0:T(8,128)}, f32[8,128]{1,0:T(8,128)S(1)}) custom-call(bf16[512,512]{1,0:T(8,128)(2,1)S(1)} %get-tuple-element.205.refs_0_, bf16[512,512]{1,0:T(8,128)(2,1)S(1)} %get-tuple-element.206.refs_1_, bf16[512,512]{1,0:T(8,128)(2,1)S(1)} %get-tuple-element.229.refs_2_, bf16[512,512]{1,0:T(8,128)(2,1)S(1)} %get-tuple-element.230.refs_3_, ...), custom_call_target="tpu_custom_call" | custom-call | tf_op jit(solution)/shard_map/output/pallas_call | solution.py:50
  88.5 3.0 %collective-permute-start.36 = (bf16[144,512]{1,0:T(8,128)(2,1)S(1)}, bf16[144,512]{1,0:T(8,128)(2,1)S(1)}, u32[]{:S(2)}, u32[]{:S(2)}) collective-permute-start(bf16[144,512]{1,0:T(8,128)(2,1)S(1)} %get-tuple-element.328), channel_id=1, source_target_pairs={{0,16},{1,17},{2,18},{3,19},{4,20},{5,21},{6,22},{7,23},{8,24},{9,... | collective-permute-start | bytes 442376 | tf_op jit(solution)/shard_map/ppermute | solution.py:537
  91.4 2.1 %collective-permute-start.35 = (bf16[128,512]{1,0:T(8,128)(2,1)S(1)}, bf16[128,512]{1,0:T(8,128)(2,1)S(1)}, u32[]{:S(2)}, u32[]{:S(2)}) collective-permute-start(bf16[128,512]{1,0:T(8,128)(2,1)S(1)} %get-tuple-element.326.refs_0_), channel_id=1, source_target_pairs={{0,4},{1,5},{2,6},{3,7},{4,0},{5,1},{6,2},{7,3},{8,12},{9,13},{10,... | collective-permute-start | bytes 393224 | tf_op jit(solution)/shard_map/ppermute | solution.py:537
  93.5 1.4 %collective-permute-done.31.refs_1_ = bf16[144,512]{1,0:T(8,128)(2,1)S(1)} collective-permute-done((bf16[144,512]{1,0:T(8,128)(2,1)S(1)}, bf16[144,512]{1,0:T(8,128)(2,1)S(1)}, u32[]{:S(2)}, u32[]{:S(2)}) %collective-permute-start.31) | collective-permute-done | bytes 147488 | tf_op jit(solution)/shard_map/ppermute | solution.py:537
  95.0 3.0 %collective-permute-done.36.refs_1_ = bf16[144,512]{1,0:T(8,128)(2,1)S(1)} collective-permute-done((bf16[144,512]{1,0:T(8,128)(2,1)S(1)}, bf16[144,512]{1,0:T(8,128)(2,1)S(1)}, u32[]{:S(2)}, u32[]{:S(2)}) %collective-permute-start.36) | collective-permute-done | bytes 147488 | tf_op jit(solution)/shard_map/ppermute | solution.py:537
  98.1 2.3 %collective-permute-start.40 = (bf16[128,512]{1,0:T(8,128)(2,1)S(1)}, bf16[128,512]{1,0:T(8,128)(2,1)S(1)}, u32[]{:S(2)}, u32[]{:S(2)}) collective-permute-start(bf16[128,512]{1,0:T(8,128)(2,1)S(1)} %get-tuple-element.335.refs_0_), channel_id=1, source_target_pairs={{0,4},{1,5},{2,6},{3,7},{4,0},{5,1},{6,2},{7,3},{8,12},{9,13},{10,... | collective-permute-start | bytes 393224 | tf_op jit(solution)/shard_map/ppermute | solution.py:537
  100.6 3.1 %collective-permute-start.37 = (bf16[256,512]{1,0:T(8,128)(2,1)S(1)}, bf16[256,512]{1,0:T(8,128)(2,1)S(1)}, u32[]{:S(2)}, u32[]{:S(2)}) collective-permute-start(bf16[256,512]{1,0:T(8,128)(2,1)S(1)} %get-tuple-element.332.refs_0_), channel_id=1, source_target_pairs={{0,4},{1,5},{2,6},{3,7},{4,0},{5,1},{6,2},{7,3},{8,12},{9,13},{10,... | collective-permute-start | bytes 786440 | tf_op jit(solution)/shard_map/ppermute | solution.py:537
  104.1 2.0 %collective-permute-start.39 = (f32[8,512]{1,0:T(8,128)S(1)}, f32[8,512]{1,0:T(8,128)S(1)}, u32[]{:S(2)}, u32[]{:S(2)}) collective-permute-start(f32[8,512]{1,0:T(8,128)S(1)} %get-tuple-element.334.refs_0_), channel_id=1, source_target_pairs={{0,2},{1,3},{2,0},{3,1},{4,6},{5,7},{6,4},{7,5},{8,10},{9,11},{10,... | collective-permute-start | bytes 49160 | tf_op jit(solution)/shard_map/ppermute | solution.py:537
  106.1 1.8 %collective-permute-done.39.refs_1_ = f32[8,512]{1,0:T(8,128)S(1)} collective-permute-done((f32[8,512]{1,0:T(8,128)S(1)}, f32[8,512]{1,0:T(8,128)S(1)}, u32[]{:S(2)}, u32[]{:S(2)}) %collective-permute-start.39) | collective-permute-done | bytes 16416 | tf_op jit(solution)/shard_map/ppermute | solution.py:537
  108.5 1.4 %finish_d.1 = (f32[512,512]{1,0:T(8,128)}, f32[8,128]{1,0:T(8,128)S(1)}) custom-call(bf16[256,512]{1,0:T(8,128)(2,1)S(1)} %get-tuple-element.333.refs_0_, bf16[256,512]{1,0:T(8,128)(2,1)S(1)} %collective-permute-done.38.refs_1_, s32[1]{0:T(128)} %bitcast.2.refs_3_.refs_2_.refs_4_, f32[8,128]{1,0:T(8,128)S(1)} %get-tuple-element.338.refs_3_), custom_call_target="tpu_custom_call" | custom-call | tf_op jit(solution)/shard_map/finish_d/pallas_call | solution.py:50
  109.9 1.2 %finish_t.1 = (f32[512,384]{1,0:T(8,128)}, f32[128,512]{1,0:T(8,128)}, f32[8,128]{1,0:T(8,128)S(1)}) custom-call(bf16[256,512]{1,0:T(8,128)(2,1)S(1)} %get-tuple-element.332.refs_0_, bf16[256,512]{1,0:T(8,128)(2,1)S(1)} %collective-permute-done.37.refs_1_, s32[1]{0:T(128)} %bitcast.2.refs_3_.refs_2_.refs_4_, f32[8,128]{1,0:T(8,128)S(1)} %get-tuple-element.339.refs_3_), custom_call_target="tpu_custom_call" | custom-call | tf_op jit(solution)/shard_map/finish_t/pallas_call | solution.py:50
  111.2 1.1 %finish_u.1 = (f32[512,512]{1,0:T(8,128)}, f32[8,128]{1,0:T(8,128)}) custom-call(bf16[256,512]{1,0:T(8,128)(2,1)S(1)} %get-tuple-element.342.refs_0_, bf16[256,512]{1,0:T(8,128)(2,1)S(1)} %collective-permute-done.41.refs_1_, s32[1]{0:T(128)} %bitcast.2.refs_3_.refs_2_.refs_4_, f32[8,128]{1,0:T(8,128)S(1)} %get-tuple-element.343.refs_3_), custom_call_target="tpu_custom_call" | custom-call | tf_op jit(solution)/shard_map/finish_u/pallas_call | solution.py:50
  (126 shorter events, 17.0 us)
Async XLA Ops:
  0.6 6.6 %collective-permute-start = (bf16[512,512]{1,0:T(8,128)(2,1)}, bf16[512,512]{1,0:T(8,128)(2,1)S(1)}, u32[]{:S(2)}, u32[]{:S(2)}) collective-permute-start(bf16[512,512]{1,0:T(8,128)(2,1)} %refs_2_.5), channel_id=1, source_target_pairs={{0,1},{1,0},{2,3},{3,2},{4,5},{5,4},{6,7},{7,6},{8,9},{9,8},{10,11... | collective-permute-start | bytes 1572872 | tf_op jit(solution)/shard_map/ppermute | solution.py:537
  1.2 6.4 %collective-permute-start.1 = (bf16[512,512]{1,0:T(8,128)(2,1)}, bf16[512,512]{1,0:T(8,128)(2,1)S(1)}, u32[]{:S(2)}, u32[]{:S(2)}) collective-permute-start(bf16[512,512]{1,0:T(8,128)(2,1)} %refs_4_.11), channel_id=1, source_target_pairs={{0,1},{1,0},{2,3},{3,2},{4,5},{5,4},{6,7},{7,6},{8,9},{9,8},{10,11... | collective-permute-start | bytes 1572872 | tf_op jit(solution)/shard_map/ppermute | solution.py:537
  1.2 8.8 %collective-permute-start.3 = (bf16[512,384]{1,0:T(8,128)(2,1)}, bf16[512,384]{1,0:T(8,128)(2,1)S(1)}, u32[]{:S(2)}, u32[]{:S(2)}) collective-permute-start(bf16[512,384]{1,0:T(8,128)(2,1)} %refs_4_.10), channel_id=1, source_target_pairs={{0,1},{1,0},{2,3},{3,2},{4,5},{5,4},{6,7},{7,6},{8,9},{9,8},{10,11... | collective-permute-start | bytes 1179656 | tf_op jit(solution)/shard_map/ppermute | solution.py:537
  1.7 12.8 %collective-permute-start.2 = (bf16[512,384]{1,0:T(8,128)(2,1)}, bf16[512,384]{1,0:T(8,128)(2,1)S(1)}, u32[]{:S(2)}, u32[]{:S(2)}) collective-permute-start(bf16[512,384]{1,0:T(8,128)(2,1)} %refs_4_.10), channel_id=1, source_target_pairs={{0,2},{1,3},{2,0},{3,1},{4,6},{5,7},{6,4},{7,5},{8,10},{9,11},{10,... | collective-permute-start | bytes 1179656 | tf_op jit(solution)/shard_map/ppermute | solution.py:537
  7.0 6.1 %collective-permute-start.4 = (bf16[528,128]{1,0:T(8,128)(2,1)S(1)}, bf16[528,128]{1,0:T(8,128)(2,1)S(1)}, u32[]{:S(2)}, u32[]{:S(2)}) collective-permute-start(bf16[528,128]{1,0:T(8,128)(2,1)S(1)} %get-tuple-element.188.refs_2_.refs_4_), channel_id=1, source_target_pairs={{0,1},{1,0},{2,3},{3,2},{4,5},{5,4},{6,7},{7,6},{8,9},{9,8},{10,11... | collective-permute-start | bytes 405512 | tf_op jit(solution)/shard_map/ppermute | solution.py:537
  7.2 15.7 %collective-permute-start.6 = (bf16[1552,128]{1,0:T(8,128)(2,1)S(1)}, bf16[1552,128]{1,0:T(8,128)(2,1)S(1)}, u32[]{:S(2)}, u32[]{:S(2)}) collective-permute-start(bf16[1552,128]{1,0:T(8,128)(2,1)S(1)} %get-tuple-element.197), channel_id=1, source_target_pairs={{0,2},{1,3},{2,0},{3,1},{4,6},{5,7},{6,4},{7,5},{8,10},{9,11},{10,... | collective-permute-start | bytes 1191944 | tf_op jit(solution)/shard_map/ppermute | solution.py:537
  8.2 1.2 %copy-start = (f32[512,512]{1,0:T(8,128)S(1)}, f32[512,512]{1,0:T(8,128)}, u32[]{:S(2)}) copy-start(f32[512,512]{1,0:T(8,128)} %refs_8_.1) | copy-start | bytes 3145732
  10.0 2.9 %copy-start.2 = (f32[512,512]{1,0:T(8,128)S(1)}, f32[512,512]{1,0:T(8,128)}, u32[]{:S(2)}) copy-start(f32[512,512]{1,0:T(8,128)} %refs_11_.1) | copy-start | bytes 3145732
  13.1 1.4 %copy-start.5 = (bf16[512,512]{1,0:T(8,128)(2,1)S(1)}, bf16[512,512]{1,0:T(8,128)(2,1)}, u32[]{:S(2)}) copy-start(bf16[512,512]{1,0:T(8,128)(2,1)} %refs_2_.5) | copy-start | bytes 1572868
  14.5 3.8 %collective-permute-start.5 = (bf16[512,384]{1,0:T(8,128)(2,1)S(1)}, bf16[512,384]{1,0:T(8,128)(2,1)S(1)}, u32[]{:S(2)}, u32[]{:S(2)}) collective-permute-start(bf16[512,384]{1,0:T(8,128)(2,1)S(1)} %get-tuple-element.194), channel_id=1, source_target_pairs={{0,1},{1,0},{2,3},{3,2},{4,5},{5,4},{6,7},{7,6},{8,9},{9,8},{10,11... | collective-permute-start | bytes 1179656 | tf_op jit(solution)/shard_map/ppermute | solution.py:537
  14.6 19.4 %collective-permute-start.8 = (bf16[512,512]{1,0:T(8,128)(2,1)S(1)}, bf16[512,512]{1,0:T(8,128)(2,1)S(1)}, u32[]{:S(2)}, u32[]{:S(2)}) collective-permute-start(bf16[512,512]{1,0:T(8,128)(2,1)S(1)} %copy-done.5), channel_id=1, source_target_pairs={{0,2},{1,3},{2,0},{3,1},{4,6},{5,7},{6,4},{7,5},{8,10},{9,11},{10,... | collective-permute-start | bytes 1572872 | tf_op jit(solution)/shard_map/ppermute | solution.py:537
  16.6 9.8 %copy-start.1 = (f32[512,512]{1,0:T(8,128)S(1)}, f32[512,512]{1,0:T(8,128)}, u32[]{:S(2)}) copy-start(f32[512,512]{1,0:T(8,128)} %refs_8_.1) | copy-start | bytes 3145732
  23.0 3.4 %copy-start.16 = (f32[512]{0:T(512)S(1)}, f32[512]{0:T(512)}, u32[]{:S(2)}) copy-start(f32[512]{0:T(512)} %param.28) | copy-start | bytes 6148
  23.0 7.9 %collective-permute-start.9 = (bf16[256,512]{1,0:T(8,128)(2,1)S(1)}, bf16[256,512]{1,0:T(8,128)(2,1)S(1)}, u32[]{:S(2)}, u32[]{:S(2)}) collective-permute-start(bf16[256,512]{1,0:T(8,128)(2,1)S(1)} %get-tuple-element.212.refs_0_), channel_id=1, source_target_pairs={{0,4},{1,5},{2,6},{3,7},{4,0},{5,1},{6,2},{7,3},{8,12},{9,13},{10,... | collective-permute-start | bytes 786440 | tf_op jit(solution)/shard_map/ppermute | solution.py:537
  25.0 1.4 %collective-permute-start.7 = (bf16[528,128]{1,0:T(8,128)(2,1)S(1)}, bf16[528,128]{1,0:T(8,128)(2,1)S(1)}, u32[]{:S(2)}, u32[]{:S(2)}) collective-permute-start(bf16[528,128]{1,0:T(8,128)(2,1)S(1)} %get-tuple-element.199.refs_2_.refs_3_.refs_4_), channel_id=1, source_target_pairs={{0,1},{1,0},{2,3},{3,2},{4,5},{5,4},{6,7},{7,6},{8,9},{9,8},{10,11... | collective-permute-start | bytes 405512 | tf_op jit(solution)/shard_map/ppermute | solution.py:537
  30.1 1.0 copy-start.4
  33.0 2.0 %collective-permute-start.12 = (bf16[512,512]{1,0:T(8,128)(2,1)S(1)}, bf16[512,512]{1,0:T(8,128)(2,1)S(1)}, u32[]{:S(2)}, u32[]{:S(2)}) collective-permute-start(bf16[512,512]{1,0:T(8,128)(2,1)S(1)} %get-tuple-element.219), channel_id=1, source_target_pairs={{0,1},{1,0},{2,3},{3,2},{4,5},{5,4},{6,7},{7,6},{8,9},{9,8},{10,11... | collective-permute-start | bytes 1572872 | tf_op jit(solution)/shard_map/ppermute | solution.py:537
  34.0 2.0 %collective-permute-start.10 = (bf16[512,512]{1,0:T(8,128)(2,1)S(1)}, bf16[512,512]{1,0:T(8,128)(2,1)S(1)}, u32[]{:S(2)}, u32[]{:S(2)}) collective-permute-start(bf16[512,512]{1,0:T(8,128)(2,1)S(1)} %get-tuple-element.217), channel_id=1, source_target_pairs={{0,1},{1,0},{2,3},{3,2},{4,5},{5,4},{6,7},{7,6},{8,9},{9,8},{10,11... | collective-permute-start | bytes 1572872 | tf_op jit(solution)/shard_map/ppermute | solution.py:537
  34.1 3.3 %collective-permute-start.11 = (bf16[512,512]{1,0:T(8,128)(2,1)S(1)}, bf16[512,512]{1,0:T(8,128)(2,1)S(1)}, u32[]{:S(2)}, u32[]{:S(2)}) collective-permute-start(bf16[512,512]{1,0:T(8,128)(2,1)S(1)} %get-tuple-element.218.refs_3_.refs_6_), channel_id=1, source_target_pairs={{0,1},{1,0},{2,3},{3,2},{4,5},{5,4},{6,7},{7,6},{8,9},{9,8},{10,11... | collective-permute-start | bytes 1572872 | tf_op jit(solution)/shard_map/ppermute | solution.py:537
  34.6 5.9 %collective-permute-start.14 = (bf16[512,512]{1,0:T(8,128)(2,1)S(1)}, bf16[512,512]{1,0:T(8,128)(2,1)S(1)}, u32[]{:S(2)}, u32[]{:S(2)}) collective-permute-start(bf16[512,512]{1,0:T(8,128)(2,1)S(1)} %get-tuple-element.236), channel_id=1, source_target_pairs={{0,1},{1,0},{2,3},{3,2},{4,5},{5,4},{6,7},{7,6},{8,9},{9,8},{10,11... | collective-permute-start | bytes 1572872 | tf_op jit(solution)/shard_map/ppermute | solution.py:537
  37.1 3.6 %collective-permute-start.13 = (bf16[512,512]{1,0:T(8,128)(2,1)S(1)}, bf16[512,512]{1,0:T(8,128)(2,1)S(1)}, u32[]{:S(2)}, u32[]{:S(2)}) collective-permute-start(bf16[512,512]{1,0:T(8,128)(2,1)S(1)} %get-tuple-element.235), channel_id=1, source_target_pairs={{0,1},{1,0},{2,3},{3,2},{4,5},{5,4},{6,7},{7,6},{8,9},{9,8},{10,11... | collective-permute-start | bytes 1572872 | tf_op jit(solution)/shard_map/ppermute | solution.py:537
  38.4 6.4 %collective-permute-start.15 = (bf16[176,512]{1,0:T(8,128)(2,1)S(1)}, bf16[176,512]{1,0:T(8,128)(2,1)S(1)}, u32[]{:S(2)}, u32[]{:S(2)}) collective-permute-start(bf16[176,512]{1,0:T(8,128)(2,1)S(1)} %get-tuple-element.256), channel_id=1, source_target_pairs={{0,1},{1,0},{2,3},{3,2},{4,5},{5,4},{6,7},{7,6},{8,9},{9,8},{10,11... | collective-permute-start | bytes 540680 | tf_op jit(solution)/shard_map/ppermute | solution.py:537
  38.8 6.0 %collective-permute-start.16 = (bf16[176,512]{1,0:T(8,128)(2,1)S(1)}, bf16[176,512]{1,0:T(8,128)(2,1)S(1)}, u32[]{:S(2)}, u32[]{:S(2)}) collective-permute-start(bf16[176,512]{1,0:T(8,128)(2,1)S(1)} %get-tuple-element.257), channel_id=1, source_target_pairs={{0,1},{1,0},{2,3},{3,2},{4,5},{5,4},{6,7},{7,6},{8,9},{9,8},{10,11... | collective-permute-start | bytes 540680 | tf_op jit(solution)/shard_map/ppermute | solution.py:537
  38.9 5.8 %collective-permute-start.17 = (bf16[160,512]{1,0:T(8,128)(2,1)S(1)}, bf16[160,512]{1,0:T(8,128)(2,1)S(1)}, u32[]{:S(2)}, u32[]{:S(2)}) collective-permute-start(bf16[160,512]{1,0:T(8,128)(2,1)S(1)} %get-tuple-element.258), channel_id=1, source_target_pairs={{0,1},{1,0},{2,3},{3,2},{4,5},{5,4},{6,7},{7,6},{8,9},{9,8},{10,11... | collective-permute-start | bytes 491528 | tf_op jit(solution)/shard_map/ppermute | solution.py:537
  40.8 18.1 %collective-permute-start.23 = (bf16[528,512]{1,0:T(8,128)(2,1)S(1)}, bf16[528,512]{1,0:T(8,128)(2,1)S(1)}, u32[]{:S(2)}, u32[]{:S(2)}) collective-permute-start(bf16[528,512]{1,0:T(8,128)(2,1)S(1)} %get-tuple-element.285), channel_id=1, source_target_pairs={{0,2},{1,3},{2,0},{3,1},{4,6},{5,7},{6,4},{7,5},{8,10},{9,11},{10,... | collective-permute-start | bytes 1622024 | tf_op jit(solution)/shard_map/ppermute | solution.py:537
  45.0 13.8 %collective-permute-start.24 = (bf16[512,512]{1,0:T(8,128)(2,1)S(1)}, bf16[512,512]{1,0:T(8,128)(2,1)S(1)}, u32[]{:S(2)}, u32[]{:S(2)}) collective-permute-start(bf16[512,512]{1,0:T(8,128)(2,1)S(1)} %get-tuple-element.287), channel_id=1, source_target_pairs={{0,4},{1,5},{2,6},{3,7},{4,0},{5,1},{6,2},{7,3},{8,12},{9,13},{10,... | collective-permute-start | bytes 1572872 | tf_op jit(solution)/shard_map/ppermute | solution.py:537
  49.2 3.8 %collective-permute-start.19 = (bf16[176,512]{1,0:T(8,128)(2,1)S(1)}, bf16[176,512]{1,0:T(8,128)(2,1)S(1)}, u32[]{:S(2)}, u32[]{:S(2)}) collective-permute-start(bf16[176,512]{1,0:T(8,128)(2,1)S(1)} %get-tuple-element.267), channel_id=1, source_target_pairs={{0,1},{1,0},{2,3},{3,2},{4,5},{5,4},{6,7},{7,6},{8,9},{9,8},{10,11... | collective-permute-start | bytes 540680 | tf_op jit(solution)/shard_map/ppermute | solution.py:537
  49.3 3.7 %collective-permute-start.20 = (bf16[176,512]{1,0:T(8,128)(2,1)S(1)}, bf16[176,512]{1,0:T(8,128)(2,1)S(1)}, u32[]{:S(2)}, u32[]{:S(2)}) collective-permute-start(bf16[176,512]{1,0:T(8,128)(2,1)S(1)} %get-tuple-element.268), channel_id=1, source_target_pairs={{0,1},{1,0},{2,3},{3,2},{4,5},{5,4},{6,7},{7,6},{8,9},{9,8},{10,11... | collective-permute-start | bytes 540680 | tf_op jit(solution)/shard_map/ppermute | solution.py:537
  49.8 2.7 %collective-permute-start.21 = (bf16[160,512]{1,0:T(8,128)(2,1)S(1)}, bf16[160,512]{1,0:T(8,128)(2,1)S(1)}, u32[]{:S(2)}, u32[]{:S(2)}) collective-permute-start(bf16[160,512]{1,0:T(8,128)(2,1)S(1)} %get-tuple-element.269), channel_id=1, source_target_pairs={{0,1},{1,0},{2,3},{3,2},{4,5},{5,4},{6,7},{7,6},{8,9},{9,8},{10,11... | collective-permute-start | bytes 491528 | tf_op jit(solution)/shard_map/ppermute | solution.py:537
  52.5 14.3 %collective-permute-start.18 = (bf16[512,512]{1,0:T(8,128)(2,1)S(1)}, bf16[512,512]{1,0:T(8,128)(2,1)S(1)}, u32[]{:S(2)}, u32[]{:S(2)}) collective-permute-start(bf16[512,512]{1,0:T(8,128)(2,1)S(1)} %get-tuple-element.265), channel_id=1, source_target_pairs={{0,1},{1,0},{2,3},{3,2},{4,5},{5,4},{6,7},{7,6},{8,9},{9,8},{10,11... | collective-permute-start | bytes 1572872 | tf_op jit(solution)/shard_map/ppermute | solution.py:537
  53.1 14.8 %collective-permute-start.22 = (bf16[512,512]{1,0:T(8,128)(2,1)S(1)}, bf16[512,512]{1,0:T(8,128)(2,1)S(1)}, u32[]{:S(2)}, u32[]{:S(2)}) collective-permute-start(bf16[512,512]{1,0:T(8,128)(2,1)S(1)} %get-tuple-element.271), channel_id=1, source_target_pairs={{0,2},{1,3},{2,0},{3,1},{4,6},{5,7},{6,4},{7,5},{8,10},{9,11},{10,... | collective-permute-start | bytes 1572872 | tf_op jit(solution)/shard_map/ppermute | solution.py:537
  59.0 7.7 %collective-permute-start.26 = (bf16[272,512]{1,0:T(8,128)(2,1)S(1)}, bf16[272,512]{1,0:T(8,128)(2,1)S(1)}, u32[]{:S(2)}, u32[]{:S(2)}) collective-permute-start(bf16[272,512]{1,0:T(8,128)(2,1)S(1)} %get-tuple-element.293), channel_id=1, source_target_pairs={{0,4},{1,5},{2,6},{3,7},{4,0},{5,1},{6,2},{7,3},{8,12},{9,13},{10,... | collective-permute-start | bytes 835592 | tf_op jit(solution)/shard_map/ppermute | solution.py:537
  60.6 6.2 %collective-permute-start.25 = (f32[16,512]{1,0:T(8,128)S(1)}, f32[16,512]{1,0:T(8,128)S(1)}, u32[]{:S(2)}, u32[]{:S(2)}) collective-permute-start(f32[16,512]{1,0:T(8,128)S(1)} %get-tuple-element.291.refs_0_), channel_id=1, source_target_pairs={{0,1},{1,0},{2,3},{3,2},{4,5},{5,4},{6,7},{7,6},{8,9},{9,8},{10,11... | collective-permute-start | bytes 98312 | tf_op jit(solution)/shard_map/ppermute | solution.py:537
  60.6 12.4 %collective-permute-start.28 = (bf16[272,512]{1,0:T(8,128)(2,1)S(1)}, bf16[272,512]{1,0:T(8,128)(2,1)S(1)}, u32[]{:S(2)}, u32[]{:S(2)}) collective-permute-start(bf16[272,512]{1,0:T(8,128)(2,1)S(1)} %get-tuple-element.302), channel_id=1, source_target_pairs={{0,2},{1,3},{2,0},{3,1},{4,6},{5,7},{6,4},{7,5},{8,10},{9,11},{10,... | collective-permute-start | bytes 835592 | tf_op jit(solution)/shard_map/ppermute | solution.py:537
  68.1 7.0 %collective-permute-start.27 = (bf16[272,512]{1,0:T(8,128)(2,1)S(1)}, bf16[272,512]{1,0:T(8,128)(2,1)S(1)}, u32[]{:S(2)}, u32[]{:S(2)}) collective-permute-start(bf16[272,512]{1,0:T(8,128)(2,1)S(1)} %get-tuple-element.299), channel_id=1, source_target_pairs={{0,4},{1,5},{2,6},{3,7},{4,0},{5,1},{6,2},{7,3},{8,12},{9,13},{10,... | collective-permute-start | bytes 835592 | tf_op jit(solution)/shard_map/ppermute | solution.py:537
  68.9 7.9 %collective-permute-start.30 = (bf16[144,512]{1,0:T(8,128)(2,1)S(1)}, bf16[144,512]{1,0:T(8,128)(2,1)S(1)}, u32[]{:S(2)}, u32[]{:S(2)}) collective-permute-start(bf16[144,512]{1,0:T(8,128)(2,1)S(1)} %get-tuple-element.309), channel_id=1, source_target_pairs={{0,8},{1,9},{2,10},{3,11},{4,12},{5,13},{6,14},{7,15},{8,0},{9,1},... | collective-permute-start | bytes 442376 | tf_op jit(solution)/shard_map/ppermute | solution.py:537
  75.2 10.1 %collective-permute-start.29 = (bf16[144,512]{1,0:T(8,128)(2,1)S(1)}, bf16[144,512]{1,0:T(8,128)(2,1)S(1)}, u32[]{:S(2)}, u32[]{:S(2)}) collective-permute-start(bf16[144,512]{1,0:T(8,128)(2,1)S(1)} %get-tuple-element.306), channel_id=1, source_target_pairs={{0,8},{1,9},{2,10},{3,11},{4,12},{5,13},{6,14},{7,15},{8,0},{9,1},... | collective-permute-start | bytes 442376 | tf_op jit(solution)/shard_map/ppermute | solution.py:537
  76.9 11.5 %collective-permute-start.33 = (bf16[144,512]{1,0:T(8,128)(2,1)S(1)}, bf16[144,512]{1,0:T(8,128)(2,1)S(1)}, u32[]{:S(2)}, u32[]{:S(2)}) collective-permute-start(bf16[144,512]{1,0:T(8,128)(2,1)S(1)} %get-tuple-element.321), channel_id=1, source_target_pairs={{0,16},{1,17},{2,18},{3,19},{4,20},{5,21},{6,22},{7,23},{8,24},{9,... | collective-permute-start | bytes 442376 | tf_op jit(solution)/shard_map/ppermute | solution.py:537
  79.6 8.9 %collective-permute-start.32 = (bf16[144,512]{1,0:T(8,128)(2,1)S(1)}, bf16[144,512]{1,0:T(8,128)(2,1)S(1)}, u32[]{:S(2)}, u32[]{:S(2)}) collective-permute-start(bf16[144,512]{1,0:T(8,128)(2,1)S(1)} %get-tuple-element.319), channel_id=1, source_target_pairs={{0,8},{1,9},{2,10},{3,11},{4,12},{5,13},{6,14},{7,15},{8,0},{9,1},... | collective-permute-start | bytes 442376 | tf_op jit(solution)/shard_map/ppermute | solution.py:537
  85.4 9.5 %collective-permute-start.31 = (bf16[144,512]{1,0:T(8,128)(2,1)S(1)}, bf16[144,512]{1,0:T(8,128)(2,1)S(1)}, u32[]{:S(2)}, u32[]{:S(2)}) collective-permute-start(bf16[144,512]{1,0:T(8,128)(2,1)S(1)} %get-tuple-element.316), channel_id=1, source_target_pairs={{0,16},{1,17},{2,18},{3,19},{4,20},{5,21},{6,22},{7,23},{8,24},{9,... | collective-permute-start | bytes 442376 | tf_op jit(solution)/shard_map/ppermute | solution.py:537
  88.5 9.5 %collective-permute-start.36 = (bf16[144,512]{1,0:T(8,128)(2,1)S(1)}, bf16[144,512]{1,0:T(8,128)(2,1)S(1)}, u32[]{:S(2)}, u32[]{:S(2)}) collective-permute-start(bf16[144,512]{1,0:T(8,128)(2,1)S(1)} %get-tuple-element.328), channel_id=1, source_target_pairs={{0,16},{1,17},{2,18},{3,19},{4,20},{5,21},{6,22},{7,23},{8,24},{9,... | collective-permute-start | bytes 442376 | tf_op jit(solution)/shard_map/ppermute | solution.py:537
  91.4 9.0 %collective-permute-start.35 = (bf16[128,512]{1,0:T(8,128)(2,1)S(1)}, bf16[128,512]{1,0:T(8,128)(2,1)S(1)}, u32[]{:S(2)}, u32[]{:S(2)}) collective-permute-start(bf16[128,512]{1,0:T(8,128)(2,1)S(1)} %get-tuple-element.326.refs_0_), channel_id=1, source_target_pairs={{0,4},{1,5},{2,6},{3,7},{4,0},{5,1},{6,2},{7,3},{8,12},{9,13},{10,... | collective-permute-start | bytes 393224 | tf_op jit(solution)/shard_map/ppermute | solution.py:537
  95.0 5.6 %collective-permute-start.34 = (bf16[128,512]{1,0:T(8,128)(2,1)S(1)}, bf16[128,512]{1,0:T(8,128)(2,1)S(1)}, u32[]{:S(2)}, u32[]{:S(2)}) collective-permute-start(bf16[128,512]{1,0:T(8,128)(2,1)S(1)} %get-tuple-element.325.refs_0_), channel_id=1, source_target_pairs={{0,8},{1,9},{2,10},{3,11},{4,12},{5,13},{6,14},{7,15},{8,0},{9,1},... | collective-permute-start | bytes 393224 | tf_op jit(solution)/shard_map/ppermute | solution.py:537
  98.1 6.0 %collective-permute-start.40 = (bf16[128,512]{1,0:T(8,128)(2,1)S(1)}, bf16[128,512]{1,0:T(8,128)(2,1)S(1)}, u32[]{:S(2)}, u32[]{:S(2)}) collective-permute-start(bf16[128,512]{1,0:T(8,128)(2,1)S(1)} %get-tuple-element.335.refs_0_), channel_id=1, source_target_pairs={{0,4},{1,5},{2,6},{3,7},{4,0},{5,1},{6,2},{7,3},{8,12},{9,13},{10,... | collective-permute-start | bytes 393224 | tf_op jit(solution)/shard_map/ppermute | solution.py:537
  100.4 8.1 %collective-permute-start.38 = (bf16[256,512]{1,0:T(8,128)(2,1)S(1)}, bf16[256,512]{1,0:T(8,128)(2,1)S(1)}, u32[]{:S(2)}, u32[]{:S(2)}) collective-permute-start(bf16[256,512]{1,0:T(8,128)(2,1)S(1)} %get-tuple-element.333.refs_0_), channel_id=1, source_target_pairs={{0,8},{1,9},{2,10},{3,11},{4,12},{5,13},{6,14},{7,15},{8,0},{9,1},... | collective-permute-start | bytes 786440 | tf_op jit(solution)/shard_map/ppermute | solution.py:537
  100.6 9.4 %collective-permute-start.37 = (bf16[256,512]{1,0:T(8,128)(2,1)S(1)}, bf16[256,512]{1,0:T(8,128)(2,1)S(1)}, u32[]{:S(2)}, u32[]{:S(2)}) collective-permute-start(bf16[256,512]{1,0:T(8,128)(2,1)S(1)} %get-tuple-element.332.refs_0_), channel_id=1, source_target_pairs={{0,4},{1,5},{2,6},{3,7},{4,0},{5,1},{6,2},{7,3},{8,12},{9,13},{10,... | collective-permute-start | bytes 786440 | tf_op jit(solution)/shard_map/ppermute | solution.py:537
  104.0 7.2 %collective-permute-start.41 = (bf16[256,512]{1,0:T(8,128)(2,1)S(1)}, bf16[256,512]{1,0:T(8,128)(2,1)S(1)}, u32[]{:S(2)}, u32[]{:S(2)}) collective-permute-start(bf16[256,512]{1,0:T(8,128)(2,1)S(1)} %get-tuple-element.342.refs_0_), channel_id=1, source_target_pairs={{0,8},{1,9},{2,10},{3,11},{4,12},{5,13},{6,14},{7,15},{8,0},{9,1},... | collective-permute-start | bytes 786440 | tf_op jit(solution)/shard_map/ppermute | solution.py:537
  104.1 3.8 %collective-permute-start.39 = (f32[8,512]{1,0:T(8,128)S(1)}, f32[8,512]{1,0:T(8,128)S(1)}, u32[]{:S(2)}, u32[]{:S(2)}) collective-permute-start(f32[8,512]{1,0:T(8,128)S(1)} %get-tuple-element.334.refs_0_), channel_id=1, source_target_pairs={{0,2},{1,3},{2,0},{3,1},{4,6},{5,7},{6,4},{7,5},{8,10},{9,11},{10,... | collective-permute-start | bytes 49160 | tf_op jit(solution)/shard_map/ppermute | solution.py:537
  (12 other events, 10.0 us)

commit v5 on v4

--- a/solution.py
+++ b/solution.py
@@ -1146,8 +1146,8 @@
         down_sum.double()
         triple_sum.double()
         up_sum.double()
+        finish_down()
         totals()
-        finish_down()
         finish_triple()
         finish_up()
         totals = [v.reshape(-1) for v in s.totals]

time: 113 us -> 113 us (level)
  transfers between devices with their start and end apart: 42 -> 42, of which waited for: 18 -> 17; matrix products, arithmetic and copies ran while one was open for 0% -> 0% of each run, Pallas kernels for 29% -> 29%
where the time goes in v5:
time: 113 us
  starting transfers between devices  37.5 us (33%)
  Pallas kernels  34.3 us (30%)
  waiting for transfers between devices  33.3 us (29%)
  local copies, waits for them, and re-layouts  6.51 us (6%)
  between operations  1.14 us (1%)
    ppermute x42, starting transfers between devices, swap(): return lax.ppermute(value, AXES, [(i, i ^ bit) for i in range(total)])  37.5 us
    pallas_call x52, Pallas kernels, call(): pl.pallas_call(ordered, out_shape=[jax.ShapeDtypeStruct(*out[:2]) for out...  34.3 us
    ppermute x42, waiting for transfers between devices, swap(): return lax.ppermute(value, AXES, [(i, i ^ bit) for i in range(total)])  33.3 us
    unnamed x36, local copies, waits for them, and re-layouts  6.51 us
  transfers between devices with their start and end apart: 42, of which 17 were waited for; matrix products, arithmetic and copies ran while one was open for 0% of the time, Pallas kernels for 29%

profile of v5, /device:TPU:0, one launch (start us, length us, event | category | flops | bytes accessed | tf_op | source)
XLA Modules:
  0.0 112.7 jit_solution(619394103743222499)
XLA Ops:
  1.7 2.6 %collective-permute-start.2 = (bf16[512,384]{1,0:T(8,128)(2,1)}, bf16[512,384]{1,0:T(8,128)(2,1)S(1)}, u32[]{:S(2)}, u32[]{:S(2)}) collective-permute-start(bf16[512,384]{1,0:T(8,128)(2,1)} %refs_4_.10), channel_id=1, source_target_pairs={{0,2},{1,3},{2,0},{3,1},{4,6},{5,7},{6,4},{7,5},{8,10},{9,11},{10,... | collective-permute-start | bytes 1179656 | tf_op jit(solution)/shard_map/ppermute | solution.py:537
  5.0 1.0 copy-done.3
  6.0 0.9 copy-done.7
  8.2 1.2 %copy-done = f32[512,512]{1,0:T(8,128)S(1)} copy-done((f32[512,512]{1,0:T(8,128)S(1)}, f32[512,512]{1,0:T(8,128)}, u32[]{:S(2)}) %copy-start) | copy-done | bytes 1048600
  10.4 2.5 %attend.3 = (bf16[512,384]{1,0:T(8,128)(2,1)S(1)}, bf16[512,384]{1,0:T(8,128)(2,1)S(1)}, f32[4,256,128]{2,1,0:T(8,128)S(1)}, f32[4,256,128]{2,1,0:T(8,128)S(1)},...) custom-call(bf16[512,512]{1,0:T(8,128)(2,1)S(1)} %get-tuple-element.184.refs_0_, ...), custom_call_target="tpu_custom_call" | custom-call | tf_op jit(solution)/shard_map/attend/pallas_call | solution.py:50
  13.6 0.9 collective-permute-done.2.refs_0_.refs_1_.refs_6_
  14.6 2.0 %collective-permute-start.8 = (bf16[512,512]{1,0:T(8,128)(2,1)S(1)}, bf16[512,512]{1,0:T(8,128)(2,1)S(1)}, u32[]{:S(2)}, u32[]{:S(2)}) collective-permute-start(bf16[512,512]{1,0:T(8,128)(2,1)S(1)} %copy-done.5), channel_id=1, source_target_pairs={{0,2},{1,3},{2,0},{3,1},{4,6},{5,7},{6,4},{7,5},{8,10},{9,11},{10,... | collective-permute-start | bytes 1572872 | tf_op jit(solution)/shard_map/ppermute | solution.py:537
  16.6 1.6 %attend.4 = (bf16[512,384]{1,0:T(8,128)(2,1)S(1)}, f32[4,256,128]{2,1,0:T(8,128)S(1)}, bf16[512,128]{1,0:T(8,128)(2,1)S(1)}, f32[8,128]{1,0:T(8,128)S(1)}) custom-call(bf16[512,512]{1,0:T(8,128)(2,1)S(1)} %get-tuple-element.184.refs_0_, bf16[512,384]{1,0:T(8,128)(2,1)S(1)} %collective-permute-done.2.refs_0_.refs_1_.refs_6_, ...), custom_call_target="tpu_custom_call" | custom-call | tf_op jit(solution)/shard_map/attend/pallas_call | solution.py:50
  18.3 1.6 %attend.5 = (bf16[512,384]{1,0:T(8,128)(2,1)S(1)}, f32[4,256,128]{2,1,0:T(8,128)S(1)}, bf16[512,128]{1,0:T(8,128)(2,1)S(1)}, f32[8,128]{1,0:T(8,128)S(1)}) custom-call(bf16[512,512]{1,0:T(8,128)(2,1)S(1)} %get-tuple-element.184.refs_0_, bf16[512,384]{1,0:T(8,128)(2,1)S(1)} %collective-permute-done.5.refs_1_.refs_7_, s32[1]{0:T(128)} %bitcast.3.refs_4_.refs_3_.refs_2_, ...), custom_call_target="tpu_custom_call" | custom-call | tf_op jit(solution)/shard_map/attend/pallas_call | solution.py:50
  19.9 3.1 %collective-permute-done.6.refs_0_ = bf16[1552,128]{1,0:T(8,128)(2,1)S(1)} collective-permute-done((bf16[1552,128]{1,0:T(8,128)(2,1)S(1)}, bf16[1552,128]{1,0:T(8,128)(2,1)S(1)}, u32[]{:S(2)}, u32[]{:S(2)}) %collective-permute-start.6) | collective-permute-done | bytes 397344 | tf_op jit(solution)/shard_map/ppermute | solution.py:537
  23.0 2.0 %collective-permute-start.9 = (bf16[256,512]{1,0:T(8,128)(2,1)S(1)}, bf16[256,512]{1,0:T(8,128)(2,1)S(1)}, u32[]{:S(2)}, u32[]{:S(2)}) collective-permute-start(bf16[256,512]{1,0:T(8,128)(2,1)S(1)} %get-tuple-element.212.refs_0_), channel_id=1, source_target_pairs={{0,4},{1,5},{2,6},{3,7},{4,0},{5,1},{6,2},{7,3},{8,12},{9,13},{10,... | collective-permute-start | bytes 786440 | tf_op jit(solution)/shard_map/ppermute | solution.py:537
  25.0 1.4 %collective-permute-done.7.refs_3_ = bf16[528,128]{1,0:T(8,128)(2,1)S(1)} collective-permute-done((bf16[528,128]{1,0:T(8,128)(2,1)S(1)}, bf16[528,128]{1,0:T(8,128)(2,1)S(1)}, u32[]{:S(2)}, u32[]{:S(2)}) %collective-permute-start.7) | collective-permute-done | bytes 135200 | tf_op jit(solution)/shard_map/ppermute | solution.py:537
  27.1 0.8 second.1
  27.9 2.2 %hidden.3 = (bf16[512,512]{1,0:T(8,128)(2,1)S(1)}, bf16[512,512]{1,0:T(8,128)(2,1)S(1)}, f32[512,512]{1,0:T(8,128)S(1)}, f32[512,512]{1,0:T(8,128)S(1)}, f32[512...) custom-call(bf16[512,512]{1,0:T(8,128)(2,1)S(1)} %get-tuple-element.202.refs_0_, ...), custom_call_target="tpu_custom_call" | custom-call | tf_op jit(solution)/shard_map/hidden/pallas_call | solution.py:50
  31.1 1.8 %hidden_back.3 = (f32[512,512]{1,0:T(8,128)S(1)}, bf16[512,512]{1,0:T(8,128)(2,1)S(1)}, f32[1,512]{1,0:T(1,128)S(1)}, f32[1,512]{1,0:T(1,128)S(1)}, f32[512,512]{1,0:T(8,128)S(1)}, /*index=5*/f32[8,128]{1,0:T(8,128)S(1)}) custom-call(bf16[512,512]{1,0:T(8,128)(2,1)S(1)} %get-tuple-element.207.refs_0_, bf16[512,512]{1,0:T(8,128)(2,1)S(1)} %get-tuple-element.208.refs_1_, ...), custom_call_target="tpu_custom_call" | custom-call | tf_op jit(solution)/shard_map/hidden_back/pallas_call | solution.py:50
  35.1 0.9 collective-permute-done.10.refs_2_
  36.0 1.2 %hidden.4 = (bf16[512,512]{1,0:T(8,128)(2,1)S(1)}, f32[512,512]{1,0:T(8,128)S(1)}, bf16[512,512]{1,0:T(8,128)(2,1)S(1)}, f32[8,128]{1,0:T(8,128)S(1)}) custom-call(bf16[512,512]{1,0:T(8,128)(2,1)S(1)} %get-tuple-element.202.refs_0_, bf16[512,512]{1,0:T(8,128)(2,1)S(1)} %get-tuple-element.203.refs_1_, bf16[512,512]{1,0:T(8,128)(2,1)S(1)} %collective-permute-done.10.refs_2_, ...), custom_call_target="tpu_custom_call" | custom-call | tf_op jit(solution)/shard_map/hidden/pallas_call | solution.py:50
  37.3 1.0 hidden_back.4
  39.3 1.2 %hidden.5 = (bf16[512,512]{1,0:T(8,128)(2,1)S(1)}, f32[512,512]{1,0:T(8,128)S(1)}, f32[512,512]{1,0:T(8,128)S(1)}, f32[8,128]{1,0:T(8,128)S(1)}) custom-call(bf16[512,512]{1,0:T(8,128)(2,1)S(1)} %get-tuple-element.202.refs_0_, bf16[512,512]{1,0:T(8,128)(2,1)S(1)} %get-tuple-element.203.refs_1_, bf16[512,512]{1,0:T(8,128)(2,1)S(1)} %collective-permute-done.8.refs_0_.refs_2_, ...), custom_call_target="tpu_custom_call" | custom-call | tf_op jit(solution)/shard_map/hidden/pallas_call | solution.py:50
  40.8 1.8 %collective-permute-start.23 = (bf16[528,512]{1,0:T(8,128)(2,1)S(1)}, bf16[528,512]{1,0:T(8,128)(2,1)S(1)}, u32[]{:S(2)}, u32[]{:S(2)}) collective-permute-start(bf16[528,512]{1,0:T(8,128)(2,1)S(1)} %get-tuple-element.285), channel_id=1, source_target_pairs={{0,2},{1,3},{2,0},{3,1},{4,6},{5,7},{6,4},{7,5},{8,10},{9,11},{10,... | collective-permute-start | bytes 1622024 | tf_op jit(solution)/shard_map/ppermute | solution.py:537
  42.6 1.0 hidden_back.5
  43.6 1.1 middle.1
  45.0 1.6 %collective-permute-start.24 = (bf16[512,512]{1,0:T(8,128)(2,1)S(1)}, bf16[512,512]{1,0:T(8,128)(2,1)S(1)}, u32[]{:S(2)}, u32[]{:S(2)}) collective-permute-start(bf16[512,512]{1,0:T(8,128)(2,1)S(1)} %get-tuple-element.287), channel_id=1, source_target_pairs={{0,4},{1,5},{2,6},{3,7},{4,0},{5,1},{6,2},{7,3},{8,12},{9,13},{10,... | collective-permute-start | bytes 1572872 | tf_op jit(solution)/shard_map/ppermute | solution.py:537
  46.6 2.6 %attend_back.2 = (bf16[512,384]{1,0:T(8,128)(2,1)S(1)}, bf16[512,384]{1,0:T(8,128)(2,1)S(1)}, bf16[176,512]{1,0:T(8,128)(2,1)S(1)}, bf16[176,512]{1,0:T(8,128)(2...) custom-call(bf16[512,512]{1,0:T(8,128)(2,1)S(1)} %get-tuple-element.243.refs_0_, ...), custom_call_target="tpu_custom_call" | custom-call | tf_op jit(solution)/shard_map/attend_back/pallas_call | solution.py:50
  49.9 2.6 %attend_back.3 = (bf16[512,384]{1,0:T(8,128)(2,1)S(1)}, bf16[512,384]{1,0:T(8,128)(2,1)S(1)}, bf16[512,512]{1,0:T(8,128)(2,1)S(1)}, f32[512,512]{1,0:T(8,128)S(1)}, f32[8,128]{1,0:T(8,128)S(1)}) custom-call(bf16[512,512]{1,0:T(8,128)(2,1)S(1)} %get-tuple-element.243.refs_0_, bf16[512,512]{1,0:T(8,128)(2,1)S(1)} %get-tuple-element.244.refs_1_, ...), custom_call_target="tpu_custom_call" | custom-call | tf_op jit(solution)/shard_map/attend_back/pallas_call | solution.py:50
  53.7 3.3 %input.1 = (f32[512,512]{1,0:T(8,128)}, f32[8,512]{1,0:T(8,128)S(1)}, f32[8,128]{1,0:T(8,128)S(1)}) custom-call(bf16[512,384]{1,0:T(8,128)(2,1)S(1)} %get-tuple-element.273.refs_0_, bf16[512,384]{1,0:T(8,128)(2,1)S(1)} %get-tuple-element.274.refs_1_, bf16[512,384]{1,0:T(8,128)(2,1)S(1)} %get-tuple-element.275.refs_2_, ...), custom_call_target="tpu_custom_call" | custom-call | tf_op jit(solution)/shard_map/input/pallas_call | solution.py:50
  57.0 1.8 %collective-permute-done.24.refs_1_ = bf16[512,512]{1,0:T(8,128)(2,1)S(1)} collective-permute-done((bf16[512,512]{1,0:T(8,128)(2,1)S(1)}, bf16[512,512]{1,0:T(8,128)(2,1)S(1)}, u32[]{:S(2)}, u32[]{:S(2)}) %collective-permute-start.24) | collective-permute-done | bytes 524320 | tf_op jit(solution)/shard_map/ppermute | solution.py:537
  59.0 1.6 %collective-permute-start.26 = (bf16[272,512]{1,0:T(8,128)(2,1)S(1)}, bf16[272,512]{1,0:T(8,128)(2,1)S(1)}, u32[]{:S(2)}, u32[]{:S(2)}) collective-permute-start(bf16[272,512]{1,0:T(8,128)(2,1)S(1)} %get-tuple-element.293), channel_id=1, source_target_pairs={{0,4},{1,5},{2,6},{3,7},{4,0},{5,1},{6,2},{7,3},{8,12},{9,13},{10,... | collective-permute-start | bytes 835592 | tf_op jit(solution)/shard_map/ppermute | solution.py:537
  61.2 5.5 %collective-permute-done.26.refs_1_ = bf16[272,512]{1,0:T(8,128)(2,1)S(1)} collective-permute-done((bf16[272,512]{1,0:T(8,128)(2,1)S(1)}, bf16[272,512]{1,0:T(8,128)(2,1)S(1)}, u32[]{:S(2)}, u32[]{:S(2)}) %collective-permute-start.26) | collective-permute-done | bytes 278560 | tf_op jit(solution)/shard_map/ppermute | solution.py:537
  66.8 1.2 %collective-permute-done.22.refs_2_ = bf16[512,512]{1,0:T(8,128)(2,1)S(1)} collective-permute-done((bf16[512,512]{1,0:T(8,128)(2,1)S(1)}, bf16[512,512]{1,0:T(8,128)(2,1)S(1)}, u32[]{:S(2)}, u32[]{:S(2)}) %collective-permute-start.22) | collective-permute-done | bytes 524320 | tf_op jit(solution)/shard_map/ppermute | solution.py:537
  68.9 1.6 %collective-permute-start.30 = (bf16[144,512]{1,0:T(8,128)(2,1)S(1)}, bf16[144,512]{1,0:T(8,128)(2,1)S(1)}, u32[]{:S(2)}, u32[]{:S(2)}) collective-permute-start(bf16[144,512]{1,0:T(8,128)(2,1)S(1)} %get-tuple-element.309), channel_id=1, source_target_pairs={{0,8},{1,9},{2,10},{3,11},{4,12},{5,13},{6,14},{7,15},{8,0},{9,1},... | collective-permute-start | bytes 442376 | tf_op jit(solution)/shard_map/ppermute | solution.py:537
  70.5 2.6 %collective-permute-done.28.refs_2_ = bf16[272,512]{1,0:T(8,128)(2,1)S(1)} collective-permute-done((bf16[272,512]{1,0:T(8,128)(2,1)S(1)}, bf16[272,512]{1,0:T(8,128)(2,1)S(1)}, u32[]{:S(2)}, u32[]{:S(2)}) %collective-permute-start.28) | collective-permute-done | bytes 278560 | tf_op jit(solution)/shard_map/ppermute | solution.py:537
  73.2 2.0 %collective-permute-done.27.refs_1_ = bf16[272,512]{1,0:T(8,128)(2,1)S(1)} collective-permute-done((bf16[272,512]{1,0:T(8,128)(2,1)S(1)}, bf16[272,512]{1,0:T(8,128)(2,1)S(1)}, u32[]{:S(2)}, u32[]{:S(2)}) %collective-permute-start.27) | collective-permute-done | bytes 278560 | tf_op jit(solution)/shard_map/ppermute | solution.py:537
  75.2 1.6 %collective-permute-start.29 = (bf16[144,512]{1,0:T(8,128)(2,1)S(1)}, bf16[144,512]{1,0:T(8,128)(2,1)S(1)}, u32[]{:S(2)}, u32[]{:S(2)}) collective-permute-start(bf16[144,512]{1,0:T(8,128)(2,1)S(1)} %get-tuple-element.306), channel_id=1, source_target_pairs={{0,8},{1,9},{2,10},{3,11},{4,12},{5,13},{6,14},{7,15},{8,0},{9,1},... | collective-permute-start | bytes 442376 | tf_op jit(solution)/shard_map/ppermute | solution.py:537
  76.9 2.7 %collective-permute-start.33 = (bf16[144,512]{1,0:T(8,128)(2,1)S(1)}, bf16[144,512]{1,0:T(8,128)(2,1)S(1)}, u32[]{:S(2)}, u32[]{:S(2)}) collective-permute-start(bf16[144,512]{1,0:T(8,128)(2,1)S(1)} %get-tuple-element.321), channel_id=1, source_target_pairs={{0,16},{1,17},{2,18},{3,19},{4,20},{5,21},{6,22},{7,23},{8,24},{9,... | collective-permute-start | bytes 442376 | tf_op jit(solution)/shard_map/ppermute | solution.py:537
  80.0 5.3 %collective-permute-done.29.refs_1_ = bf16[144,512]{1,0:T(8,128)(2,1)S(1)} collective-permute-done((bf16[144,512]{1,0:T(8,128)(2,1)S(1)}, bf16[144,512]{1,0:T(8,128)(2,1)S(1)}, u32[]{:S(2)}, u32[]{:S(2)}) %collective-permute-start.29) | collective-permute-done | bytes 147488 | tf_op jit(solution)/shard_map/ppermute | solution.py:537
  86.2 2.2 %output.1 = (f32[512,512]{1,0:T(8,128)}, f32[8,128]{1,0:T(8,128)S(1)}) custom-call(bf16[512,512]{1,0:T(8,128)(2,1)S(1)} %get-tuple-element.205.refs_0_, bf16[512,512]{1,0:T(8,128)(2,1)S(1)} %get-tuple-element.206.refs_1_, bf16[512,512]{1,0:T(8,128)(2,1)S(1)} %get-tuple-element.229.refs_2_, bf16[512,512]{1,0:T(8,128)(2,1)S(1)} %get-tuple-element.230.refs_3_, ...), custom_call_target="tpu_custom_call" | custom-call | tf_op jit(solution)/shard_map/output/pallas_call | solution.py:50
  88.5 3.0 %collective-permute-start.36 = (bf16[144,512]{1,0:T(8,128)(2,1)S(1)}, bf16[144,512]{1,0:T(8,128)(2,1)S(1)}, u32[]{:S(2)}, u32[]{:S(2)}) collective-permute-start(bf16[144,512]{1,0:T(8,128)(2,1)S(1)} %get-tuple-element.328), channel_id=1, source_target_pairs={{0,16},{1,17},{2,18},{3,19},{4,20},{5,21},{6,22},{7,23},{8,24},{9,... | collective-permute-start | bytes 442376 | tf_op jit(solution)/shard_map/ppermute | solution.py:537
  91.4 2.1 %collective-permute-start.35 = (bf16[128,512]{1,0:T(8,128)(2,1)S(1)}, bf16[128,512]{1,0:T(8,128)(2,1)S(1)}, u32[]{:S(2)}, u32[]{:S(2)}) collective-permute-start(bf16[128,512]{1,0:T(8,128)(2,1)S(1)} %get-tuple-element.326.refs_0_), channel_id=1, source_target_pairs={{0,4},{1,5},{2,6},{3,7},{4,0},{5,1},{6,2},{7,3},{8,12},{9,13},{10,... | collective-permute-start | bytes 393224 | tf_op jit(solution)/shard_map/ppermute | solution.py:537
  93.5 1.4 %collective-permute-done.31.refs_1_ = bf16[144,512]{1,0:T(8,128)(2,1)S(1)} collective-permute-done((bf16[144,512]{1,0:T(8,128)(2,1)S(1)}, bf16[144,512]{1,0:T(8,128)(2,1)S(1)}, u32[]{:S(2)}, u32[]{:S(2)}) %collective-permute-start.31) | collective-permute-done | bytes 147488 | tf_op jit(solution)/shard_map/ppermute | solution.py:537
  95.0 3.0 %collective-permute-done.36.refs_1_ = bf16[144,512]{1,0:T(8,128)(2,1)S(1)} collective-permute-done((bf16[144,512]{1,0:T(8,128)(2,1)S(1)}, bf16[144,512]{1,0:T(8,128)(2,1)S(1)}, u32[]{:S(2)}, u32[]{:S(2)}) %collective-permute-start.36) | collective-permute-done | bytes 147488 | tf_op jit(solution)/shard_map/ppermute | solution.py:537
  98.1 2.3 %collective-permute-start.40 = (bf16[128,512]{1,0:T(8,128)(2,1)S(1)}, bf16[128,512]{1,0:T(8,128)(2,1)S(1)}, u32[]{:S(2)}, u32[]{:S(2)}) collective-permute-start(bf16[128,512]{1,0:T(8,128)(2,1)S(1)} %get-tuple-element.335.refs_0_), channel_id=1, source_target_pairs={{0,4},{1,5},{2,6},{3,7},{4,0},{5,1},{6,2},{7,3},{8,12},{9,13},{10,... | collective-permute-start | bytes 393224 | tf_op jit(solution)/shard_map/ppermute | solution.py:537
  100.6 3.1 %collective-permute-start.37 = (bf16[256,512]{1,0:T(8,128)(2,1)S(1)}, bf16[256,512]{1,0:T(8,128)(2,1)S(1)}, u32[]{:S(2)}, u32[]{:S(2)}) collective-permute-start(bf16[256,512]{1,0:T(8,128)(2,1)S(1)} %get-tuple-element.332.refs_0_), channel_id=1, source_target_pairs={{0,4},{1,5},{2,6},{3,7},{4,0},{5,1},{6,2},{7,3},{8,12},{9,13},{10,... | collective-permute-start | bytes 786440 | tf_op jit(solution)/shard_map/ppermute | solution.py:537
  104.1 2.0 %collective-permute-start.38 = (f32[8,512]{1,0:T(8,128)S(1)}, f32[8,512]{1,0:T(8,128)S(1)}, u32[]{:S(2)}, u32[]{:S(2)}) collective-permute-start(f32[8,512]{1,0:T(8,128)S(1)} %get-tuple-element.333.refs_0_), channel_id=1, source_target_pairs={{0,2},{1,3},{2,0},{3,1},{4,6},{5,7},{6,4},{7,5},{8,10},{9,11},{10,... | collective-permute-start | bytes 49160 | tf_op jit(solution)/shard_map/ppermute | solution.py:537
  106.1 2.3 %collective-permute-done.39.refs_1_ = bf16[256,512]{1,0:T(8,128)(2,1)S(1)} collective-permute-done((bf16[256,512]{1,0:T(8,128)(2,1)S(1)}, bf16[256,512]{1,0:T(8,128)(2,1)S(1)}, u32[]{:S(2)}, u32[]{:S(2)}) %collective-permute-start.39) | collective-permute-done | bytes 262176 | tf_op jit(solution)/shard_map/ppermute | solution.py:537
  108.4 1.4 %finish_d.1 = (f32[512,512]{1,0:T(8,128)}, f32[8,128]{1,0:T(8,128)S(1)}) custom-call(bf16[256,512]{1,0:T(8,128)(2,1)S(1)} %get-tuple-element.334.refs_0_, bf16[256,512]{1,0:T(8,128)(2,1)S(1)} %collective-permute-done.39.refs_1_, s32[1]{0:T(128)} %bitcast.2.refs_3_.refs_2_.refs_4_, f32[8,128]{1,0:T(8,128)S(1)} %get-tuple-element.337.refs_3_), custom_call_target="tpu_custom_call" | custom-call | tf_op jit(solution)/shard_map/finish_d/pallas_call | solution.py:50
  110.4 1.2 %finish_t.1 = (f32[512,384]{1,0:T(8,128)}, f32[128,512]{1,0:T(8,128)}, f32[8,128]{1,0:T(8,128)S(1)}) custom-call(bf16[256,512]{1,0:T(8,128)(2,1)S(1)} %get-tuple-element.332.refs_0_, bf16[256,512]{1,0:T(8,128)(2,1)S(1)} %collective-permute-done.37.refs_1_, s32[1]{0:T(128)} %bitcast.2.refs_3_.refs_2_.refs_4_, f32[8,128]{1,0:T(8,128)S(1)} %get-tuple-element.339.refs_3_), custom_call_target="tpu_custom_call" | custom-call | tf_op jit(solution)/shard_map/finish_t/pallas_call | solution.py:50
  111.6 1.1 %finish_u.1 = (f32[512,512]{1,0:T(8,128)}, f32[8,128]{1,0:T(8,128)}) custom-call(bf16[256,512]{1,0:T(8,128)(2,1)S(1)} %get-tuple-element.342.refs_0_, bf16[256,512]{1,0:T(8,128)(2,1)S(1)} %collective-permute-done.41.refs_1_, s32[1]{0:T(128)} %bitcast.2.refs_3_.refs_2_.refs_4_, f32[8,128]{1,0:T(8,128)S(1)} %get-tuple-element.343.refs_3_), custom_call_target="tpu_custom_call" | custom-call | tf_op jit(solution)/shard_map/finish_u/pallas_call | solution.py:50
  (126 shorter events, 16.9 us)
Async XLA Ops:
  0.6 6.6 %collective-permute-start = (bf16[512,512]{1,0:T(8,128)(2,1)}, bf16[512,512]{1,0:T(8,128)(2,1)S(1)}, u32[]{:S(2)}, u32[]{:S(2)}) collective-permute-start(bf16[512,512]{1,0:T(8,128)(2,1)} %refs_2_.5), channel_id=1, source_target_pairs={{0,1},{1,0},{2,3},{3,2},{4,5},{5,4},{6,7},{7,6},{8,9},{9,8},{10,11... | collective-permute-start | bytes 1572872 | tf_op jit(solution)/shard_map/ppermute | solution.py:537
  1.2 6.4 %collective-permute-start.1 = (bf16[512,512]{1,0:T(8,128)(2,1)}, bf16[512,512]{1,0:T(8,128)(2,1)S(1)}, u32[]{:S(2)}, u32[]{:S(2)}) collective-permute-start(bf16[512,512]{1,0:T(8,128)(2,1)} %refs_4_.11), channel_id=1, source_target_pairs={{0,1},{1,0},{2,3},{3,2},{4,5},{5,4},{6,7},{7,6},{8,9},{9,8},{10,11... | collective-permute-start | bytes 1572872 | tf_op jit(solution)/shard_map/ppermute | solution.py:537
  1.2 8.8 %collective-permute-start.3 = (bf16[512,384]{1,0:T(8,128)(2,1)}, bf16[512,384]{1,0:T(8,128)(2,1)S(1)}, u32[]{:S(2)}, u32[]{:S(2)}) collective-permute-start(bf16[512,384]{1,0:T(8,128)(2,1)} %refs_4_.10), channel_id=1, source_target_pairs={{0,1},{1,0},{2,3},{3,2},{4,5},{5,4},{6,7},{7,6},{8,9},{9,8},{10,11... | collective-permute-start | bytes 1179656 | tf_op jit(solution)/shard_map/ppermute | solution.py:537
  1.7 12.8 %collective-permute-start.2 = (bf16[512,384]{1,0:T(8,128)(2,1)}, bf16[512,384]{1,0:T(8,128)(2,1)S(1)}, u32[]{:S(2)}, u32[]{:S(2)}) collective-permute-start(bf16[512,384]{1,0:T(8,128)(2,1)} %refs_4_.10), channel_id=1, source_target_pairs={{0,2},{1,3},{2,0},{3,1},{4,6},{5,7},{6,4},{7,5},{8,10},{9,11},{10,... | collective-permute-start | bytes 1179656 | tf_op jit(solution)/shard_map/ppermute | solution.py:537
  7.0 6.1 %collective-permute-start.4 = (bf16[528,128]{1,0:T(8,128)(2,1)S(1)}, bf16[528,128]{1,0:T(8,128)(2,1)S(1)}, u32[]{:S(2)}, u32[]{:S(2)}) collective-permute-start(bf16[528,128]{1,0:T(8,128)(2,1)S(1)} %get-tuple-element.188.refs_2_.refs_4_), channel_id=1, source_target_pairs={{0,1},{1,0},{2,3},{3,2},{4,5},{5,4},{6,7},{7,6},{8,9},{9,8},{10,11... | collective-permute-start | bytes 405512 | tf_op jit(solution)/shard_map/ppermute | solution.py:537
  7.2 15.7 %collective-permute-start.6 = (bf16[1552,128]{1,0:T(8,128)(2,1)S(1)}, bf16[1552,128]{1,0:T(8,128)(2,1)S(1)}, u32[]{:S(2)}, u32[]{:S(2)}) collective-permute-start(bf16[1552,128]{1,0:T(8,128)(2,1)S(1)} %get-tuple-element.197), channel_id=1, source_target_pairs={{0,2},{1,3},{2,0},{3,1},{4,6},{5,7},{6,4},{7,5},{8,10},{9,11},{10,... | collective-permute-start | bytes 1191944 | tf_op jit(solution)/shard_map/ppermute | solution.py:537
  8.2 1.2 %copy-start = (f32[512,512]{1,0:T(8,128)S(1)}, f32[512,512]{1,0:T(8,128)}, u32[]{:S(2)}) copy-start(f32[512,512]{1,0:T(8,128)} %refs_8_.1) | copy-start | bytes 3145732
  10.0 2.9 %copy-start.2 = (f32[512,512]{1,0:T(8,128)S(1)}, f32[512,512]{1,0:T(8,128)}, u32[]{:S(2)}) copy-start(f32[512,512]{1,0:T(8,128)} %refs_11_.1) | copy-start | bytes 3145732
  13.1 1.4 %copy-start.5 = (bf16[512,512]{1,0:T(8,128)(2,1)S(1)}, bf16[512,512]{1,0:T(8,128)(2,1)}, u32[]{:S(2)}) copy-start(bf16[512,512]{1,0:T(8,128)(2,1)} %refs_2_.5) | copy-start | bytes 1572868
  14.5 3.8 %collective-permute-start.5 = (bf16[512,384]{1,0:T(8,128)(2,1)S(1)}, bf16[512,384]{1,0:T(8,128)(2,1)S(1)}, u32[]{:S(2)}, u32[]{:S(2)}) collective-permute-start(bf16[512,384]{1,0:T(8,128)(2,1)S(1)} %get-tuple-element.194), channel_id=1, source_target_pairs={{0,1},{1,0},{2,3},{3,2},{4,5},{5,4},{6,7},{7,6},{8,9},{9,8},{10,11... | collective-permute-start | bytes 1179656 | tf_op jit(solution)/shard_map/ppermute | solution.py:537
  14.6 19.4 %collective-permute-start.8 = (bf16[512,512]{1,0:T(8,128)(2,1)S(1)}, bf16[512,512]{1,0:T(8,128)(2,1)S(1)}, u32[]{:S(2)}, u32[]{:S(2)}) collective-permute-start(bf16[512,512]{1,0:T(8,128)(2,1)S(1)} %copy-done.5), channel_id=1, source_target_pairs={{0,2},{1,3},{2,0},{3,1},{4,6},{5,7},{6,4},{7,5},{8,10},{9,11},{10,... | collective-permute-start | bytes 1572872 | tf_op jit(solution)/shard_map/ppermute | solution.py:537
  16.6 9.8 %copy-start.1 = (f32[512,512]{1,0:T(8,128)S(1)}, f32[512,512]{1,0:T(8,128)}, u32[]{:S(2)}) copy-start(f32[512,512]{1,0:T(8,128)} %refs_8_.1) | copy-start | bytes 3145732
  23.0 3.4 %copy-start.16 = (f32[512]{0:T(512)S(1)}, f32[512]{0:T(512)}, u32[]{:S(2)}) copy-start(f32[512]{0:T(512)} %param.28) | copy-start | bytes 6148
  23.0 7.9 %collective-permute-start.9 = (bf16[256,512]{1,0:T(8,128)(2,1)S(1)}, bf16[256,512]{1,0:T(8,128)(2,1)S(1)}, u32[]{:S(2)}, u32[]{:S(2)}) collective-permute-start(bf16[256,512]{1,0:T(8,128)(2,1)S(1)} %get-tuple-element.212.refs_0_), channel_id=1, source_target_pairs={{0,4},{1,5},{2,6},{3,7},{4,0},{5,1},{6,2},{7,3},{8,12},{9,13},{10,... | collective-permute-start | bytes 786440 | tf_op jit(solution)/shard_map/ppermute | solution.py:537
  25.0 1.4 %collective-permute-start.7 = (bf16[528,128]{1,0:T(8,128)(2,1)S(1)}, bf16[528,128]{1,0:T(8,128)(2,1)S(1)}, u32[]{:S(2)}, u32[]{:S(2)}) collective-permute-start(bf16[528,128]{1,0:T(8,128)(2,1)S(1)} %get-tuple-element.199.refs_2_.refs_3_.refs_4_), channel_id=1, source_target_pairs={{0,1},{1,0},{2,3},{3,2},{4,5},{5,4},{6,7},{7,6},{8,9},{9,8},{10,11... | collective-permute-start | bytes 405512 | tf_op jit(solution)/shard_map/ppermute | solution.py:537
  30.1 1.0 copy-start.4
  33.0 2.0 %collective-permute-start.12 = (bf16[512,512]{1,0:T(8,128)(2,1)S(1)}, bf16[512,512]{1,0:T(8,128)(2,1)S(1)}, u32[]{:S(2)}, u32[]{:S(2)}) collective-permute-start(bf16[512,512]{1,0:T(8,128)(2,1)S(1)} %get-tuple-element.219), channel_id=1, source_target_pairs={{0,1},{1,0},{2,3},{3,2},{4,5},{5,4},{6,7},{7,6},{8,9},{9,8},{10,11... | collective-permute-start | bytes 1572872 | tf_op jit(solution)/shard_map/ppermute | solution.py:537
  34.0 2.0 %collective-permute-start.10 = (bf16[512,512]{1,0:T(8,128)(2,1)S(1)}, bf16[512,512]{1,0:T(8,128)(2,1)S(1)}, u32[]{:S(2)}, u32[]{:S(2)}) collective-permute-start(bf16[512,512]{1,0:T(8,128)(2,1)S(1)} %get-tuple-element.217), channel_id=1, source_target_pairs={{0,1},{1,0},{2,3},{3,2},{4,5},{5,4},{6,7},{7,6},{8,9},{9,8},{10,11... | collective-permute-start | bytes 1572872 | tf_op jit(solution)/shard_map/ppermute | solution.py:537
  34.1 3.3 %collective-permute-start.11 = (bf16[512,512]{1,0:T(8,128)(2,1)S(1)}, bf16[512,512]{1,0:T(8,128)(2,1)S(1)}, u32[]{:S(2)}, u32[]{:S(2)}) collective-permute-start(bf16[512,512]{1,0:T(8,128)(2,1)S(1)} %get-tuple-element.218.refs_3_.refs_6_), channel_id=1, source_target_pairs={{0,1},{1,0},{2,3},{3,2},{4,5},{5,4},{6,7},{7,6},{8,9},{9,8},{10,11... | collective-permute-start | bytes 1572872 | tf_op jit(solution)/shard_map/ppermute | solution.py:537
  34.6 5.9 %collective-permute-start.14 = (bf16[512,512]{1,0:T(8,128)(2,1)S(1)}, bf16[512,512]{1,0:T(8,128)(2,1)S(1)}, u32[]{:S(2)}, u32[]{:S(2)}) collective-permute-start(bf16[512,512]{1,0:T(8,128)(2,1)S(1)} %get-tuple-element.236), channel_id=1, source_target_pairs={{0,1},{1,0},{2,3},{3,2},{4,5},{5,4},{6,7},{7,6},{8,9},{9,8},{10,11... | collective-permute-start | bytes 1572872 | tf_op jit(solution)/shard_map/ppermute | solution.py:537
  37.1 3.6 %collective-permute-start.13 = (bf16[512,512]{1,0:T(8,128)(2,1)S(1)}, bf16[512,512]{1,0:T(8,128)(2,1)S(1)}, u32[]{:S(2)}, u32[]{:S(2)}) collective-permute-start(bf16[512,512]{1,0:T(8,128)(2,1)S(1)} %get-tuple-element.235), channel_id=1, source_target_pairs={{0,1},{1,0},{2,3},{3,2},{4,5},{5,4},{6,7},{7,6},{8,9},{9,8},{10,11... | collective-permute-start | bytes 1572872 | tf_op jit(solution)/shard_map/ppermute | solution.py:537
  38.4 6.4 %collective-permute-start.15 = (bf16[176,512]{1,0:T(8,128)(2,1)S(1)}, bf16[176,512]{1,0:T(8,128)(2,1)S(1)}, u32[]{:S(2)}, u32[]{:S(2)}) collective-permute-start(bf16[176,512]{1,0:T(8,128)(2,1)S(1)} %get-tuple-element.256), channel_id=1, source_target_pairs={{0,1},{1,0},{2,3},{3,2},{4,5},{5,4},{6,7},{7,6},{8,9},{9,8},{10,11... | collective-permute-start | bytes 540680 | tf_op jit(solution)/shard_map/ppermute | solution.py:537
  38.8 6.0 %collective-permute-start.16 = (bf16[176,512]{1,0:T(8,128)(2,1)S(1)}, bf16[176,512]{1,0:T(8,128)(2,1)S(1)}, u32[]{:S(2)}, u32[]{:S(2)}) collective-permute-start(bf16[176,512]{1,0:T(8,128)(2,1)S(1)} %get-tuple-element.257), channel_id=1, source_target_pairs={{0,1},{1,0},{2,3},{3,2},{4,5},{5,4},{6,7},{7,6},{8,9},{9,8},{10,11... | collective-permute-start | bytes 540680 | tf_op jit(solution)/shard_map/ppermute | solution.py:537
  38.9 5.8 %collective-permute-start.17 = (bf16[160,512]{1,0:T(8,128)(2,1)S(1)}, bf16[160,512]{1,0:T(8,128)(2,1)S(1)}, u32[]{:S(2)}, u32[]{:S(2)}) collective-permute-start(bf16[160,512]{1,0:T(8,128)(2,1)S(1)} %get-tuple-element.258), channel_id=1, source_target_pairs={{0,1},{1,0},{2,3},{3,2},{4,5},{5,4},{6,7},{7,6},{8,9},{9,8},{10,11... | collective-permute-start | bytes 491528 | tf_op jit(solution)/shard_map/ppermute | solution.py:537
  40.8 18.1 %collective-permute-start.23 = (bf16[528,512]{1,0:T(8,128)(2,1)S(1)}, bf16[528,512]{1,0:T(8,128)(2,1)S(1)}, u32[]{:S(2)}, u32[]{:S(2)}) collective-permute-start(bf16[528,512]{1,0:T(8,128)(2,1)S(1)} %get-tuple-element.285), channel_id=1, source_target_pairs={{0,2},{1,3},{2,0},{3,1},{4,6},{5,7},{6,4},{7,5},{8,10},{9,11},{10,... | collective-permute-start | bytes 1622024 | tf_op jit(solution)/shard_map/ppermute | solution.py:537
  45.0 13.8 %collective-permute-start.24 = (bf16[512,512]{1,0:T(8,128)(2,1)S(1)}, bf16[512,512]{1,0:T(8,128)(2,1)S(1)}, u32[]{:S(2)}, u32[]{:S(2)}) collective-permute-start(bf16[512,512]{1,0:T(8,128)(2,1)S(1)} %get-tuple-element.287), channel_id=1, source_target_pairs={{0,4},{1,5},{2,6},{3,7},{4,0},{5,1},{6,2},{7,3},{8,12},{9,13},{10,... | collective-permute-start | bytes 1572872 | tf_op jit(solution)/shard_map/ppermute | solution.py:537
  49.2 3.8 %collective-permute-start.19 = (bf16[176,512]{1,0:T(8,128)(2,1)S(1)}, bf16[176,512]{1,0:T(8,128)(2,1)S(1)}, u32[]{:S(2)}, u32[]{:S(2)}) collective-permute-start(bf16[176,512]{1,0:T(8,128)(2,1)S(1)} %get-tuple-element.267), channel_id=1, source_target_pairs={{0,1},{1,0},{2,3},{3,2},{4,5},{5,4},{6,7},{7,6},{8,9},{9,8},{10,11... | collective-permute-start | bytes 540680 | tf_op jit(solution)/shard_map/ppermute | solution.py:537
  49.3 3.7 %collective-permute-start.20 = (bf16[176,512]{1,0:T(8,128)(2,1)S(1)}, bf16[176,512]{1,0:T(8,128)(2,1)S(1)}, u32[]{:S(2)}, u32[]{:S(2)}) collective-permute-start(bf16[176,512]{1,0:T(8,128)(2,1)S(1)} %get-tuple-element.268), channel_id=1, source_target_pairs={{0,1},{1,0},{2,3},{3,2},{4,5},{5,4},{6,7},{7,6},{8,9},{9,8},{10,11... | collective-permute-start | bytes 540680 | tf_op jit(solution)/shard_map/ppermute | solution.py:537
  49.8 2.7 %collective-permute-start.21 = (bf16[160,512]{1,0:T(8,128)(2,1)S(1)}, bf16[160,512]{1,0:T(8,128)(2,1)S(1)}, u32[]{:S(2)}, u32[]{:S(2)}) collective-permute-start(bf16[160,512]{1,0:T(8,128)(2,1)S(1)} %get-tuple-element.269), channel_id=1, source_target_pairs={{0,1},{1,0},{2,3},{3,2},{4,5},{5,4},{6,7},{7,6},{8,9},{9,8},{10,11... | collective-permute-start | bytes 491528 | tf_op jit(solution)/shard_map/ppermute | solution.py:537
  52.5 14.3 %collective-permute-start.18 = (bf16[512,512]{1,0:T(8,128)(2,1)S(1)}, bf16[512,512]{1,0:T(8,128)(2,1)S(1)}, u32[]{:S(2)}, u32[]{:S(2)}) collective-permute-start(bf16[512,512]{1,0:T(8,128)(2,1)S(1)} %get-tuple-element.265), channel_id=1, source_target_pairs={{0,1},{1,0},{2,3},{3,2},{4,5},{5,4},{6,7},{7,6},{8,9},{9,8},{10,11... | collective-permute-start | bytes 1572872 | tf_op jit(solution)/shard_map/ppermute | solution.py:537
  53.1 14.8 %collective-permute-start.22 = (bf16[512,512]{1,0:T(8,128)(2,1)S(1)}, bf16[512,512]{1,0:T(8,128)(2,1)S(1)}, u32[]{:S(2)}, u32[]{:S(2)}) collective-permute-start(bf16[512,512]{1,0:T(8,128)(2,1)S(1)} %get-tuple-element.271), channel_id=1, source_target_pairs={{0,2},{1,3},{2,0},{3,1},{4,6},{5,7},{6,4},{7,5},{8,10},{9,11},{10,... | collective-permute-start | bytes 1572872 | tf_op jit(solution)/shard_map/ppermute | solution.py:537
  59.0 7.7 %collective-permute-start.26 = (bf16[272,512]{1,0:T(8,128)(2,1)S(1)}, bf16[272,512]{1,0:T(8,128)(2,1)S(1)}, u32[]{:S(2)}, u32[]{:S(2)}) collective-permute-start(bf16[272,512]{1,0:T(8,128)(2,1)S(1)} %get-tuple-element.293), channel_id=1, source_target_pairs={{0,4},{1,5},{2,6},{3,7},{4,0},{5,1},{6,2},{7,3},{8,12},{9,13},{10,... | collective-permute-start | bytes 835592 | tf_op jit(solution)/shard_map/ppermute | solution.py:537
  60.6 6.2 %collective-permute-start.25 = (f32[16,512]{1,0:T(8,128)S(1)}, f32[16,512]{1,0:T(8,128)S(1)}, u32[]{:S(2)}, u32[]{:S(2)}) collective-permute-start(f32[16,512]{1,0:T(8,128)S(1)} %get-tuple-element.291.refs_0_), channel_id=1, source_target_pairs={{0,1},{1,0},{2,3},{3,2},{4,5},{5,4},{6,7},{7,6},{8,9},{9,8},{10,11... | collective-permute-start | bytes 98312 | tf_op jit(solution)/shard_map/ppermute | solution.py:537
  60.6 12.4 %collective-permute-start.28 = (bf16[272,512]{1,0:T(8,128)(2,1)S(1)}, bf16[272,512]{1,0:T(8,128)(2,1)S(1)}, u32[]{:S(2)}, u32[]{:S(2)}) collective-permute-start(bf16[272,512]{1,0:T(8,128)(2,1)S(1)} %get-tuple-element.302), channel_id=1, source_target_pairs={{0,2},{1,3},{2,0},{3,1},{4,6},{5,7},{6,4},{7,5},{8,10},{9,11},{10,... | collective-permute-start | bytes 835592 | tf_op jit(solution)/shard_map/ppermute | solution.py:537
  68.1 7.0 %collective-permute-start.27 = (bf16[272,512]{1,0:T(8,128)(2,1)S(1)}, bf16[272,512]{1,0:T(8,128)(2,1)S(1)}, u32[]{:S(2)}, u32[]{:S(2)}) collective-permute-start(bf16[272,512]{1,0:T(8,128)(2,1)S(1)} %get-tuple-element.299), channel_id=1, source_target_pairs={{0,4},{1,5},{2,6},{3,7},{4,0},{5,1},{6,2},{7,3},{8,12},{9,13},{10,... | collective-permute-start | bytes 835592 | tf_op jit(solution)/shard_map/ppermute | solution.py:537
  68.9 7.9 %collective-permute-start.30 = (bf16[144,512]{1,0:T(8,128)(2,1)S(1)}, bf16[144,512]{1,0:T(8,128)(2,1)S(1)}, u32[]{:S(2)}, u32[]{:S(2)}) collective-permute-start(bf16[144,512]{1,0:T(8,128)(2,1)S(1)} %get-tuple-element.309), channel_id=1, source_target_pairs={{0,8},{1,9},{2,10},{3,11},{4,12},{5,13},{6,14},{7,15},{8,0},{9,1},... | collective-permute-start | bytes 442376 | tf_op jit(solution)/shard_map/ppermute | solution.py:537
  75.2 10.1 %collective-permute-start.29 = (bf16[144,512]{1,0:T(8,128)(2,1)S(1)}, bf16[144,512]{1,0:T(8,128)(2,1)S(1)}, u32[]{:S(2)}, u32[]{:S(2)}) collective-permute-start(bf16[144,512]{1,0:T(8,128)(2,1)S(1)} %get-tuple-element.306), channel_id=1, source_target_pairs={{0,8},{1,9},{2,10},{3,11},{4,12},{5,13},{6,14},{7,15},{8,0},{9,1},... | collective-permute-start | bytes 442376 | tf_op jit(solution)/shard_map/ppermute | solution.py:537
  76.9 11.5 %collective-permute-start.33 = (bf16[144,512]{1,0:T(8,128)(2,1)S(1)}, bf16[144,512]{1,0:T(8,128)(2,1)S(1)}, u32[]{:S(2)}, u32[]{:S(2)}) collective-permute-start(bf16[144,512]{1,0:T(8,128)(2,1)S(1)} %get-tuple-element.321), channel_id=1, source_target_pairs={{0,16},{1,17},{2,18},{3,19},{4,20},{5,21},{6,22},{7,23},{8,24},{9,... | collective-permute-start | bytes 442376 | tf_op jit(solution)/shard_map/ppermute | solution.py:537
  79.6 8.9 %collective-permute-start.32 = (bf16[144,512]{1,0:T(8,128)(2,1)S(1)}, bf16[144,512]{1,0:T(8,128)(2,1)S(1)}, u32[]{:S(2)}, u32[]{:S(2)}) collective-permute-start(bf16[144,512]{1,0:T(8,128)(2,1)S(1)} %get-tuple-element.319), channel_id=1, source_target_pairs={{0,8},{1,9},{2,10},{3,11},{4,12},{5,13},{6,14},{7,15},{8,0},{9,1},... | collective-permute-start | bytes 442376 | tf_op jit(solution)/shard_map/ppermute | solution.py:537
  85.4 9.5 %collective-permute-start.31 = (bf16[144,512]{1,0:T(8,128)(2,1)S(1)}, bf16[144,512]{1,0:T(8,128)(2,1)S(1)}, u32[]{:S(2)}, u32[]{:S(2)}) collective-permute-start(bf16[144,512]{1,0:T(8,128)(2,1)S(1)} %get-tuple-element.316), channel_id=1, source_target_pairs={{0,16},{1,17},{2,18},{3,19},{4,20},{5,21},{6,22},{7,23},{8,24},{9,... | collective-permute-start | bytes 442376 | tf_op jit(solution)/shard_map/ppermute | solution.py:537
  88.5 9.5 %collective-permute-start.36 = (bf16[144,512]{1,0:T(8,128)(2,1)S(1)}, bf16[144,512]{1,0:T(8,128)(2,1)S(1)}, u32[]{:S(2)}, u32[]{:S(2)}) collective-permute-start(bf16[144,512]{1,0:T(8,128)(2,1)S(1)} %get-tuple-element.328), channel_id=1, source_target_pairs={{0,16},{1,17},{2,18},{3,19},{4,20},{5,21},{6,22},{7,23},{8,24},{9,... | collective-permute-start | bytes 442376 | tf_op jit(solution)/shard_map/ppermute | solution.py:537
  91.4 9.0 %collective-permute-start.35 = (bf16[128,512]{1,0:T(8,128)(2,1)S(1)}, bf16[128,512]{1,0:T(8,128)(2,1)S(1)}, u32[]{:S(2)}, u32[]{:S(2)}) collective-permute-start(bf16[128,512]{1,0:T(8,128)(2,1)S(1)} %get-tuple-element.326.refs_0_), channel_id=1, source_target_pairs={{0,4},{1,5},{2,6},{3,7},{4,0},{5,1},{6,2},{7,3},{8,12},{9,13},{10,... | collective-permute-start | bytes 393224 | tf_op jit(solution)/shard_map/ppermute | solution.py:537
  95.0 5.6 %collective-permute-start.34 = (bf16[128,512]{1,0:T(8,128)(2,1)S(1)}, bf16[128,512]{1,0:T(8,128)(2,1)S(1)}, u32[]{:S(2)}, u32[]{:S(2)}) collective-permute-start(bf16[128,512]{1,0:T(8,128)(2,1)S(1)} %get-tuple-element.325.refs_0_), channel_id=1, source_target_pairs={{0,8},{1,9},{2,10},{3,11},{4,12},{5,13},{6,14},{7,15},{8,0},{9,1},... | collective-permute-start | bytes 393224 | tf_op jit(solution)/shard_map/ppermute | solution.py:537
  98.1 6.0 %collective-permute-start.40 = (bf16[128,512]{1,0:T(8,128)(2,1)S(1)}, bf16[128,512]{1,0:T(8,128)(2,1)S(1)}, u32[]{:S(2)}, u32[]{:S(2)}) collective-permute-start(bf16[128,512]{1,0:T(8,128)(2,1)S(1)} %get-tuple-element.335.refs_0_), channel_id=1, source_target_pairs={{0,4},{1,5},{2,6},{3,7},{4,0},{5,1},{6,2},{7,3},{8,12},{9,13},{10,... | collective-permute-start | bytes 393224 | tf_op jit(solution)/shard_map/ppermute | solution.py:537
  100.4 8.0 %collective-permute-start.39 = (bf16[256,512]{1,0:T(8,128)(2,1)S(1)}, bf16[256,512]{1,0:T(8,128)(2,1)S(1)}, u32[]{:S(2)}, u32[]{:S(2)}) collective-permute-start(bf16[256,512]{1,0:T(8,128)(2,1)S(1)} %get-tuple-element.334.refs_0_), channel_id=1, source_target_pairs={{0,8},{1,9},{2,10},{3,11},{4,12},{5,13},{6,14},{7,15},{8,0},{9,1},... | collective-permute-start | bytes 786440 | tf_op jit(solution)/shard_map/ppermute | solution.py:537
  100.6 9.9 %collective-permute-start.37 = (bf16[256,512]{1,0:T(8,128)(2,1)S(1)}, bf16[256,512]{1,0:T(8,128)(2,1)S(1)}, u32[]{:S(2)}, u32[]{:S(2)}) collective-permute-start(bf16[256,512]{1,0:T(8,128)(2,1)S(1)} %get-tuple-element.332.refs_0_), channel_id=1, source_target_pairs={{0,4},{1,5},{2,6},{3,7},{4,0},{5,1},{6,2},{7,3},{8,12},{9,13},{10,... | collective-permute-start | bytes 786440 | tf_op jit(solution)/shard_map/ppermute | solution.py:537
  104.0 7.5 %collective-permute-start.41 = (bf16[256,512]{1,0:T(8,128)(2,1)S(1)}, bf16[256,512]{1,0:T(8,128)(2,1)S(1)}, u32[]{:S(2)}, u32[]{:S(2)}) collective-permute-start(bf16[256,512]{1,0:T(8,128)(2,1)S(1)} %get-tuple-element.342.refs_0_), channel_id=1, source_target_pairs={{0,8},{1,9},{2,10},{3,11},{4,12},{5,13},{6,14},{7,15},{8,0},{9,1},... | collective-permute-start | bytes 786440 | tf_op jit(solution)/shard_map/ppermute | solution.py:537
  104.1 5.7 %collective-permute-start.38 = (f32[8,512]{1,0:T(8,128)S(1)}, f32[8,512]{1,0:T(8,128)S(1)}, u32[]{:S(2)}, u32[]{:S(2)}) collective-permute-start(f32[8,512]{1,0:T(8,128)S(1)} %get-tuple-element.333.refs_0_), channel_id=1, source_target_pairs={{0,2},{1,3},{2,0},{3,1},{4,6},{5,7},{6,4},{7,5},{8,10},{9,11},{10,... | collective-permute-start | bytes 49160 | tf_op jit(solution)/shard_map/ppermute | solution.py:537
  (12 other events, 10.0 us)
